TPU v7x, 512 devices: a whole 4x4x16 slice. The times are simulated.
512 devices in a mesh: ctx: 64 (over z, y), head: 8 (over x, core).
Axes of the slice: x: 4, y: 4, z: 16, core: 2. Of those that a mesh axis runs over, the one named last changes fastest.
Arguments:
- inputs: bfloat16 [8192, 4096], P('ctx', 'head'), may hold values from -6 to 6
- log_decay: float32 [64, 8192], P('head', 'ctx'), may hold values from -1 to 0
- b_proj: bfloat16 [8192, 1024], P('ctx', 'head'), may hold values from -1.25 to 1.25
- c_proj: bfloat16 [8192, 1024], P('ctx', 'head'), may hold values from -1.25 to 1.25
- grad_out: bfloat16 [8192, 4096], P('ctx', 'head'), may hold values from -0.625 to 0.625
- w_bc: bfloat16 [2, 1024, 4096], P(None, 'head'), may hold values from -0.09375 to 0.09375
Outputs:
- grad_inputs: bfloat16 [8192, 4096], P('ctx', 'head')
- grad_decay: float32 [64, 8192], P('head', 'ctx')
- grad_b: bfloat16 [8192, 1024], P('ctx', 'head')
- grad_c: bfloat16 [8192, 1024], P('ctx', 'head')
- grad_tokens: bfloat16 [8192, 4096], P(('ctx', 'head'))
All inputs are finite; a program needn't handle non-finite values.
Results may differ from a plain program's by a relative error of at most 0.017.
Values may be sent and summed in bfloat16 or wider, within the bound.
No kernel may reach another device: no remote copies, remote signals or barrier semaphores. Data moves between devices by JAX's collectives and lax.ppermute only.
A program may use at most 128 MiB of HBM per device.

v0:
```python
import jax
import jax.numpy as jnp
from jax import lax
from jax.sharding import PartitionSpec as P

HEAD_TOTAL = 64
P_SIZE = 64
N = 128
GROUPS = 8


def prefix(x, axis, combine, identity, reverse):
    size, index = (lax.axis_size(axis), lax.axis_index(axis))
    everything = jax.tree.map(lambda part: lax.all_gather(part, axis), x)
    start = jax.tree.map(
        lambda part, zero: jnp.broadcast_to(jnp.asarray(zero, part.dtype), part.shape), x, identity
    )

    def hop(k, before):
        at = size - 1 - k if reverse else k
        reached = at > index if reverse else at < index
        new = combine(before, jax.tree.map(lambda part: part[at], everything))
        return jax.tree.map(lambda a, b: jnp.where(reached, a, b), new, before)

    return lax.fori_loop(0, size, hop, start)


def local_grads(input_four, output_gradient_four, b_three, c_three, cum_rate):
    length = input_four.shape[0]
    group_count = input_four.shape[1]
    per_group = input_four.shape[2]
    scores = jnp.einsum("tgn,sgn->gts", c_three, b_three, preferred_element_type=jnp.float32)
    rows = lax.broadcasted_iota(jnp.int32, (length, length), 0)
    cols = lax.broadcasted_iota(jnp.int32, (length, length), 1)
    lower_mask = rows >= cols
    gap_log = cum_rate[:, :, None] - cum_rate[:, None, :]
    decays = jnp.where(lower_mask, jnp.exp(jnp.where(lower_mask, gap_log, 0.0)), 0.0)
    decays = decays.reshape(group_count, per_group, length, length)
    weight_matrix = scores[:, None] * decays
    grad_weights = jnp.einsum(
        "laky,jaky->aklj", output_gradient_four, input_four, preferred_element_type=jnp.float32
    )
    grad_scores = jnp.sum(grad_weights * decays, axis=1)
    product = grad_weights * weight_matrix
    grad_cum = (jnp.sum(product, axis=3) - jnp.sum(product, axis=2)).reshape(
        group_count * per_group, length
    )
    input_gradient = jnp.einsum(
        "yvbi,byve->iyve", weight_matrix, output_gradient_four, precision=lax.Precision.HIGHEST
    )
    grad_c = jnp.einsum("gts,sgn->tgn", grad_scores, b_three, precision=lax.Precision.HIGHEST)
    grad_b = jnp.einsum("gts,tgn->sgn", grad_scores, c_three, precision=lax.Precision.HIGHEST)
    return (input_gradient, grad_cum, grad_b, grad_c)


def carried_grads(
    input_four,
    scaled_inputs,
    scaled_grads,
    tail_wide,
    b_three,
    c_three,
    cum_rate,
    entering,
    leaving_grad,
):
    length = input_four.shape[0]
    group_count = input_four.shape[1]
    per_group = input_four.shape[2]
    head_count = group_count * per_group
    state_four = entering.reshape(group_count, per_group, N, P_SIZE)
    grad_four = leaving_grad.reshape(group_count, per_group, N, P_SIZE)
    from_state = jnp.einsum("tgn,grnp->tgrp", c_three, state_four, precision=lax.Precision.HIGHEST)
    grad_c = jnp.einsum("tgrp,grnp->tgn", scaled_grads, state_four, precision=lax.Precision.HIGHEST)
    state_back = jnp.einsum("sgn,grnp->sgrp", b_three, grad_four, precision=lax.Precision.HIGHEST)
    input_gradient = tail_wide.reshape(length, group_count, per_group, P_SIZE) * state_back
    grad_b = jnp.einsum("sgrp,grnp->sgn", scaled_inputs, grad_four, precision=lax.Precision.HIGHEST)
    through_tail = jnp.sum(input_gradient * input_four, axis=3)
    through_head = jnp.sum(scaled_grads * from_state, axis=3)
    grad_cum = (through_head - through_tail).reshape(length, head_count).T
    last_term = jnp.sum(through_tail, axis=0).reshape(head_count)
    last_term = last_term + jnp.exp(cum_rate[:, -1]) * jnp.sum(leaving_grad * entering, axis=(1, 2))
    grad_cum = grad_cum.at[:, -1].add(last_term)
    return (input_gradient, grad_cum, grad_b, grad_c)


def chain_step(earlier, later):
    return (earlier[0] * later[0], later[0][:, None, None] * earlier[1] + later[1])


def local(inputs, log_decay, b_proj, c_proj, grad_out, w_bc):
    length = inputs.shape[0]
    head_count = log_decay.shape[0]
    per_group = HEAD_TOTAL // GROUPS
    group_count = head_count // per_group
    input_four = inputs.reshape(length, group_count, per_group, P_SIZE)
    output_gradient_four = grad_out.reshape(length, group_count, per_group, P_SIZE)
    b_three = b_proj.reshape(length, group_count, N)
    c_three = c_proj.reshape(length, group_count, N)
    cum_rate = jnp.cumsum(log_decay, axis=1)
    totals = jnp.exp(cum_rate[:, -1])
    tail_wide = jnp.repeat(jnp.exp(cum_rate[:, -1:] - cum_rate).T, P_SIZE, axis=1)
    head_wide = jnp.repeat(jnp.exp(cum_rate).T, P_SIZE, axis=1)
    scaled_inputs = (tail_wide * inputs).reshape(length, group_count, per_group, P_SIZE)
    scaled_grads = (head_wide * grad_out).reshape(length, group_count, per_group, P_SIZE)
    local_state = jnp.einsum(
        "sgn,sgrp->grnp", b_three, scaled_inputs, precision=lax.Precision.HIGHEST
    ).reshape(head_count, N, P_SIZE)
    local_grad = jnp.einsum(
        "tgn,tgrp->grnp", c_three, scaled_grads, precision=lax.Precision.HIGHEST
    ).reshape(head_count, N, P_SIZE)
    zero_state = jnp.zeros_like(local_state)
    identity = (jnp.ones((head_count,), jnp.float32), zero_state)
    first_part = None
    entering = prefix((totals, local_state), "ctx", chain_step, identity, False)[1]
    leaving_grad = prefix((totals, local_grad), "ctx", chain_step, identity, True)[1]
    first_part = local_grads(input_four, output_gradient_four, b_three, c_three, cum_rate)
    second = carried_grads(
        input_four,
        scaled_inputs,
        scaled_grads,
        tail_wide,
        b_three,
        c_three,
        cum_rate,
        entering,
        leaving_grad,
    )
    gradients = jax.tree.map(jnp.add, first_part, second)
    grad_inputs = gradients[0].reshape(length, head_count * P_SIZE).astype(jnp.bfloat16)
    grad_decay = lax.cumsum(gradients[1], axis=1, reverse=True)
    grad_b = gradients[2].reshape(length, group_count * N).astype(jnp.bfloat16)
    grad_c = gradients[3].reshape(length, group_count * N).astype(jnp.bfloat16)
    partial_value = jnp.dot(grad_b, w_bc[0], preferred_element_type=jnp.float32)
    partial_value = partial_value + jnp.dot(grad_c, w_bc[1], preferred_element_type=jnp.float32)
    columns = lax.psum_scatter(
        partial_value.astype(jnp.bfloat16), "head", scatter_dimension=1, tiled=True
    )
    grad_tokens = lax.all_to_all(columns, "head", split_axis=0, concat_axis=1, tiled=True)
    return (grad_inputs, grad_decay, grad_b, grad_c, grad_tokens)


def solution(mesh):
    placed = (
        P("ctx", "head"),
        P("head", "ctx"),
        P("ctx", "head"),
        P("ctx", "head"),
        P("ctx", "head"),
        P(None, "head", None),
    )
    return jax.shard_map(
        local,
        mesh=mesh,
        in_specs=placed,
        out_specs=(
            P("ctx", "head"),
            P("head", "ctx"),
            P("ctx", "head"),
            P("ctx", "head"),
            P(("ctx", "head"), None),
        ),
        check_vma=False,
    )
```

profile of v0, /device:TPU:1, one launch (start us, length us, event | category | flops | bytes accessed | tf_op | source)
XLA Modules:
  0.0 547.8 jit_solution(11317576616958885986)
XLA Ops:
  8.4 1.0 copy.73
  9.5 1.7 convolution_bitcast_fusion.4
  11.3 1.0 copy.77
  13.5 1.3 dynamic-slice.9
  15.6 123.7 %all-reduce = f32[512]{0:T(512)S(1)} all-reduce(f32[512]{0:T(512)S(1)} %dynamic-update-slice.3), channel_id=2, replica_groups=mesh['ctx'=64,'head'=8] {'ctx'}, use_global_device_ids=true, to_apply=%add | all-reduce | flops 512 | bytes 4096
  140.1 70.5 %all-gather.4.cloned.1.call-done = f32[64,8,128,64]{2,3,1,0:T(8,128)} async-done(((f32[1,8,128,64]{2,3,1,0:T(8,128)}), f32[64,8,128,64]{2,3,1,0:T(8,128)}) %all-gather.4.cloned.1.call-update) | async-done | bytes 16777232 | tf_op jit(solution)/shard_map/all_gather | solution.py:14
  210.6 87.5 %while.31 = (s32[]{:T(128)}, f32[8,128,64]{2,1,0:T(8,128)S(1)}, s32[]{:T(128)}, f32[64,8]{1,0:T(8,128)S(1)}, f32[64,8,128,64]{2,3,1,0:T(8,128)}, /*index=5*/s32[]{:T(128)}, s32[]{:T(128)}, s32[]{:T(128)}, s32[]{:T(128)}) while((s32[]{:T(128)}, f32[8,128,64]{2,1,0:T(8,128)S(1)}, s32[]{:T(128)}, f32[64,8]{1,0:T(8,128)S(1)}, ...), condition=%wide.region_2.3_spmd.clone, body=%wide.region_1.2_spmd.clone.sunk | while | flops 262152 | bytes 1835279 | solution.py:25
  212.0 1.0 constant_dynamic-slice_fusion.4
  214.7 1.0 constant_dynamic-slice_fusion.4
  217.4 1.0 constant_dynamic-slice_fusion.4
  220.2 1.0 constant_dynamic-slice_fusion.4
  221.5 1.0 constant_dynamic-slice_fusion.4
  224.3 1.0 constant_dynamic-slice_fusion.4
  227.0 1.0 constant_dynamic-slice_fusion.4
  229.7 1.0 constant_dynamic-slice_fusion.4
  231.1 1.0 constant_dynamic-slice_fusion.4
  232.5 1.0 constant_dynamic-slice_fusion.4
  235.2 1.0 constant_dynamic-slice_fusion.4
  236.6 1.0 constant_dynamic-slice_fusion.4
  238.0 1.0 constant_dynamic-slice_fusion.4
  239.3 1.0 constant_dynamic-slice_fusion.4
  242.1 1.0 constant_dynamic-slice_fusion.4
  243.4 1.0 constant_dynamic-slice_fusion.4
  244.8 1.0 constant_dynamic-slice_fusion.4
  246.2 1.0 constant_dynamic-slice_fusion.4
  248.9 1.0 constant_dynamic-slice_fusion.4
  250.3 1.0 constant_dynamic-slice_fusion.4
  253.0 1.0 constant_dynamic-slice_fusion.4
  254.4 1.0 constant_dynamic-slice_fusion.4
  255.8 1.0 constant_dynamic-slice_fusion.4
  257.1 1.0 constant_dynamic-slice_fusion.4
  258.5 1.0 constant_dynamic-slice_fusion.4
  259.9 1.0 constant_dynamic-slice_fusion.4
  261.2 1.0 constant_dynamic-slice_fusion.4
  262.6 1.0 constant_dynamic-slice_fusion.4
  265.3 1.0 constant_dynamic-slice_fusion.4
  268.1 1.0 constant_dynamic-slice_fusion.4
  270.8 1.0 constant_dynamic-slice_fusion.4
  272.2 1.0 constant_dynamic-slice_fusion.4
  298.1 105.4 %all-gather.6.cloned.1.call-done = f32[64,8,128,64]{2,3,1,0:T(8,128)} async-done(((f32[1,8,128,64]{2,3,1,0:T(8,128)}), f32[64,8,128,64]{2,3,1,0:T(8,128)}) %all-gather.6.cloned.1.call-update) | async-done | bytes 16777232 | tf_op jit(solution)/shard_map/all_gather | solution.py:14
  403.6 87.1 %while.32 = (s32[]{:T(128)}, f32[8,128,64]{2,1,0:T(8,128)S(1)}, s32[]{:T(128)}, f32[64,8]{1,0:T(8,128)S(1)}, f32[64,8,128,64]{2,3,1,0:T(8,128)}, /*index=5*/s32[]{:T(128)}, s32[]{:T(128)}) while((s32[]{:T(128)}, f32[8,128,64]{2,1,0:T(8,128)S(1)}, s32[]{:T(128)}, f32[64,8]{1,0:T(8,128)S(1)}, f32[64,8,128,64]{2,3,1,0:T(8,128)}, ...), condition=%wide.region_6.7_spmd.clone, body=%wide.region_5.6_spmd.clone.sunk | while | flops 262148 | bytes 1835217 | solution.py:25
  490.6 1.0 convolution_bitcast_fusion.7
  491.6 1.0 convolution_bitcast_fusion.5
  493.5 1.4 fusion.2
  498.1 31.7 %reduce-scatter.2.cloned.1.call-done = bf16[128,512]{1,0:T(8,128)(2,1)} async-done(((bf16[128,4096]{1,0:T(8,128)(2,1)}), bf16[128,512]{1,0:T(8,128)(2,1)}) %reduce-scatter.2.cloned.1.call-update) | async-done | bytes 131088 | tf_op jit(solution)/shard_map/reduce_scatter | solution.py:136
  529.8 5.6 %all-to-all-start = ((bf16[8,16,512]{2,1,0:T(8,128)(2,1)}), bf16[8,16,512]{2,1,0:T(8,128)(2,1)S(1)}, u32[]{:S(2)}, u32[]{:S(2)}) async-start(bf16[8,16,512]{2,1,0:T(8,128)(2,1)} %bitcast.157), calls=%async_computation.1 | async-start | bytes 262144 | tf_op jit(solution)/shard_map/all_to_all | solution.py:139
  535.4 1.8 reduce_window_sum.22
  537.2 3.5 all-to-all-done
  (525 shorter events, 145.2 us)
Async XLA Ops:
  7.2 5.2 copy-start
  7.2 132.3 %copy-start.2 = (bf16[128,128]{1,0:T(8,128)(2,1)S(1)}, bf16[128,128]{1,0:T(8,128)(2,1)}, u32[]{:S(2)}) copy-start(bf16[128,128]{1,0:T(8,128)(2,1)} %param.15) | copy-start | bytes 98308
  7.2 203.4 %all-gather.4.cloned.1.call-start = ((), (), s32[]{:S(2)}) async-start(), calls=%async_computation.2 | async-start | bytes 17039360 | tf_op jit(solution)/shard_map/all_gather | solution.py:14
  11.3 392.3 %all-gather.6.cloned.1.call-start = ((), (), s32[]{:S(2)}) async-start(), calls=%async_computation.3 | async-start | bytes 17039360 | tf_op jit(solution)/shard_map/all_gather | solution.py:14
  13.4 516.4 %reduce-scatter.2.cloned.1.call-start = ((), (), s32[]{:S(2)}) async-start(), calls=%async_computation.4 | async-start | bytes 1179648 | tf_op jit(solution)/shard_map/reduce_scatter | solution.py:136
  490.6 2.5 copy-start.1
  492.9 2.1 copy-start.3
  493.1 1.9 copy-start.4
  529.8 10.9 %all-to-all-start = ((bf16[8,16,512]{2,1,0:T(8,128)(2,1)}), bf16[8,16,512]{2,1,0:T(8,128)(2,1)S(1)}, u32[]{:S(2)}, u32[]{:S(2)}) async-start(bf16[8,16,512]{2,1,0:T(8,128)(2,1)} %bitcast.157), calls=%async_computation.1 | async-start | bytes 262144 | tf_op jit(solution)/shard_map/all_to_all | solution.py:139
Sparse Core Ops, SparseCore 0:
  11.4 199.1 all-gather.3
  213.5 189.9 all-gather.5
  495.1 34.5 reduce-scatter.1
where the time goes:
time: 552 us; the launch traced here: 548 us
  waiting for transfers between devices  211 us (38%)
  local copies, waits for them, and re-layouts  157 us (28%)
  blocking collectives  124 us (22%)
  other arithmetic  19.8 us (4%)
  between operations  14.6 us (3%)
  matrix products  9.4 us (2%)
  loops' own time  6.29 us (1%)
  starting transfers between devices  5.71 us (1%)
    all_gather x2, waiting for transfers between devices, prefix(): everything = jax.tree.map(lambda part: lax.all_gather(part, axis), x)  176 us
    dynamic_slice x256, local copies, waits for them, and re-layouts, hop(): new = combine(before, jax.tree.map(lambda part: part[at], everything))  150 us
    unnamed x1, blocking collectives  124 us
    reduce_scatter x1, waiting for transfers between devices, local(): lax.psum_scatter(partial_value.astype(jnp.bfloat16), 'head', scatter_dime...  31.7 us
    select_n x128, other arithmetic, hop(): return jax.tree.map(lambda a, b: jnp.where(reached, a, b), new, before)  16.6 us
  transfers between devices with their start and end apart: 4, of which 4 were waited for; matrix products, arithmetic and copies ran while one was open for 17% of the time, Pallas kernels for 0%

commit v1 on v0

v1 whole, which is shorter than its diff:
```python
import functools

import jax
import jax.numpy as jnp
from jax import lax
from jax.experimental import pallas as pl
from jax.experimental.pallas import tpu as pltpu
from jax.sharding import Mesh, PartitionSpec as P

F32 = jnp.float32
BF16 = jnp.bfloat16
P_SIZE = 64
N = 128
HEADS = 8
WIDE = HEADS * P_SIZE
LO = 8
HI = 8
ROWS = N // LO
LANES = 128
HIGHEST = lax.Precision.HIGHEST
VMEM = pl.BlockSpec(memory_space=pltpu.VMEM)
SMEM = pl.BlockSpec(memory_space=pltpu.SMEM)


def iota(shape, axis):
    return lax.broadcasted_iota(jnp.int32, shape, axis)


def matmul(a, b, precision=None):
    return lax.dot_general(
        a, b, (((1,), (0,)), ((), ())), precision=precision, preferred_element_type=F32
    )


def matmul_nt(a, b, precision=None):
    return lax.dot_general(
        a, b, (((1,), (1,)), ((), ())), precision=precision, preferred_element_type=F32
    )


def matmul_tn(a, b):
    return lax.dot_general(a, b, (((0,), (0,)), ((), ())), preferred_element_type=F32)


def cumulative(rate):
    length = rate.shape[1]
    upper = (iota((length, length), 0) <= iota((length, length), 1)).astype(F32)
    rows = matmul(rate, upper, HIGHEST)
    return rows, jnp.transpose(rows)


def widen(columns):
    pick = (iota((HEADS, WIDE), 0) == iota((HEADS, WIDE), 1) // P_SIZE).astype(F32)
    return matmul(columns, pick, HIGHEST)


def split_three(row):
    lane = iota(row.shape, 1)
    first = row.astype(BF16).astype(F32)
    rest = row - first
    second = rest.astype(BF16).astype(F32)
    third = rest - second
    parts = jnp.where(lane < HEADS, first, jnp.where(lane < 2 * HEADS, second, third))
    return jnp.where(lane < 3 * HEADS, parts, 0.0).astype(BF16)


def join_three(rows):
    lane, column = iota((LANES, WIDE), 0), iota((LANES, WIDE), 1)
    pick = jnp.logical_and(lane % HEADS == column // P_SIZE, lane < 3 * HEADS)
    return matmul(rows, pick.astype(BF16))


def states_kernel(x_ref, rate_ref, b_ref, c_ref, g_ref, out_ref):
    _, columns = cumulative(rate_ref[...])
    wide = widen(columns)
    length = wide.shape[0]
    last = wide[length - 1 : length]
    scaled_inputs = (x_ref[...].astype(F32) * jnp.exp(last - wide)).astype(BF16)
    scaled_grads = (g_ref[...].astype(F32) * jnp.exp(wide)).astype(BF16)
    state = matmul_tn(b_ref[...], scaled_inputs).astype(BF16)
    grad = matmul_tn(c_ref[...], scaled_grads).astype(BF16)
    repeat = (iota((HEADS, LANES), 1) % HEADS == iota((HEADS, LANES), 0)).astype(F32)
    total = matmul(columns[length - 1 : length], repeat, HIGHEST)
    total = jnp.broadcast_to(split_three(total), (2 * ROWS, LANES))
    for block in range(LO):
        rows = slice(block * ROWS, (block + 1) * ROWS)
        out_ref[block, 0:ROWS, 0:WIDE] = state[rows]
        out_ref[block, ROWS : 2 * ROWS, 0:WIDE] = grad[rows]
        out_ref[block, :, WIDE : WIDE + LANES] = total


def totals_of(ref):
    rows = [ref[k, 0:ROWS, WIDE : WIDE + LANES].astype(F32)[0:1] for k in range(ref.shape[0])]
    rows = jnp.concatenate(rows, axis=0)
    return rows, join_three(rows.astype(BF16))


def segment_kernel(me_ref, in_ref, out_ref):
    me = me_ref[0]
    rows, wide = totals_of(in_ref)
    decay = jnp.exp(wide)
    state = jnp.zeros((ROWS, WIDE), F32)
    grad = jnp.zeros((ROWS, WIDE), F32)
    for k in range(LO):
        state = decay[k : k + 1] * state + in_ref[k, 0:ROWS, 0:WIDE].astype(F32)
        j = LO - 1 - k
        grad = decay[j : j + 1] * grad + in_ref[j, ROWS : 2 * ROWS, 0:WIDE].astype(F32)
    lane, other = iota((LANES, LANES), 0), iota((LANES, LANES), 1)
    fold = jnp.logical_and(lane % HEADS == other % HEADS, lane < 3 * HEADS).astype(F32)
    total = jnp.sum(matmul(rows, fold, HIGHEST), axis=0, keepdims=True)
    total = jnp.broadcast_to(split_three(total), (ROWS, LANES))
    state = state.astype(BF16)
    grad = grad.astype(BF16)
    for k in range(HI):
        out_ref[k, :, 0:WIDE] = jnp.where(k > me, state, grad)
        out_ref[k, :, WIDE : WIDE + LANES] = total


def entering_kernel(me_ref, far_ref, near_ref, out_ref):
    me = me_ref[0]
    far = jnp.exp(totals_of(far_ref)[1])
    near = jnp.exp(totals_of(near_ref)[1])
    state = jnp.zeros((ROWS, WIDE), F32)
    grad = jnp.zeros((ROWS, WIDE), F32)
    for k in range(HI):
        new = far[k : k + 1] * state + far_ref[k, :, 0:WIDE].astype(F32)
        state = jnp.where(k < me, new, state)
        j = HI - 1 - k
        new = far[j : j + 1] * grad + far_ref[j, :, 0:WIDE].astype(F32)
        grad = jnp.where(j > me, new, grad)
    for k in range(LO):
        out_ref[k, 0:ROWS, :] = state.astype(BF16)
        state = near[k : k + 1] * state + near_ref[k, 0:ROWS, 0:WIDE].astype(F32)
        j = LO - 1 - k
        out_ref[j, ROWS : 2 * ROWS, :] = grad.astype(BF16)
        grad = near[j : j + 1] * grad + near_ref[j, ROWS : 2 * ROWS, 0:WIDE].astype(F32)


def block_kernel(
    x_ref, rate_ref, b_ref, c_ref, g_ref, gx_ref, gd_ref, gb_ref, gc_ref, sx_ref, sg_ref, tail_ref, all_ref
):
    rows, columns = cumulative(rate_ref[...])
    length = columns.shape[0]
    wide = widen(columns)
    last = wide[length - 1 : length]
    tail = jnp.exp(last - wide)
    tail_ref[...] = tail
    all_ref[...] = jnp.broadcast_to(jnp.exp(last), all_ref.shape)
    sx_ref[...] = (x_ref[...].astype(F32) * tail).astype(BF16)
    sg_ref[...] = (g_ref[...].astype(F32) * jnp.exp(wide)).astype(BF16)
    b, c = b_ref[...], c_ref[...]
    scores = matmul_nt(b, c)
    source, target = iota((length, length), 0), iota((length, length), 1)
    lower = source <= target
    before = source < target
    after = (source >= target).astype(BF16)
    lane = iota((length, LANES), 1)
    grad_scores = jnp.zeros((length, length), F32)
    decay_rows = []
    for pair in range(HEADS // 2):
        at = slice(pair * LANES, (pair + 1) * LANES)
        x_pair, g_pair = x_ref[:, at], g_ref[:, at]
        weights, masked = [], []
        for side in range(2):
            head = 2 * pair + side
            mine = (lane < P_SIZE) if side == 0 else (lane >= P_SIZE)
            x_mine = jnp.where(mine, x_pair, jnp.zeros_like(x_pair))
            g_mine = jnp.where(mine, g_pair, jnp.zeros_like(g_pair))
            gap = rows[head : head + 1, :] - columns[:, head : head + 1]
            decay = jnp.where(lower, jnp.exp(jnp.where(lower, gap, 0.0)), 0.0)
            grad_weights = matmul_nt(x_mine, g_pair)
            weight = scores * decay
            grad_scores = grad_scores + grad_weights * decay
            product = (grad_weights * weight).astype(BF16)
            through = matmul(product, after)
            decay_rows.append(jnp.sum(jnp.where(before, through, 0.0), axis=0, keepdims=True))
            weights.append(weight.astype(BF16))
            masked.append(g_mine)
        gx_ref[:, at] = matmul(jnp.concatenate(weights, axis=1), jnp.concatenate(masked, axis=0))
    gd_ref[...] = jnp.concatenate(decay_rows, axis=0)
    gb_ref[...] = matmul(grad_scores.astype(BF16), c)
    gc_ref[...] = matmul(jnp.transpose(grad_scores).astype(BF16), b)


def carried_kernel(
    core_ref,
    state_ref,
    x_ref,
    b_ref,
    c_ref,
    gx_ref,
    gd_ref,
    gb_ref,
    gc_ref,
    sx_ref,
    sg_ref,
    tail_ref,
    all_ref,
    w_ref,
    out_x_ref,
    out_d_ref,
    out_b_ref,
    out_c_ref,
    keep_ref,
    send_ref,
    w_vmem,
    w_sem,
):
    fetch = pltpu.make_async_copy(w_ref, w_vmem, w_sem)
    fetch.start()
    length = x_ref.shape[0]
    state = state_ref[:, 0:ROWS, :].reshape(N, WIDE)
    grad = state_ref[:, ROWS : 2 * ROWS, :].reshape(N, WIDE)
    sx, sg = sx_ref[...], sg_ref[...]
    grad_c = (matmul_nt(sg, state) + gc_ref[...]).astype(BF16)
    grad_b = (matmul_nt(sx, grad) + gb_ref[...]).astype(BF16)
    out_b_ref[...] = grad_b
    out_c_ref[...] = grad_c
    from_state = matmul(c_ref[...], state)
    state_back = matmul(b_ref[...], grad)
    out_x_ref[...] = (gx_ref[...] + tail_ref[...] * state_back).astype(BF16)
    pick = (iota((HEADS, WIDE), 0) == iota((HEADS, WIDE), 1) // P_SIZE).astype(F32)
    through_head = matmul_nt(pick, sg.astype(F32) * from_state, HIGHEST)
    through_tail = matmul_nt(pick, sx.astype(F32) * state_back, HIGHEST)
    whole = jnp.sum(grad.astype(F32) * state.astype(F32), axis=0, keepdims=True) * all_ref[...]
    whole = jnp.sum(pick * whole, axis=1, keepdims=True)
    one, two = iota((length, length), 0), iota((length, length), 1)
    out_d_ref[...] = (
        gd_ref[...]
        + matmul(through_head, (one >= two).astype(F32), HIGHEST)
        + matmul(through_tail, (one < two).astype(F32), HIGHEST)
        + whole
    )
    both = jnp.concatenate([grad_b, grad_c], axis=1)
    sixteen = length // 8
    even = jnp.concatenate([both[2 * k * sixteen : (2 * k + 1) * sixteen] for k in range(4)], axis=0)
    odd = jnp.concatenate([both[(2 * k + 1) * sixteen : (2 * k + 2) * sixteen] for k in range(4)], axis=0)
    first = core_ref[0] == 0
    keep = jnp.where(first, even, odd)
    send = jnp.where(first, odd, even)
    both = jnp.concatenate([keep, send], axis=0)
    half = length // 2
    fetch.wait()
    step = 512
    for k in range(w_ref.shape[1] // step):
        at = slice(k * step, (k + 1) * step)
        part = matmul(both, w_vmem[:, at]).astype(BF16)
        keep_ref[:, at] = part[:half]
        send_ref[:, at] = part[half:]


def struct(shape, dtype):
    return jax.ShapeDtypeStruct(shape, dtype)


def call(kernel, out, operands, name, specs=None, scratch=(), flops=0, moved=0):
    return pl.pallas_call(
        kernel,
        out_shape=out,
        in_specs=specs or [VMEM] * len(operands),
        out_specs=jax.tree.map(lambda _: VMEM, out),
        scratch_shapes=list(scratch),
        cost_estimate=pl.CostEstimate(flops=flops, bytes_accessed=moved, transcendentals=0),
        compiler_params=pltpu.CompilerParams(vmem_limit_bytes=24 * 2**20),
        name=name,
    )(*operands)


def local(inputs, log_decay, b_proj, c_proj, grad_out, w_bc):
    length = inputs.shape[0]
    width = w_bc.shape[2]
    hi = lax.axis_index("hi").astype(jnp.int32).reshape(1)
    core = lax.axis_index("core").astype(jnp.int32).reshape(1)
    near = call(
        states_kernel,
        struct((LO, 2 * ROWS, WIDE + LANES), BF16),
        (inputs, log_decay, b_proj, c_proj, grad_out),
        "states",
        flops=4 * length * N * WIDE,
        moved=2**20,
    )
    near = lax.all_to_all(near, "lo", 0, 0)
    far = call(
        segment_kernel,
        struct((HI, ROWS, WIDE + LANES), BF16),
        (hi, near),
        "segment",
        specs=[SMEM, VMEM],
        moved=2**19,
    )
    far = lax.all_to_all(far, "hi", 0, 0)
    inside = call(
        block_kernel,
        (
            struct((length, WIDE), F32),
            struct((HEADS, length), F32),
            struct((length, N), F32),
            struct((length, N), F32),
            struct((length, WIDE), BF16),
            struct((length, WIDE), BF16),
            struct((length, WIDE), F32),
            struct((HEADS, WIDE), F32),
        ),
        (inputs, log_decay, b_proj, c_proj, grad_out),
        "block",
        flops=2**30,
        moved=4 * 2**20,
    )
    states = call(
        entering_kernel,
        struct((LO, 2 * ROWS, WIDE), BF16),
        (hi, far, near),
        "entering",
        specs=[SMEM, VMEM, VMEM],
        moved=2**19,
    )
    states = lax.all_to_all(states, "lo", 0, 0)
    operands = (core, states, inputs, b_proj, c_proj) + tuple(inside) + (w_bc.reshape(2 * N, width),)
    grad_inputs, grad_decay, grad_b, grad_c, keep, send = call(
        carried_kernel,
        (
            struct((length, WIDE), BF16),
            struct((HEADS, length), F32),
            struct((length, N), BF16),
            struct((length, N), BF16),
            struct((length // 2, width), BF16),
            struct((length // 2, width), BF16),
        ),
        operands,
        "carried",
        specs=[SMEM] + [VMEM] * (len(operands) - 2) + [pl.BlockSpec(memory_space=pl.ANY)],
        scratch=(pltpu.VMEM((2 * N, width), BF16), pltpu.SemaphoreType.DMA),
        flops=2**29,
        moved=4 * 2**20,
    )
    other = lax.ppermute(send, "core", [(0, 1), (1, 0)])
    pair = (keep.astype(F32) + other.astype(F32)).astype(BF16)
    blocks = lax.all_to_all(pair.reshape(4, length // 8, width), "x", 0, 0)
    grad_tokens = jnp.sum(blocks.astype(F32), axis=0).astype(BF16)
    return grad_inputs, grad_decay, grad_b, grad_c, grad_tokens


def solution(mesh):
    fine = Mesh(mesh.devices.reshape(HI, LO, 4, 2), ("hi", "lo", "x", "core"))
    ctx, head = ("hi", "lo"), ("x", "core")
    return jax.shard_map(
        local,
        mesh=fine,
        in_specs=(P(ctx, head), P(head, ctx), P(ctx, head), P(ctx, head), P(ctx, head), P(None, head, None)),
        out_specs=(P(ctx, head), P(head, ctx), P(ctx, head), P(ctx, head), P(ctx + head, None)),
        check_vma=False,
    )
```

time: 552 us -> 83.5 us (0.15)
  waiting for transfers between devices: 211 us -> 10.4 us
  local copies, waits for them, and re-layouts: 157 us -> 7.59 us
  blocking collectives: 124 us -> 39.8 us
  other arithmetic: 19.8 us -> 0.86 us
  between operations: 14.6 us -> 0.73 us
  starting transfers between devices: 5.71 us -> 17.4 us
  matrix products: 9.4 us -> 0 us
  loops' own time: 6.29 us -> 0 us
  Pallas kernels: 0 us -> 6.04 us
    all_gather x2 -> x0, waiting for transfers between devices: 176 us -> none  [prefix(): everything = jax.tree.map(lambda part: lax.all_gather(part, axis), x)]
    dynamic_slice x256 -> x0, local copies, waits for them, and re-layouts: 150 us -> none  [hop(): new = combine(before, jax.tree.map(lambda part: part[at], everything))]
    unnamed x1 -> x0, blocking collectives: 124 us -> none
    all_to_all x0 -> x2, blocking collectives: none -> 39.8 us  [the longest x1 27.4 us: local(): far = lax.all_to_all(far, 'hi', 0, 0)]
    reduce_scatter x1 -> x0, waiting for transfers between devices: 31.7 us -> none  [local(): lax.psum_scatter(partial_value.astype(jnp.bfloat16), 'head', scatter_dime...]
    select_n x128 -> x0, other arithmetic: 16.6 us -> none  [hop(): return jax.tree.map(lambda a, b: jnp.where(reached, a, b), new, before)]
    dot_general x13 -> x0, matrix products: 9.4 us -> none  [the longest x1 1.71 us: local(): jnp.einsum('tgn,tgrp->grnp', c_three, scaled_grads, precision=lax.Precisi...]
    ppermute x0 -> x1, starting transfers between devices: none -> 7.06 us  [local(): other = lax.ppermute(send, 'core', [(0, 1), (1, 0)])]
  transfers between devices with their start and end apart: 4 -> 3, of which waited for: 4 -> 3; matrix products, arithmetic and copies ran while one was open for 17% -> 0% of each run, Pallas kernels for 0% -> 2%
where the time goes in v1:
time: 83.5 us; the launch traced here: 82.9 us
  blocking collectives  39.8 us (48%)
  starting transfers between devices  17.4 us (21%)
  waiting for transfers between devices  10.4 us (12%)
  local copies, waits for them, and re-layouts  7.59 us (9%)
  Pallas kernels  6.04 us (7%)
  other arithmetic  0.86 us (1%)
    all_to_all x1, blocking collectives, local(): far = lax.all_to_all(far, 'hi', 0, 0)  27.4 us
    all_to_all x1, blocking collectives, local(): blocks = lax.all_to_all(pair.reshape(4, length // 8, width), 'x', 0, 0)  12.4 us
    unnamed x30, local copies, waits for them, and re-layouts  7.59 us
    ppermute x1, starting transfers between devices, local(): other = lax.ppermute(send, 'core', [(0, 1), (1, 0)])  7.06 us
    all_to_all x1, starting transfers between devices, local(): near = lax.all_to_all(near, 'lo', 0, 0)  6.37 us
    all_to_all x1, waiting for transfers between devices, local(): near = lax.all_to_all(near, 'lo', 0, 0)  6.34 us
    pallas_call x5, Pallas kernels, call(): pl.pallas_call(kernel, out_shape=out, in_specs=specs or [VMEM] * len(oper...  6.04 us
    all_to_all x1, starting transfers between devices, local(): states = lax.all_to_all(states, 'lo', 0, 0)  4.02 us
  transfers between devices with their start and end apart: 3, of which 3 were waited for; matrix products, arithmetic and copies ran while one was open for 0% of the time, Pallas kernels for 2%

profile of v1, /device:TPU:1, one launch (start us, length us, event | category | flops | bytes accessed | tf_op | source)
XLA Modules:
  0.0 82.9 jit_solution(3764371488778734397)
XLA Ops:
  0.6 0.0 copy-start.1
  0.6 0.9 %copy-done.1 = bf16[128,512]{1,0:T(8,128)(2,1)S(1)} copy-done((bf16[128,512]{1,0:T(8,128)(2,1)S(1)}, bf16[128,512]{1,0:T(8,128)(2,1)}, u32[]{:S(2)}) %copy-start.1) | copy-done | bytes 131096
  1.5 0.0 copy-start.3
  1.5 0.8 copy-done.3
  2.3 0.0 copy-start.5
  2.3 0.8 copy-done.5
  3.1 0.0 copy-start.7
  3.1 0.9 %copy-done.7 = bf16[128,512]{1,0:T(8,128)(2,1)S(1)} copy-done((bf16[128,512]{1,0:T(8,128)(2,1)S(1)}, bf16[128,512]{1,0:T(8,128)(2,1)}, u32[]{:S(2)}) %copy-start.7) | copy-done | bytes 131096
  4.0 0.0 copy-start.11
  4.0 0.7 copy-done.11
  4.6 0.0 copy-start.2
  4.6 0.0 copy-start.4
  4.7 0.0 copy-start.6
  4.7 0.0 copy-start.8
  4.7 1.7 %states.1 = bf16[8,32,640]{2,1,0:T(8,128)(2,1)} custom-call(bf16[128,512]{1,0:T(8,128)(2,1)S(1)} %copy-done.1, f32[8,128]{1,0:T(8,128)S(1)} %copy-done.11, bf16[128,128]{1,0:T(8,128)(2,1)S(1)} %copy-done.3, bf16[128,128]{1,0:T(8,128)(2,1)S(1)} %copy-done.5, bf16[128,512]{1,0:T(8,128)(2,1)S(1)} %copy-done.7), custom_call_target="tpu_custom_call" | custom-call | flops 33554432 | bytes 1048576 | tf_op jit(solution)/shard_map/states/pallas_call | solution.py:257
  6.3 6.4 %all-to-all-start = ((bf16[8,32,640]{2,1,0:T(8,128)(2,1)}), bf16[8,32,640]{2,1,0:T(8,128)(2,1)S(1)}, u32[]{:S(2)}, u32[]{:S(2)}) async-start(bf16[8,32,640]{2,1,0:T(8,128)(2,1)} %states.1), calls=%async_computation | async-start | bytes 655360 | tf_op jit(solution)/shard_map/all_to_all | solution.py:282
  12.7 6.3 %all-to-all-done.in_ref.near_ref = bf16[8,32,640]{2,1,0:T(8,128)(2,1)S(1)} async-done(((bf16[8,32,640]{2,1,0:T(8,128)(2,1)}), bf16[8,32,640]{2,1,0:T(8,128)(2,1)S(1)}, u32[]{:S(2)}, u32[]{:S(2)}) %all-to-all-start) | async-done | bytes 327712 | tf_op jit(solution)/shard_map/all_to_all | solution.py:282
  19.0 0.2 segment.1
  19.2 27.4 %all_to_all.20.far_ref = bf16[8,16,640]{2,1,0:T(8,128)(2,1)S(1)} all-to-all(bf16[8,16,640]{2,1,0:T(8,128)(2,1)S(1)} %segment.1), channel_id=1, replica_groups=mesh['hi'=8,'lo'=8,'x'=4,'core'=2] {'hi'}, dimensions={0} | all-to-all | bytes 327680 | tf_op jit(solution)/shard_map/all_to_all | solution.py:291
  46.6 1.0 %entering.1 = bf16[8,32,512]{2,1,0:T(8,128)(2,1)} custom-call(s32[1]{0:T(128)} %bitcast.1.me_ref, bf16[8,16,640]{2,1,0:T(8,128)(2,1)S(1)} %all_to_all.20.far_ref, bf16[8,32,640]{2,1,0:T(8,128)(2,1)S(1)} %all-to-all-done.in_ref.near_ref), custom_call_target="tpu_custom_call" | custom-call | bytes 524288 | tf_op jit(solution)/shard_map/entering/pallas_call | solution.py:257
  47.6 4.0 %all-to-all-start.2 = ((bf16[8,32,512]{2,1,0:T(8,128)(2,1)}), bf16[8,32,512]{2,1,0:T(8,128)(2,1)S(1)}, u32[]{:S(2)}, u32[]{:S(2)}) async-start(bf16[8,32,512]{2,1,0:T(8,128)(2,1)} %entering.1), calls=%async_computation.2 | async-start | bytes 524288 | tf_op jit(solution)/shard_map/all_to_all | solution.py:317
  51.6 0.0 copy-start
  51.6 0.0 copy-done.2
  51.6 0.0 copy-done.4
  51.6 0.0 copy-done.6
  51.6 0.0 copy-done.8
  51.6 0.0 copy-start.12
  51.6 0.8 copy-done.12
  52.4 1.4 %block.1 = (f32[128,512]{1,0:T(8,128)S(1)}, f32[8,128]{1,0:T(8,128)S(1)}, f32[128,128]{1,0:T(8,128)S(1)}, f32[128,128]{1,0:T(8,128)S(1)}, bf16[128,512]{1,0:T(8,...) custom-call(bf16[128,512]{1,0:T(8,128)(2,1)S(1)} %copy-done.2, ...), custom_call_target="tpu_custom_call" | custom-call | flops 1073741824 | bytes 4194304 | tf_op jit(solution)/shard_map/block/pallas_call | solution.py:257
  53.9 0.0 copy-start.9
  53.9 0.6 copy-done.9
  54.5 0.0 copy-start.13
  54.5 0.6 copy-done.13
  55.1 2.5 %all-to-all-done.2.state_ref = bf16[8,32,512]{2,1,0:T(8,128)(2,1)S(1)} async-done(((bf16[8,32,512]{2,1,0:T(8,128)(2,1)}), bf16[8,32,512]{2,1,0:T(8,128)(2,1)S(1)}, u32[]{:S(2)}, u32[]{:S(2)}) %all-to-all-start.2) | async-done | bytes 262176 | tf_op jit(solution)/shard_map/all_to_all | solution.py:317
  57.6 0.0 copy-done
  57.7 0.0 copy-start.10
  57.7 0.8 %copy-done.10 = f32[128,128]{1,0:T(8,128)S(1)} copy-done((f32[128,128]{1,0:T(8,128)S(1)}, f32[128,128]{1,0:T(8,128)}, u32[]{:S(2)}) %copy-start.10) | copy-done | bytes 65560
  58.5 0.0 copy-start.14
  58.5 0.7 copy-done.14
  59.2 1.8 %carried.1 = (bf16[128,512]{1,0:T(8,128)(2,1)}, f32[8,128]{1,0:T(8,128)}, bf16[128,128]{1,0:T(8,128)(2,1)}, bf16[128,128]{1,0:T(8,128)(2,1)}, bf16[64,4096]{1,0:...) custom-call(s32[1]{0:T(128)} %bitcast.core_ref, bf16[8,32,512]{2,1,0:T(8,128)(2,1)S(1)} %all-to-all-done.2.state_ref, ...), custom_call_target="tpu_custom_call" | custom-call | flops 536870912 | bytes 4194304 | tf_op jit(solution)/shard_map/carried/pallas_call | solution.py:257
  61.0 7.1 %collective-permute-start = (bf16[64,4096]{1,0:T(8,128)(2,1)S(1)}, bf16[64,4096]{1,0:T(8,128)(2,1)S(1)}, u32[]{:S(2)}, u32[]{:S(2)}) collective-permute-start(bf16[64,4096]{1,0:T(8,128)(2,1)S(1)} %get-tuple-element.32), channel_id=1, source_target_pairs={{0,1},{1,0},{2,3},{3,2},{4,5},{5,4},{6,7},{7,6},{8,9},{9,8},{10,11... | collective-permute-start | bytes 1572872 | tf_op jit(solution)/shard_map/ppermute | solution.py:336
  68.0 1.5 %collective-permute-done = bf16[64,4096]{1,0:T(8,128)(2,1)S(1)} collective-permute-done((bf16[64,4096]{1,0:T(8,128)(2,1)S(1)}, bf16[64,4096]{1,0:T(8,128)(2,1)S(1)}, u32[]{:S(2)}, u32[]{:S(2)}) %collective-permute-start) | collective-permute-done | bytes 524320 | tf_op jit(solution)/shard_map/ppermute | solution.py:336
  69.6 0.1 add_convert_fusion
  69.7 12.4 %all_to_all.21 = bf16[4,16,4096]{2,1,0:T(8,128)(2,1)S(1)} all-to-all(bf16[4,16,4096]{2,1,0:T(8,128)(2,1)S(1)} %bitcast.5), channel_id=1, replica_groups=mesh['hi'=8,'lo'=8,'x'=4,'core'=2] {'x'}, dimensions={0} | all-to-all | bytes 1048576 | tf_op jit(solution)/shard_map/all_to_all | solution.py:338
  82.1 0.7 reduce_sum.12
Async XLA Ops:
  0.6 0.9 %copy-start.1 = (bf16[128,512]{1,0:T(8,128)(2,1)S(1)}, bf16[128,512]{1,0:T(8,128)(2,1)}, u32[]{:S(2)}) copy-start(bf16[128,512]{1,0:T(8,128)(2,1)} %x_ref.5) | copy-start | bytes 393220
  1.5 0.8 copy-start.3
  2.3 0.8 copy-start.5
  3.1 0.9 %copy-start.7 = (bf16[128,512]{1,0:T(8,128)(2,1)S(1)}, bf16[128,512]{1,0:T(8,128)(2,1)}, u32[]{:S(2)}) copy-start(bf16[128,512]{1,0:T(8,128)(2,1)} %g_ref.3) | copy-start | bytes 393220
  4.0 0.7 copy-start.11
  4.6 46.9 %copy-start.2 = (bf16[128,512]{1,0:T(8,128)(2,1)S(1)}, bf16[128,512]{1,0:T(8,128)(2,1)}, u32[]{:S(2)}) copy-start(bf16[128,512]{1,0:T(8,128)(2,1)} %x_ref.5) | copy-start | bytes 393220
  4.6 46.9 %copy-start.4 = (bf16[128,128]{1,0:T(8,128)(2,1)S(1)}, bf16[128,128]{1,0:T(8,128)(2,1)}, u32[]{:S(2)}) copy-start(bf16[128,128]{1,0:T(8,128)(2,1)} %b_ref.5) | copy-start | bytes 98308
  4.7 46.9 %copy-start.6 = (bf16[128,128]{1,0:T(8,128)(2,1)S(1)}, bf16[128,128]{1,0:T(8,128)(2,1)}, u32[]{:S(2)}) copy-start(bf16[128,128]{1,0:T(8,128)(2,1)} %c_ref.5) | copy-start | bytes 98308
  4.7 47.0 %copy-start.8 = (bf16[128,512]{1,0:T(8,128)(2,1)S(1)}, bf16[128,512]{1,0:T(8,128)(2,1)}, u32[]{:S(2)}) copy-start(bf16[128,512]{1,0:T(8,128)(2,1)} %g_ref.3) | copy-start | bytes 393220
  6.3 12.7 %all-to-all-start = ((bf16[8,32,640]{2,1,0:T(8,128)(2,1)}), bf16[8,32,640]{2,1,0:T(8,128)(2,1)S(1)}, u32[]{:S(2)}, u32[]{:S(2)}) async-start(bf16[8,32,640]{2,1,0:T(8,128)(2,1)} %states.1), calls=%async_computation | async-start | bytes 655360 | tf_op jit(solution)/shard_map/all_to_all | solution.py:282
  47.6 10.1 %all-to-all-start.2 = ((bf16[8,32,512]{2,1,0:T(8,128)(2,1)}), bf16[8,32,512]{2,1,0:T(8,128)(2,1)S(1)}, u32[]{:S(2)}, u32[]{:S(2)}) async-start(bf16[8,32,512]{2,1,0:T(8,128)(2,1)} %entering.1), calls=%async_computation.2 | async-start | bytes 524288 | tf_op jit(solution)/shard_map/all_to_all | solution.py:317
  51.6 6.1 %copy-start = (bf16[2,128,4096]{2,1,0:T(8,128)(2,1)S(1)}, bf16[2,128,4096]{2,1,0:T(8,128)(2,1)}, u32[]{:S(2)}) copy-start(bf16[2,128,4096]{2,1,0:T(8,128)(2,1)} %param.11) | copy-start | bytes 6291460
  51.6 0.8 %copy-start.12 = (f32[8,128]{1,0:T(8,128)S(1)}, f32[8,128]{1,0:T(8,128)}, u32[]{:S(2)}) copy-start(f32[8,128]{1,0:T(8,128)} %rate_ref.3) | copy-start | bytes 12292
  53.9 0.6 copy-start.9
  54.5 0.6 copy-start.13
  57.7 0.8 %copy-start.10 = (f32[128,128]{1,0:T(8,128)S(1)}, f32[128,128]{1,0:T(8,128)}, u32[]{:S(2)}) copy-start(f32[128,128]{1,0:T(8,128)} %copy-done.9) | copy-start | bytes 196612
  58.5 0.7 copy-start.14
  61.0 8.6 %collective-permute-start = (bf16[64,4096]{1,0:T(8,128)(2,1)S(1)}, bf16[64,4096]{1,0:T(8,128)(2,1)S(1)}, u32[]{:S(2)}, u32[]{:S(2)}) collective-permute-start(bf16[64,4096]{1,0:T(8,128)(2,1)S(1)} %get-tuple-element.32), channel_id=1, source_target_pairs={{0,1},{1,0},{2,3},{3,2},{4,5},{5,4},{6,7},{7,6},{8,9},{9,8},{10,11... | collective-permute-start | bytes 1572872 | tf_op jit(solution)/shard_map/ppermute | solution.py:336

commit v2 on v1

--- a/solution.py
+++ b/solution.py
@@ -15,10 +15,17 @@
 WIDE = HEADS * P_SIZE
 LO = 8
 HI = 8
+LANES = 128
 ROWS = N // LO
-LANES = 128
 HIGHEST = lax.Precision.HIGHEST
+GROUPS = WIDE // LANES
+STATE = GROUPS * ROWS
+NEAR = 2 * STATE + 16
+FAR = STATE + 16
+FIRST = 4
+ORDER = [(k + FIRST) & (HI - 1) for k in range(HI)]
 VMEM = pl.BlockSpec(memory_space=pltpu.VMEM)
+HBM = pl.BlockSpec(memory_space=pltpu.HBM)
 SMEM = pl.BlockSpec(memory_space=pltpu.SMEM)
 
 
@@ -50,7 +57,7 @@
 
 
 def widen(columns):
-    pick = (iota((HEADS, WIDE), 0) == iota((HEADS, WIDE), 1) // P_SIZE).astype(F32)
+    pick = (iota((HEADS, WIDE), 0) == iota((HEADS, WIDE), 1) >> 6).astype(F32)
     return matmul(columns, pick, HIGHEST)
 
 
@@ -66,78 +73,126 @@
 
 def join_three(rows):
     lane, column = iota((LANES, WIDE), 0), iota((LANES, WIDE), 1)
-    pick = jnp.logical_and(lane % HEADS == column // P_SIZE, lane < 3 * HEADS)
+    pick = jnp.logical_and((lane & 7) == (column >> 6), lane < 3 * HEADS)
     return matmul(rows, pick.astype(BF16))
 
 
-def states_kernel(x_ref, rate_ref, b_ref, c_ref, g_ref, out_ref):
+def start_copies(sources, targets, sems):
+    copies = [
+        pltpu.make_async_copy(source, target, sems.at[k])
+        for k, (source, target) in enumerate(zip(sources, targets))
+    ]
+    for copy in copies:
+        copy.start()
+    return copies
+
+
+def states_kernel(rate_in, x_in, g_in, b_in, c_in, out_ref, rate_ref, x_ref, g_ref, b_ref, c_ref, sems):
+    copies = start_copies(
+        (rate_in, x_in, g_in, b_in, c_in), (rate_ref, x_ref, g_ref, b_ref, c_ref), sems
+    )
+    copies[0].wait()
     _, columns = cumulative(rate_ref[...])
     wide = widen(columns)
     length = wide.shape[0]
     last = wide[length - 1 : length]
-    scaled_inputs = (x_ref[...].astype(F32) * jnp.exp(last - wide)).astype(BF16)
-    scaled_grads = (g_ref[...].astype(F32) * jnp.exp(wide)).astype(BF16)
+    repeat = ((iota((HEADS, LANES), 1) & 7) == iota((HEADS, LANES), 0)).astype(F32)
+    total = matmul(columns[length - 1 : length], repeat, HIGHEST)
+    total = jnp.broadcast_to(split_three(total), (NEAR - 2 * STATE, LANES))
+    tail = jnp.exp(last - wide)
+    head = jnp.exp(wide)
+    for copy in copies[1:]:
+        copy.wait()
+    scaled_inputs = (x_ref[...].astype(F32) * tail).astype(BF16)
+    scaled_grads = (g_ref[...].astype(F32) * head).astype(BF16)
     state = matmul_tn(b_ref[...], scaled_inputs).astype(BF16)
     grad = matmul_tn(c_ref[...], scaled_grads).astype(BF16)
-    repeat = (iota((HEADS, LANES), 1) % HEADS == iota((HEADS, LANES), 0)).astype(F32)
-    total = matmul(columns[length - 1 : length], repeat, HIGHEST)
-    total = jnp.broadcast_to(split_three(total), (2 * ROWS, LANES))
     for block in range(LO):
         rows = slice(block * ROWS, (block + 1) * ROWS)
-        out_ref[block, 0:ROWS, 0:WIDE] = state[rows]
-        out_ref[block, ROWS : 2 * ROWS, 0:WIDE] = grad[rows]
-        out_ref[block, :, WIDE : WIDE + LANES] = total
-
-
-def totals_of(ref):
-    rows = [ref[k, 0:ROWS, WIDE : WIDE + LANES].astype(F32)[0:1] for k in range(ref.shape[0])]
+        for k in range(GROUPS):
+            at = slice(k * LANES, (k + 1) * LANES)
+            out_ref[block, k * ROWS : (k + 1) * ROWS, :] = state[rows, at]
+            out_ref[block, STATE + k * ROWS : STATE + (k + 1) * ROWS, :] = grad[rows, at]
+        out_ref[block, 2 * STATE : NEAR, :] = total
+
+
+def totals_of(ref, row):
+    rows = [ref[k, row : row + 16, :].astype(F32)[0:1] for k in range(ref.shape[0])]
     rows = jnp.concatenate(rows, axis=0)
     return rows, join_three(rows.astype(BF16))
 
 
+def chunk_decays(wide):
+    decay = jnp.exp(wide)
+    return [
+        jnp.concatenate(
+            [
+                jnp.broadcast_to(decay[k : k + 1, j * LANES : (j + 1) * LANES], (ROWS, LANES))
+                for j in range(GROUPS)
+            ],
+            axis=0,
+        )
+        for k in range(decay.shape[0])
+    ]
+
+
 def segment_kernel(me_ref, in_ref, out_ref):
     me = me_ref[0]
-    rows, wide = totals_of(in_ref)
-    decay = jnp.exp(wide)
-    state = jnp.zeros((ROWS, WIDE), F32)
-    grad = jnp.zeros((ROWS, WIDE), F32)
+    rows, wide = totals_of(in_ref, 2 * STATE)
+    decay = chunk_decays(wide)
+    state = jnp.zeros((STATE, LANES), F32)
+    grad = jnp.zeros((STATE, LANES), F32)
     for k in range(LO):
-        state = decay[k : k + 1] * state + in_ref[k, 0:ROWS, 0:WIDE].astype(F32)
+        state = decay[k] * state + in_ref[k, 0:STATE, :].astype(F32)
         j = LO - 1 - k
-        grad = decay[j : j + 1] * grad + in_ref[j, ROWS : 2 * ROWS, 0:WIDE].astype(F32)
+        grad = decay[j] * grad + in_ref[j, STATE : 2 * STATE, :].astype(F32)
     lane, other = iota((LANES, LANES), 0), iota((LANES, LANES), 1)
-    fold = jnp.logical_and(lane % HEADS == other % HEADS, lane < 3 * HEADS).astype(F32)
+    fold = jnp.logical_and((lane & 7) == (other & 7), lane < 3 * HEADS).astype(F32)
     total = jnp.sum(matmul(rows, fold, HIGHEST), axis=0, keepdims=True)
-    total = jnp.broadcast_to(split_three(total), (ROWS, LANES))
+    total = jnp.broadcast_to(split_three(total), (FAR - STATE, LANES))
     state = state.astype(BF16)
     grad = grad.astype(BF16)
-    for k in range(HI):
-        out_ref[k, :, 0:WIDE] = jnp.where(k > me, state, grad)
-        out_ref[k, :, WIDE : WIDE + LANES] = total
+    for k, segment in enumerate(ORDER):
+        out_ref[k, 0:STATE, :] = jnp.where(segment > me, state, grad)
+        out_ref[k, STATE:FAR, :] = total
 
 
 def entering_kernel(me_ref, far_ref, near_ref, out_ref):
     me = me_ref[0]
-    far = jnp.exp(totals_of(far_ref)[1])
-    near = jnp.exp(totals_of(near_ref)[1])
-    state = jnp.zeros((ROWS, WIDE), F32)
-    grad = jnp.zeros((ROWS, WIDE), F32)
+    far = chunk_decays(totals_of(far_ref, STATE)[1])
+    near = chunk_decays(totals_of(near_ref, 2 * STATE)[1])
+    state = jnp.zeros((STATE, LANES), F32)
+    grad = jnp.zeros((STATE, LANES), F32)
     for k in range(HI):
-        new = far[k : k + 1] * state + far_ref[k, :, 0:WIDE].astype(F32)
+        at = ORDER.index(k)
+        new = far[at] * state + far_ref[at, 0:STATE, :].astype(F32)
         state = jnp.where(k < me, new, state)
         j = HI - 1 - k
-        new = far[j : j + 1] * grad + far_ref[j, :, 0:WIDE].astype(F32)
+        at = ORDER.index(j)
+        new = far[at] * grad + far_ref[at, 0:STATE, :].astype(F32)
         grad = jnp.where(j > me, new, grad)
     for k in range(LO):
-        out_ref[k, 0:ROWS, :] = state.astype(BF16)
-        state = near[k : k + 1] * state + near_ref[k, 0:ROWS, 0:WIDE].astype(F32)
+        out_ref[k, 0:STATE, :] = state.astype(BF16)
+        state = near[k] * state + near_ref[k, 0:STATE, :].astype(F32)
         j = LO - 1 - k
-        out_ref[j, ROWS : 2 * ROWS, :] = grad.astype(BF16)
-        grad = near[j : j + 1] * grad + near_ref[j, ROWS : 2 * ROWS, 0:WIDE].astype(F32)
+        out_ref[j, STATE : 2 * STATE, :] = grad.astype(BF16)
+        grad = near[j] * grad + near_ref[j, STATE : 2 * STATE, :].astype(F32)
 
 
 def block_kernel(
-    x_ref, rate_ref, b_ref, c_ref, g_ref, gx_ref, gd_ref, gb_ref, gc_ref, sx_ref, sg_ref, tail_ref, all_ref
+    rate_ref,
+    x_ref,
+    g_ref,
+    b_ref,
+    c_ref,
+    gx_ref,
+    gd_ref,
+    gb_ref,
+    gc_ref,
+    sx_ref,
+    sg_ref,
+    tail_ref,
+    all_ref,
 ):
     rows, columns = cumulative(rate_ref[...])
     length = columns.shape[0]
@@ -185,9 +240,6 @@
 def carried_kernel(
     core_ref,
     state_ref,
-    x_ref,
-    b_ref,
-    c_ref,
     gx_ref,
     gd_ref,
     gb_ref,
@@ -196,30 +248,42 @@
     sg_ref,
     tail_ref,
     all_ref,
-    w_ref,
+    b_in,
+    c_in,
+    w_in,
     out_x_ref,
     out_d_ref,
     out_b_ref,
     out_c_ref,
     keep_ref,
     send_ref,
+    b_ref,
+    c_ref,
     w_vmem,
-    w_sem,
+    sems,
 ):
-    fetch = pltpu.make_async_copy(w_ref, w_vmem, w_sem)
-    fetch.start()
-    length = x_ref.shape[0]
-    state = state_ref[:, 0:ROWS, :].reshape(N, WIDE)
-    grad = state_ref[:, ROWS : 2 * ROWS, :].reshape(N, WIDE)
+    copies = start_copies((b_in, c_in, w_in), (b_ref, c_ref, w_vmem), sems)
+    length = sx_ref.shape[0]
+
+    def whole_state(row):
+        parts = [
+            state_ref[:, row + k * ROWS : row + (k + 1) * ROWS, :].reshape(N, LANES)
+            for k in range(GROUPS)
+        ]
+        return jnp.concatenate(parts, axis=1)
+
+    state, grad = whole_state(0), whole_state(STATE)
     sx, sg = sx_ref[...], sg_ref[...]
     grad_c = (matmul_nt(sg, state) + gc_ref[...]).astype(BF16)
     grad_b = (matmul_nt(sx, grad) + gb_ref[...]).astype(BF16)
     out_b_ref[...] = grad_b
     out_c_ref[...] = grad_c
+    copies[0].wait()
+    copies[1].wait()
     from_state = matmul(c_ref[...], state)
     state_back = matmul(b_ref[...], grad)
     out_x_ref[...] = (gx_ref[...] + tail_ref[...] * state_back).astype(BF16)
-    pick = (iota((HEADS, WIDE), 0) == iota((HEADS, WIDE), 1) // P_SIZE).astype(F32)
+    pick = (iota((HEADS, WIDE), 0) == iota((HEADS, WIDE), 1) >> 6).astype(F32)
     through_head = matmul_nt(pick, sg.astype(F32) * from_state, HIGHEST)
     through_tail = matmul_nt(pick, sx.astype(F32) * state_back, HIGHEST)
     whole = jnp.sum(grad.astype(F32) * state.astype(F32), axis=0, keepdims=True) * all_ref[...]
@@ -240,9 +304,9 @@
     send = jnp.where(first, odd, even)
     both = jnp.concatenate([keep, send], axis=0)
     half = length // 2
-    fetch.wait()
+    copies[2].wait()
     step = 512
-    for k in range(w_ref.shape[1] // step):
+    for k in range(w_vmem.shape[1] // step):
         at = slice(k * step, (k + 1) * step)
         part = matmul(both, w_vmem[:, at]).astype(BF16)
         keep_ref[:, at] = part[:half]
@@ -253,7 +317,7 @@
     return jax.ShapeDtypeStruct(shape, dtype)
 
 
-def call(kernel, out, operands, name, specs=None, scratch=(), flops=0, moved=0):
+def call(kernel, out, operands, name, specs=None, scratch=(), flops=0, moved=0, limit=24):
     return pl.pallas_call(
         kernel,
         out_shape=out,
@@ -261,7 +325,7 @@
         out_specs=jax.tree.map(lambda _: VMEM, out),
         scratch_shapes=list(scratch),
         cost_estimate=pl.CostEstimate(flops=flops, bytes_accessed=moved, transcendentals=0),
-        compiler_params=pltpu.CompilerParams(vmem_limit_bytes=24 * 2**20),
+        compiler_params=pltpu.CompilerParams(vmem_limit_bytes=limit * 2**20),
         name=name,
     )(*operands)
 
@@ -271,24 +335,29 @@
     width = w_bc.shape[2]
     hi = lax.axis_index("hi").astype(jnp.int32).reshape(1)
     core = lax.axis_index("core").astype(jnp.int32).reshape(1)
+    block = (log_decay, inputs, grad_out, b_proj, c_proj)
+    held = [pltpu.VMEM(part.shape, part.dtype) for part in block]
     near = call(
         states_kernel,
-        struct((LO, 2 * ROWS, WIDE + LANES), BF16),
-        (inputs, log_decay, b_proj, c_proj, grad_out),
+        struct((LO, NEAR, LANES), BF16),
+        block,
         "states",
+        specs=[HBM] * 5,
+        scratch=held + [pltpu.SemaphoreType.DMA((5,))],
         flops=4 * length * N * WIDE,
         moved=2**20,
+        limit=60,
     )
     near = lax.all_to_all(near, "lo", 0, 0)
     far = call(
         segment_kernel,
-        struct((HI, ROWS, WIDE + LANES), BF16),
+        struct((HI, FAR, LANES), BF16),
         (hi, near),
         "segment",
         specs=[SMEM, VMEM],
         moved=2**19,
     )
-    far = lax.all_to_all(far, "hi", 0, 0)
+    far = lax.all_to_all(far, "hi", 0, 0, axis_index_groups=[ORDER])
     inside = call(
         block_kernel,
         (
@@ -301,21 +370,22 @@
             struct((length, WIDE), F32),
             struct((HEADS, WIDE), F32),
         ),
-        (inputs, log_decay, b_proj, c_proj, grad_out),
+        block,
         "block",
         flops=2**30,
         moved=4 * 2**20,
     )
+    far, inside = lax.optimization_barrier((far, inside))
     states = call(
         entering_kernel,
-        struct((LO, 2 * ROWS, WIDE), BF16),
+        struct((LO, 2 * STATE, LANES), BF16),
         (hi, far, near),
         "entering",
         specs=[SMEM, VMEM, VMEM],
         moved=2**19,
     )
     states = lax.all_to_all(states, "lo", 0, 0)
-    operands = (core, states, inputs, b_proj, c_proj) + tuple(inside) + (w_bc.reshape(2 * N, width),)
+    operands = (core, states) + tuple(inside) + (b_proj, c_proj, w_bc.reshape(2 * N, width))
     grad_inputs, grad_decay, grad_b, grad_c, keep, send = call(
         carried_kernel,
         (
@@ -328,8 +398,13 @@
         ),
         operands,
         "carried",
-        specs=[SMEM] + [VMEM] * (len(operands) - 2) + [pl.BlockSpec(memory_space=pl.ANY)],
-        scratch=(pltpu.VMEM((2 * N, width), BF16), pltpu.SemaphoreType.DMA),
+        specs=[SMEM] + [VMEM] * (len(operands) - 4) + [HBM] * 3,
+        scratch=(
+            pltpu.VMEM(b_proj.shape, BF16),
+            pltpu.VMEM(c_proj.shape, BF16),
+            pltpu.VMEM((2 * N, width), BF16),
+            pltpu.SemaphoreType.DMA((3,)),
+        ),
         flops=2**29,
         moved=4 * 2**20,
     )

time: 83.5 us -> 74.2 us (0.89)
  blocking collectives: 39.8 us -> 12.4 us
  starting transfers between devices: 17.4 us -> 32.8 us
  waiting for transfers between devices: 10.4 us -> 13.8 us
  local copies, waits for them, and re-layouts: 7.59 us -> 5.3 us
  Pallas kernels: 6.04 us -> 7.71 us
    all_to_all x1 -> x0, blocking collectives: 27.4 us -> none  [local(): far = lax.all_to_all(far, 'hi', 0, 0)]
    all_to_all x0 -> x1, starting transfers between devices: none -> 17 us  [local(): far = lax.all_to_all(far, 'hi', 0, 0, axis_index_groups=[ORDER])]
    all_to_all x1, waiting for transfers between devices: 2.54 us -> 6.08 us  [local(): states = lax.all_to_all(states, 'lo', 0, 0)]
    unnamed x30 -> x20, local copies, waits for them, and re-layouts: 7.59 us -> 5.3 us
    pallas_call x5, Pallas kernels: 6.04 us -> 7.71 us  [call(): pl.pallas_call(kernel, out_shape=out, in_specs=specs or [VMEM] * len(oper...]
    ppermute x1, starting transfers between devices: 7.06 us -> 5.39 us  [local(): other = lax.ppermute(send, 'core', [(0, 1), (1, 0)])]
  transfers between devices with their start and end apart: 3 -> 4, of which waited for: 3 -> 3; matrix products, arithmetic and copies ran while one was open for 0% -> 0% of each run, Pallas kernels for 2% -> 2%
where the time goes in v2:
time: 74.2 us; the launch traced here: 73.5 us
  starting transfers between devices  32.8 us (44%)
  waiting for transfers between devices  13.8 us (19%)
  blocking collectives  12.4 us (17%)
  Pallas kernels  7.71 us (10%)
  local copies, waits for them, and re-layouts  5.3 us (7%)
  other arithmetic  0.86 us (1%)
    all_to_all x1, starting transfers between devices, local(): far = lax.all_to_all(far, 'hi', 0, 0, axis_index_groups=[ORDER])  17 us
    all_to_all x1, blocking collectives, local(): blocks = lax.all_to_all(pair.reshape(4, length // 8, width), 'x', 0, 0)  12.4 us
    pallas_call x5, Pallas kernels, call(): pl.pallas_call(kernel, out_shape=out, in_specs=specs or [VMEM] * len(oper...  7.71 us
    all_to_all x1, starting transfers between devices, local(): near = lax.all_to_all(near, 'lo', 0, 0)  6.4 us
    all_to_all x1, waiting for transfers between devices, local(): near = lax.all_to_all(near, 'lo', 0, 0)  6.21 us
    all_to_all x1, waiting for transfers between devices, local(): states = lax.all_to_all(states, 'lo', 0, 0)  6.08 us
    ppermute x1, starting transfers between devices, local(): other = lax.ppermute(send, 'core', [(0, 1), (1, 0)])  5.39 us
    unnamed x20, local copies, waits for them, and re-layouts  5.3 us
  transfers between devices with their start and end apart: 4, of which 3 were waited for; matrix products, arithmetic and copies ran while one was open for 0% of the time, Pallas kernels for 2%

profile of v2, /device:TPU:1, one launch (start us, length us, event | category | flops | bytes accessed | tf_op | source)
XLA Modules:
  0.0 73.5 jit_solution(7371732049917432933)
XLA Ops:
  0.6 2.4 %states.1 = bf16[8,144,128]{2,1,0:T(8,128)(2,1)} custom-call(f32[8,128]{1,0:T(8,128)} %rate_ref.1, bf16[128,512]{1,0:T(8,128)(2,1)} %x_ref.1, bf16[128,512]{1,0:T(8,128)(2,1)} %g_ref.1, bf16[128,128]{1,0:T(8,128)(2,1)} %b_in.3, bf16[128,128]{1,0:T(8,128)(2,1)} %c_in.3), custom_call_target="tpu_custom_call" | custom-call | flops 33554432 | bytes 1048576 | tf_op jit(solution)/shard_map/states/pallas_call | solution.py:321
  3.0 6.4 %all-to-all-start = ((bf16[8,144,128]{2,1,0:T(8,128)(2,1)}), bf16[8,144,128]{2,1,0:T(8,128)(2,1)S(1)}, u32[]{:S(2)}, u32[]{:S(2)}) async-start(bf16[8,144,128]{2,1,0:T(8,128)(2,1)} %states.1), calls=%async_computation | async-start | bytes 589824 | tf_op jit(solution)/shard_map/all_to_all | solution.py:351
  9.4 6.2 %all-to-all-done.in_ref.near_ref = bf16[8,144,128]{2,1,0:T(8,128)(2,1)S(1)} async-done(((bf16[8,144,128]{2,1,0:T(8,128)(2,1)}), bf16[8,144,128]{2,1,0:T(8,128)(2,1)S(1)}, u32[]{:S(2)}, u32[]{:S(2)}) %all-to-all-start) | async-done | bytes 294944 | tf_op jit(solution)/shard_map/all_to_all | solution.py:351
  15.6 0.9 %segment.1 = bf16[8,80,128]{2,1,0:T(8,128)(2,1)} custom-call(s32[1]{0:T(128)} %bitcast.1.me_ref, bf16[8,144,128]{2,1,0:T(8,128)(2,1)S(1)} %all-to-all-done.in_ref.near_ref), custom_call_target="tpu_custom_call" | custom-call | bytes 524288 | tf_op jit(solution)/shard_map/segment/pallas_call | solution.py:321
  16.5 17.0 %all-to-all-start.1 = ((bf16[8,80,128]{2,1,0:T(8,128)(2,1)}), bf16[8,80,128]{2,1,0:T(8,128)(2,1)S(1)}, u32[]{:S(2)}, u32[]{:S(2)}) async-start(bf16[8,80,128]{2,1,0:T(8,128)(2,1)} %segment.1), calls=%async_computation.1 | async-start | bytes 327680 | tf_op jit(solution)/shard_map/all_to_all | solution.py:360
  33.5 0.0 copy-start.1
  33.5 0.8 %copy-done.1 = bf16[128,128]{1,0:T(8,128)(2,1)S(1)} copy-done((bf16[128,128]{1,0:T(8,128)(2,1)S(1)}, bf16[128,128]{1,0:T(8,128)(2,1)}, u32[]{:S(2)}) %copy-start.1) | copy-done | bytes 32792
  34.3 0.0 copy-start.3
  34.3 0.8 %copy-done.3 = bf16[128,128]{1,0:T(8,128)(2,1)S(1)} copy-done((bf16[128,128]{1,0:T(8,128)(2,1)S(1)}, bf16[128,128]{1,0:T(8,128)(2,1)}, u32[]{:S(2)}) %copy-start.3) | copy-done | bytes 32792
  35.0 0.0 copy-start.5
  35.0 0.9 %copy-done.5 = bf16[128,512]{1,0:T(8,128)(2,1)S(1)} copy-done((bf16[128,512]{1,0:T(8,128)(2,1)S(1)}, bf16[128,512]{1,0:T(8,128)(2,1)}, u32[]{:S(2)}) %copy-start.5) | copy-done | bytes 131096
  35.9 0.0 copy-start.6
  35.9 0.9 %copy-done.6 = bf16[128,512]{1,0:T(8,128)(2,1)S(1)} copy-done((bf16[128,512]{1,0:T(8,128)(2,1)S(1)}, bf16[128,512]{1,0:T(8,128)(2,1)}, u32[]{:S(2)}) %copy-start.6) | copy-done | bytes 131096
  36.8 0.0 copy-start.7
  36.8 0.7 copy-done.7
  37.5 0.0 copy-start
  37.5 0.0 copy-start.2
  37.5 0.0 copy-start.4
  37.5 1.4 %block.1 = (f32[128,512]{1,0:T(8,128)S(1)}, f32[8,128]{1,0:T(8,128)S(1)}, f32[128,128]{1,0:T(8,128)S(1)}, f32[128,128]{1,0:T(8,128)S(1)}, bf16[128,512]{1,0:T(8,...) custom-call(f32[8,128]{1,0:T(8,128)S(1)} %copy-done.7, ...), custom_call_target="tpu_custom_call" | custom-call | flops 1073741824 | bytes 4194304 | tf_op jit(solution)/shard_map/block/pallas_call | solution.py:321
  39.0 0.0 copy-start.8
  39.0 0.6 copy-done.8
  39.6 0.0 all-to-all-done.1.far_ref
  39.6 1.0 %entering.1 = bf16[8,128,128]{2,1,0:T(8,128)(2,1)} custom-call(s32[1]{0:T(128)} %bitcast.1.me_ref, bf16[8,80,128]{2,1,0:T(8,128)(2,1)S(1)} %all-to-all-done.1.far_ref, bf16[8,144,128]{2,1,0:T(8,128)(2,1)S(1)} %all-to-all-done.in_ref.near_ref), custom_call_target="tpu_custom_call" | custom-call | bytes 524288 | tf_op jit(solution)/shard_map/entering/pallas_call | solution.py:321
  40.5 4.0 %all-to-all-start.2 = ((bf16[8,128,128]{2,1,0:T(8,128)(2,1)}), bf16[8,128,128]{2,1,0:T(8,128)(2,1)S(1)}, u32[]{:S(2)}, u32[]{:S(2)}) async-start(bf16[8,128,128]{2,1,0:T(8,128)(2,1)} %entering.1), calls=%async_computation.2 | async-start | bytes 524288 | tf_op jit(solution)/shard_map/all_to_all | solution.py:387
  44.5 6.1 %all-to-all-done.2.state_ref = bf16[8,128,128]{2,1,0:T(8,128)(2,1)S(1)} async-done(((bf16[8,128,128]{2,1,0:T(8,128)(2,1)}), bf16[8,128,128]{2,1,0:T(8,128)(2,1)S(1)}, u32[]{:S(2)}, u32[]{:S(2)}) %all-to-all-start.2) | async-done | bytes 262176 | tf_op jit(solution)/shard_map/all_to_all | solution.py:387
  50.6 0.0 copy-done
  50.6 0.0 copy-done.2
  50.6 0.0 copy-done.4
  50.6 0.0 copy-start.9
  50.6 0.7 copy-done.9
  51.3 2.0 %carried.1 = (bf16[128,512]{1,0:T(8,128)(2,1)}, f32[8,128]{1,0:T(8,128)}, bf16[128,128]{1,0:T(8,128)(2,1)}, bf16[128,128]{1,0:T(8,128)(2,1)}, bf16[64,4096]{1,0:...) custom-call(s32[1]{0:T(128)} %bitcast.core_ref, bf16[8,128,128]{2,1,0:T(8,128)(2,1)S(1)} %all-to-all-done.2.state_ref, ...), custom_call_target="tpu_custom_call" | custom-call | flops 536870912 | bytes 4194304 | tf_op jit(solution)/shard_map/carried/pallas_call | solution.py:321
  53.3 5.4 %collective-permute-start = (bf16[64,4096]{1,0:T(8,128)(2,1)S(1)}, bf16[64,4096]{1,0:T(8,128)(2,1)S(1)}, u32[]{:S(2)}, u32[]{:S(2)}) collective-permute-start(bf16[64,4096]{1,0:T(8,128)(2,1)S(1)} %get-tuple-element.50), channel_id=1, source_target_pairs={{0,1},{1,0},{2,3},{3,2},{4,5},{5,4},{6,7},{7,6},{8,9},{9,8},{10,11... | collective-permute-start | bytes 1572872 | tf_op jit(solution)/shard_map/ppermute | solution.py:411
  58.7 1.5 %collective-permute-done = bf16[64,4096]{1,0:T(8,128)(2,1)S(1)} collective-permute-done((bf16[64,4096]{1,0:T(8,128)(2,1)S(1)}, bf16[64,4096]{1,0:T(8,128)(2,1)S(1)}, u32[]{:S(2)}, u32[]{:S(2)}) %collective-permute-start) | collective-permute-done | bytes 524320 | tf_op jit(solution)/shard_map/ppermute | solution.py:411
  60.3 0.1 add_convert_fusion
  60.4 12.4 %all_to_all.20 = bf16[4,16,4096]{2,1,0:T(8,128)(2,1)S(1)} all-to-all(bf16[4,16,4096]{2,1,0:T(8,128)(2,1)S(1)} %bitcast.5), channel_id=1, replica_groups=mesh['hi'=8,'lo'=8,'x'=4,'core'=2] {'x'}, dimensions={0} | all-to-all | bytes 1048576 | tf_op jit(solution)/shard_map/all_to_all | solution.py:413
  72.8 0.7 %reduce_sum.12 = bf16[16,4096]{1,0:T(8,128)(2,1)} reduce(bf16[4,16,4096]{2,1,0:T(8,128)(2,1)S(1)} %all_to_all.20, bf16[]{:T(256)} %constant.12.clone.1), dimensions={0}, to_apply=%region_0.0 | reduce | flops 196608 | bytes 655362 | tf_op jit(solution)/shard_map/reduce_sum | solution.py:414
Async XLA Ops:
  3.0 12.6 %all-to-all-start = ((bf16[8,144,128]{2,1,0:T(8,128)(2,1)}), bf16[8,144,128]{2,1,0:T(8,128)(2,1)S(1)}, u32[]{:S(2)}, u32[]{:S(2)}) async-start(bf16[8,144,128]{2,1,0:T(8,128)(2,1)} %states.1), calls=%async_computation | async-start | bytes 589824 | tf_op jit(solution)/shard_map/all_to_all | solution.py:351
  16.5 23.0 %all-to-all-start.1 = ((bf16[8,80,128]{2,1,0:T(8,128)(2,1)}), bf16[8,80,128]{2,1,0:T(8,128)(2,1)S(1)}, u32[]{:S(2)}, u32[]{:S(2)}) async-start(bf16[8,80,128]{2,1,0:T(8,128)(2,1)} %segment.1), calls=%async_computation.1 | async-start | bytes 327680 | tf_op jit(solution)/shard_map/all_to_all | solution.py:360
  33.5 0.8 %copy-start.1 = (bf16[128,128]{1,0:T(8,128)(2,1)S(1)}, bf16[128,128]{1,0:T(8,128)(2,1)}, u32[]{:S(2)}) copy-start(bf16[128,128]{1,0:T(8,128)(2,1)} %b_in.3) | copy-start | bytes 98308
  34.3 0.8 %copy-start.3 = (bf16[128,128]{1,0:T(8,128)(2,1)S(1)}, bf16[128,128]{1,0:T(8,128)(2,1)}, u32[]{:S(2)}) copy-start(bf16[128,128]{1,0:T(8,128)(2,1)} %c_in.3) | copy-start | bytes 98308
  35.0 0.9 %copy-start.5 = (bf16[128,512]{1,0:T(8,128)(2,1)S(1)}, bf16[128,512]{1,0:T(8,128)(2,1)}, u32[]{:S(2)}) copy-start(bf16[128,512]{1,0:T(8,128)(2,1)} %x_ref.1) | copy-start | bytes 393220
  35.9 0.9 %copy-start.6 = (bf16[128,512]{1,0:T(8,128)(2,1)S(1)}, bf16[128,512]{1,0:T(8,128)(2,1)}, u32[]{:S(2)}) copy-start(bf16[128,512]{1,0:T(8,128)(2,1)} %g_ref.1) | copy-start | bytes 393220
  36.8 0.7 copy-start.7
  37.5 13.1 %copy-start = (bf16[2,128,4096]{2,1,0:T(8,128)(2,1)S(1)}, bf16[2,128,4096]{2,1,0:T(8,128)(2,1)}, u32[]{:S(2)}) copy-start(bf16[2,128,4096]{2,1,0:T(8,128)(2,1)} %param.11) | copy-start | bytes 6291460
  37.5 13.1 %copy-start.2 = (bf16[128,128]{1,0:T(8,128)(2,1)S(1)}, bf16[128,128]{1,0:T(8,128)(2,1)}, u32[]{:S(2)}) copy-start(bf16[128,128]{1,0:T(8,128)(2,1)} %b_in.3) | copy-start | bytes 98308
  37.5 13.1 %copy-start.4 = (bf16[128,128]{1,0:T(8,128)(2,1)S(1)}, bf16[128,128]{1,0:T(8,128)(2,1)}, u32[]{:S(2)}) copy-start(bf16[128,128]{1,0:T(8,128)(2,1)} %c_in.3) | copy-start | bytes 98308
  39.0 0.6 copy-start.8
  40.5 10.1 %all-to-all-start.2 = ((bf16[8,128,128]{2,1,0:T(8,128)(2,1)}), bf16[8,128,128]{2,1,0:T(8,128)(2,1)S(1)}, u32[]{:S(2)}, u32[]{:S(2)}) async-start(bf16[8,128,128]{2,1,0:T(8,128)(2,1)} %entering.1), calls=%async_computation.2 | async-start | bytes 524288 | tf_op jit(solution)/shard_map/all_to_all | solution.py:387
  50.6 0.7 copy-start.9
  53.3 6.9 %collective-permute-start = (bf16[64,4096]{1,0:T(8,128)(2,1)S(1)}, bf16[64,4096]{1,0:T(8,128)(2,1)S(1)}, u32[]{:S(2)}, u32[]{:S(2)}) collective-permute-start(bf16[64,4096]{1,0:T(8,128)(2,1)S(1)} %get-tuple-element.50), channel_id=1, source_target_pairs={{0,1},{1,0},{2,3},{3,2},{4,5},{5,4},{6,7},{7,6},{8,9},{9,8},{10,11... | collective-permute-start | bytes 1572872 | tf_op jit(solution)/shard_map/ppermute | solution.py:411

commit v3 on v2

--- a/solution.py
+++ b/solution.py
@@ -22,8 +22,11 @@
 STATE = GROUPS * ROWS
 NEAR = 2 * STATE + 16
 FAR = STATE + 16
-FIRST = 4
-ORDER = [(k + FIRST) & (HI - 1) for k in range(HI)]
+NEAR_ORDER = [4, 5, 6, 7, 0, 1, 2, 3]
+FAR_ORDER = [4, 5, 6, 7, 0, 1, 2, 3]
+BACK_ORDER = [6, 7, 0, 1, 2, 3, 4, 5]
+X_ORDER = [2, 3, 0, 1]
+NEAR_ORDER_OF = [NEAR_ORDER.index(k) for k in range(LO)]
 VMEM = pl.BlockSpec(memory_space=pltpu.VMEM)
 HBM = pl.BlockSpec(memory_space=pltpu.HBM)
 SMEM = pl.BlockSpec(memory_space=pltpu.SMEM)
@@ -107,13 +110,13 @@
     scaled_grads = (g_ref[...].astype(F32) * head).astype(BF16)
     state = matmul_tn(b_ref[...], scaled_inputs).astype(BF16)
     grad = matmul_tn(c_ref[...], scaled_grads).astype(BF16)
-    for block in range(LO):
+    for place, block in enumerate(NEAR_ORDER):
         rows = slice(block * ROWS, (block + 1) * ROWS)
         for k in range(GROUPS):
             at = slice(k * LANES, (k + 1) * LANES)
-            out_ref[block, k * ROWS : (k + 1) * ROWS, :] = state[rows, at]
-            out_ref[block, STATE + k * ROWS : STATE + (k + 1) * ROWS, :] = grad[rows, at]
-        out_ref[block, 2 * STATE : NEAR, :] = total
+            out_ref[place, k * ROWS : (k + 1) * ROWS, :] = state[rows, at]
+            out_ref[place, STATE + k * ROWS : STATE + (k + 1) * ROWS, :] = grad[rows, at]
+        out_ref[place, 2 * STATE : NEAR, :] = total
 
 
 def totals_of(ref, row):
@@ -142,9 +145,9 @@
     decay = chunk_decays(wide)
     state = jnp.zeros((STATE, LANES), F32)
     grad = jnp.zeros((STATE, LANES), F32)
-    for k in range(LO):
+    for k in NEAR_ORDER_OF:
         state = decay[k] * state + in_ref[k, 0:STATE, :].astype(F32)
-        j = LO - 1 - k
+    for j in reversed(NEAR_ORDER_OF):
         grad = decay[j] * grad + in_ref[j, STATE : 2 * STATE, :].astype(F32)
     lane, other = iota((LANES, LANES), 0), iota((LANES, LANES), 1)
     fold = jnp.logical_and((lane & 7) == (other & 7), lane < 3 * HEADS).astype(F32)
@@ -152,7 +155,7 @@
     total = jnp.broadcast_to(split_three(total), (FAR - STATE, LANES))
     state = state.astype(BF16)
     grad = grad.astype(BF16)
-    for k, segment in enumerate(ORDER):
+    for k, segment in enumerate(FAR_ORDER):
         out_ref[k, 0:STATE, :] = jnp.where(segment > me, state, grad)
         out_ref[k, STATE:FAR, :] = total
 
@@ -164,45 +167,53 @@
     state = jnp.zeros((STATE, LANES), F32)
     grad = jnp.zeros((STATE, LANES), F32)
     for k in range(HI):
-        at = ORDER.index(k)
+        at = FAR_ORDER.index(k)
         new = far[at] * state + far_ref[at, 0:STATE, :].astype(F32)
         state = jnp.where(k < me, new, state)
         j = HI - 1 - k
-        at = ORDER.index(j)
+        at = FAR_ORDER.index(j)
         new = far[at] * grad + far_ref[at, 0:STATE, :].astype(F32)
         grad = jnp.where(j > me, new, grad)
     for k in range(LO):
-        out_ref[k, 0:STATE, :] = state.astype(BF16)
-        state = near[k] * state + near_ref[k, 0:STATE, :].astype(F32)
-        j = LO - 1 - k
-        out_ref[j, STATE : 2 * STATE, :] = grad.astype(BF16)
+        at = NEAR_ORDER.index(k)
+        out_ref[BACK_ORDER.index(k), 0:STATE, :] = state.astype(BF16)
+        state = near[at] * state + near_ref[at, 0:STATE, :].astype(F32)
+        k = LO - 1 - k
+        j = NEAR_ORDER.index(k)
+        out_ref[BACK_ORDER.index(k), STATE : 2 * STATE, :] = grad.astype(BF16)
         grad = near[j] * grad + near_ref[j, STATE : 2 * STATE, :].astype(F32)
 
 
 def block_kernel(
+    rate_in,
+    x_in,
+    g_in,
+    b_in,
+    c_in,
+    wide_ref,
+    narrow_ref,
+    scaled_ref,
     rate_ref,
     x_ref,
     g_ref,
     b_ref,
     c_ref,
-    gx_ref,
-    gd_ref,
-    gb_ref,
-    gc_ref,
-    sx_ref,
-    sg_ref,
-    tail_ref,
-    all_ref,
+    sems,
 ):
+    copies = start_copies(
+        (rate_in, x_in, g_in, b_in, c_in), (rate_ref, x_ref, g_ref, b_ref, c_ref), sems
+    )
+    for copy in copies:
+        copy.wait()
     rows, columns = cumulative(rate_ref[...])
     length = columns.shape[0]
     wide = widen(columns)
     last = wide[length - 1 : length]
     tail = jnp.exp(last - wide)
-    tail_ref[...] = tail
-    all_ref[...] = jnp.broadcast_to(jnp.exp(last), all_ref.shape)
-    sx_ref[...] = (x_ref[...].astype(F32) * tail).astype(BF16)
-    sg_ref[...] = (g_ref[...].astype(F32) * jnp.exp(wide)).astype(BF16)
+    wide_ref[length : 2 * length, :] = tail
+    wide_ref[2 * length : 2 * length + 8, :] = jnp.broadcast_to(jnp.exp(last), (8, WIDE))
+    scaled_ref[0:length, :] = (x_ref[...].astype(F32) * tail).astype(BF16)
+    scaled_ref[length : 2 * length, :] = (g_ref[...].astype(F32) * jnp.exp(wide)).astype(BF16)
     b, c = b_ref[...], c_ref[...]
     scores = matmul_nt(b, c)
     source, target = iota((length, length), 0), iota((length, length), 1)
@@ -231,26 +242,21 @@
             decay_rows.append(jnp.sum(jnp.where(before, through, 0.0), axis=0, keepdims=True))
             weights.append(weight.astype(BF16))
             masked.append(g_mine)
-        gx_ref[:, at] = matmul(jnp.concatenate(weights, axis=1), jnp.concatenate(masked, axis=0))
-    gd_ref[...] = jnp.concatenate(decay_rows, axis=0)
-    gb_ref[...] = matmul(grad_scores.astype(BF16), c)
-    gc_ref[...] = matmul(jnp.transpose(grad_scores).astype(BF16), b)
+        wide_ref[0:length, at] = matmul(jnp.concatenate(weights, axis=1), jnp.concatenate(masked, axis=0))
+    narrow_ref[2 * length : 2 * length + HEADS, :] = jnp.concatenate(decay_rows, axis=0)
+    narrow_ref[0:length, :] = matmul(grad_scores.astype(BF16), c)
+    narrow_ref[length : 2 * length, :] = matmul(jnp.transpose(grad_scores).astype(BF16), b)
 
 
 def carried_kernel(
     core_ref,
     state_ref,
-    gx_ref,
-    gd_ref,
-    gb_ref,
-    gc_ref,
-    sx_ref,
-    sg_ref,
-    tail_ref,
-    all_ref,
+    wide_ref,
+    narrow_ref,
+    scaled_ref,
+    w_ref,
     b_in,
     c_in,
-    w_in,
     out_x_ref,
     out_d_ref,
     out_b_ref,
@@ -259,56 +265,57 @@
     send_ref,
     b_ref,
     c_ref,
-    w_vmem,
     sems,
 ):
-    copies = start_copies((b_in, c_in, w_in), (b_ref, c_ref, w_vmem), sems)
-    length = sx_ref.shape[0]
+    copies = start_copies((b_in, c_in), (b_ref, c_ref), sems)
+    length = b_ref.shape[0]
+    first, second = slice(0, length), slice(length, 2 * length)
+    heads = slice(2 * length, 2 * length + HEADS)
 
     def whole_state(row):
-        parts = [
-            state_ref[:, row + k * ROWS : row + (k + 1) * ROWS, :].reshape(N, LANES)
-            for k in range(GROUPS)
-        ]
+        parts = []
+        for k in range(GROUPS):
+            at = slice(row + k * ROWS, row + (k + 1) * ROWS)
+            chunks = [state_ref[BACK_ORDER.index(block), at, :] for block in range(LO)]
+            parts.append(jnp.concatenate(chunks, axis=0))
         return jnp.concatenate(parts, axis=1)
 
     state, grad = whole_state(0), whole_state(STATE)
-    sx, sg = sx_ref[...], sg_ref[...]
-    grad_c = (matmul_nt(sg, state) + gc_ref[...]).astype(BF16)
-    grad_b = (matmul_nt(sx, grad) + gb_ref[...]).astype(BF16)
+    sx, sg = scaled_ref[first, :], scaled_ref[second, :]
+    grad_c = (matmul_nt(sg, state) + narrow_ref[second, :]).astype(BF16)
+    grad_b = (matmul_nt(sx, grad) + narrow_ref[first, :]).astype(BF16)
     out_b_ref[...] = grad_b
     out_c_ref[...] = grad_c
     copies[0].wait()
     copies[1].wait()
     from_state = matmul(c_ref[...], state)
     state_back = matmul(b_ref[...], grad)
-    out_x_ref[...] = (gx_ref[...] + tail_ref[...] * state_back).astype(BF16)
+    out_x_ref[...] = (wide_ref[first, :] + wide_ref[second, :] * state_back).astype(BF16)
     pick = (iota((HEADS, WIDE), 0) == iota((HEADS, WIDE), 1) >> 6).astype(F32)
     through_head = matmul_nt(pick, sg.astype(F32) * from_state, HIGHEST)
     through_tail = matmul_nt(pick, sx.astype(F32) * state_back, HIGHEST)
-    whole = jnp.sum(grad.astype(F32) * state.astype(F32), axis=0, keepdims=True) * all_ref[...]
+    whole = jnp.sum(grad.astype(F32) * state.astype(F32), axis=0, keepdims=True) * wide_ref[heads, :]
     whole = jnp.sum(pick * whole, axis=1, keepdims=True)
     one, two = iota((length, length), 0), iota((length, length), 1)
     out_d_ref[...] = (
-        gd_ref[...]
+        narrow_ref[heads, :]
         + matmul(through_head, (one >= two).astype(F32), HIGHEST)
         + matmul(through_tail, (one < two).astype(F32), HIGHEST)
         + whole
     )
     both = jnp.concatenate([grad_b, grad_c], axis=1)
     sixteen = length // 8
-    even = jnp.concatenate([both[2 * k * sixteen : (2 * k + 1) * sixteen] for k in range(4)], axis=0)
-    odd = jnp.concatenate([both[(2 * k + 1) * sixteen : (2 * k + 2) * sixteen] for k in range(4)], axis=0)
-    first = core_ref[0] == 0
-    keep = jnp.where(first, even, odd)
-    send = jnp.where(first, odd, even)
+    even = jnp.concatenate([both[2 * k * sixteen : (2 * k + 1) * sixteen] for k in X_ORDER], axis=0)
+    odd = jnp.concatenate([both[(2 * k + 1) * sixteen : (2 * k + 2) * sixteen] for k in X_ORDER], axis=0)
+    here = core_ref[0] == 0
+    keep = jnp.where(here, even, odd)
+    send = jnp.where(here, odd, even)
     both = jnp.concatenate([keep, send], axis=0)
     half = length // 2
-    copies[2].wait()
     step = 512
-    for k in range(w_vmem.shape[1] // step):
+    for k in range(w_ref.shape[1] // step):
         at = slice(k * step, (k + 1) * step)
-        part = matmul(both, w_vmem[:, at]).astype(BF16)
+        part = matmul(both, w_ref[:, at]).astype(BF16)
         keep_ref[:, at] = part[:half]
         send_ref[:, at] = part[half:]
 
@@ -335,7 +342,10 @@
     width = w_bc.shape[2]
     hi = lax.axis_index("hi").astype(jnp.int32).reshape(1)
     core = lax.axis_index("core").astype(jnp.int32).reshape(1)
-    block = (log_decay, inputs, grad_out, b_proj, c_proj)
+    block = [
+        pltpu.with_memory_space_constraint(part, pltpu.HBM)
+        for part in (log_decay, inputs, grad_out, b_proj, c_proj)
+    ]
     held = [pltpu.VMEM(part.shape, part.dtype) for part in block]
     near = call(
         states_kernel,
@@ -346,9 +356,8 @@
         scratch=held + [pltpu.SemaphoreType.DMA((5,))],
         flops=4 * length * N * WIDE,
         moved=2**20,
-        limit=60,
-    )
-    near = lax.all_to_all(near, "lo", 0, 0)
+    )
+    near = lax.all_to_all(near, "lo", 0, 0, axis_index_groups=[NEAR_ORDER])
     far = call(
         segment_kernel,
         struct((HI, FAR, LANES), BF16),
@@ -357,21 +366,18 @@
         specs=[SMEM, VMEM],
         moved=2**19,
     )
-    far = lax.all_to_all(far, "hi", 0, 0, axis_index_groups=[ORDER])
+    far = lax.all_to_all(far, "hi", 0, 0, axis_index_groups=[FAR_ORDER])
     inside = call(
         block_kernel,
         (
-            struct((length, WIDE), F32),
-            struct((HEADS, length), F32),
-            struct((length, N), F32),
-            struct((length, N), F32),
-            struct((length, WIDE), BF16),
-            struct((length, WIDE), BF16),
-            struct((length, WIDE), F32),
-            struct((HEADS, WIDE), F32),
+            struct((2 * length + HEADS, WIDE), F32),
+            struct((2 * length + HEADS, N), F32),
+            struct((2 * length, WIDE), BF16),
         ),
         block,
         "block",
+        specs=[HBM] * 5,
+        scratch=held + [pltpu.SemaphoreType.DMA((5,))],
         flops=2**30,
         moved=4 * 2**20,
     )
@@ -384,8 +390,8 @@
         specs=[SMEM, VMEM, VMEM],
         moved=2**19,
     )
-    states = lax.all_to_all(states, "lo", 0, 0)
-    operands = (core, states) + tuple(inside) + (b_proj, c_proj, w_bc.reshape(2 * N, width))
+    states = lax.all_to_all(states, "lo", 0, 0, axis_index_groups=[BACK_ORDER])
+    operands = (core, states) + tuple(inside) + (w_bc.reshape(2 * N, width), block[3], block[4])
     grad_inputs, grad_decay, grad_b, grad_c, keep, send = call(
         carried_kernel,
         (
@@ -398,19 +404,19 @@
         ),
         operands,
         "carried",
-        specs=[SMEM] + [VMEM] * (len(operands) - 4) + [HBM] * 3,
+        specs=[SMEM] + [VMEM] * (len(operands) - 3) + [HBM] * 2,
         scratch=(
             pltpu.VMEM(b_proj.shape, BF16),
             pltpu.VMEM(c_proj.shape, BF16),
-            pltpu.VMEM((2 * N, width), BF16),
-            pltpu.SemaphoreType.DMA((3,)),
+            pltpu.SemaphoreType.DMA((2,)),
         ),
         flops=2**29,
         moved=4 * 2**20,
     )
     other = lax.ppermute(send, "core", [(0, 1), (1, 0)])
     pair = (keep.astype(F32) + other.astype(F32)).astype(BF16)
-    blocks = lax.all_to_all(pair.reshape(4, length // 8, width), "x", 0, 0)
+    blocks = pair.reshape(4, length // 8, width)
+    blocks = lax.all_to_all(blocks, "x", 0, 0, axis_index_groups=[X_ORDER])
     grad_tokens = jnp.sum(blocks.astype(F32), axis=0).astype(BF16)
     return grad_inputs, grad_decay, grad_b, grad_c, grad_tokens
 

time: 74.2 us -> 71.6 us (0.965)
  local copies, waits for them, and re-layouts: 5.3 us -> 0.01 us
  starting transfers between devices: 32.8 us -> 37 us
  waiting for transfers between devices: 13.8 us -> 11.5 us
  Pallas kernels: 7.71 us -> 9.45 us
  blocking collectives: 12.4 us -> 11.6 us
    unnamed x20 -> x2, local copies, waits for them, and re-layouts: 5.3 us -> 0.01 us
    all_to_all x3, starting transfers between devices: 27.4 us -> 31.6 us  [the longest x1 17.4 us: local(): far = lax.all_to_all(far, 'hi', 0, 0, axis_index_groups=[FAR_ORDER])]
    all_to_all x3, waiting for transfers between devices: 12.3 us -> 9.98 us  [the longest x1 5.13 us: local(): near = lax.all_to_all(near, 'lo', 0, 0, axis_index_groups=[NEAR_ORDER])]
    pallas_call x5, Pallas kernels: 7.71 us -> 9.45 us  [call(): pl.pallas_call(kernel, out_shape=out, in_specs=specs or [VMEM] * len(oper...]
    all_to_all x1, blocking collectives: 12.4 us -> 11.6 us  [local(): blocks = lax.all_to_all(blocks, 'x', 0, 0, axis_index_groups=[X_ORDER])]
  transfers between devices with their start and end apart: 4 -> 4, of which waited for: 3 -> 4; matrix products, arithmetic and copies ran while one was open for 0% -> 0% of each run, Pallas kernels for 2% -> 4%
where the time goes in v3:
time: 71.6 us; the launch traced here: 71.1 us
  starting transfers between devices  37 us (52%)
  blocking collectives  11.6 us (16%)
  waiting for transfers between devices  11.5 us (16%)
  Pallas kernels  9.45 us (13%)
  other arithmetic  0.86 us (1%)
    all_to_all x1, starting transfers between devices, local(): far = lax.all_to_all(far, 'hi', 0, 0, axis_index_groups=[FAR_ORDER])  17.4 us
    all_to_all x1, blocking collectives, local(): blocks = lax.all_to_all(blocks, 'x', 0, 0, axis_index_groups=[X_ORDER])  11.6 us
    pallas_call x5, Pallas kernels, call(): pl.pallas_call(kernel, out_shape=out, in_specs=specs or [VMEM] * len(oper...  9.45 us
    all_to_all x1, starting transfers between devices, local(): states = lax.all_to_all(states, 'lo', 0, 0, axis_index_groups=[BACK_ORDER])  7.51 us
    all_to_all x1, starting transfers between devices, local(): near = lax.all_to_all(near, 'lo', 0, 0, axis_index_groups=[NEAR_ORDER])  6.68 us
    ppermute x1, starting transfers between devices, local(): other = lax.ppermute(send, 'core', [(0, 1), (1, 0)])  5.43 us
    all_to_all x1, waiting for transfers between devices, local(): near = lax.all_to_all(near, 'lo', 0, 0, axis_index_groups=[NEAR_ORDER])  5.13 us
    all_to_all x1, waiting for transfers between devices, local(): states = lax.all_to_all(states, 'lo', 0, 0, axis_index_groups=[BACK_ORDER])  2.85 us
  transfers between devices with their start and end apart: 4, of which 4 were waited for; matrix products, arithmetic and copies ran while one was open for 0% of the time, Pallas kernels for 4%

profile of v3, /device:TPU:1, one launch (start us, length us, event | category | flops | bytes accessed | tf_op | source)
XLA Modules:
  0.0 71.1 jit_solution(13555107810379303310)
XLA Ops:
  0.6 2.4 %states.1 = bf16[8,144,128]{2,1,0:T(8,128)(2,1)} custom-call(f32[8,128]{1,0:T(8,128)} %rate_in.3, bf16[128,512]{1,0:T(8,128)(2,1)} %x_in.3, bf16[128,512]{1,0:T(8,128)(2,1)} %g_in.3, bf16[128,128]{1,0:T(8,128)(2,1)} %b_in.5, bf16[128,128]{1,0:T(8,128)(2,1)} %c_in.5), custom_call_target="tpu_custom_call" | custom-call | flops 33554432 | bytes 1048576 | tf_op jit(solution)/shard_map/states/pallas_call | solution.py:328
  3.0 6.7 %all-to-all-start = ((bf16[8,144,128]{2,1,0:T(8,128)(2,1)}), bf16[8,144,128]{2,1,0:T(8,128)(2,1)S(1)}, u32[]{:S(2)}, u32[]{:S(2)}) async-start(bf16[8,144,128]{2,1,0:T(8,128)(2,1)} %states.1), calls=%async_computation | async-start | bytes 589824 | tf_op jit(solution)/shard_map/all_to_all | solution.py:360
  9.7 5.1 %all-to-all-done.in_ref.near_ref = bf16[8,144,128]{2,1,0:T(8,128)(2,1)S(1)} async-done(((bf16[8,144,128]{2,1,0:T(8,128)(2,1)}), bf16[8,144,128]{2,1,0:T(8,128)(2,1)S(1)}, u32[]{:S(2)}, u32[]{:S(2)}) %all-to-all-start) | async-done | bytes 294944 | tf_op jit(solution)/shard_map/all_to_all | solution.py:360
  14.8 0.9 %segment.1 = bf16[8,80,128]{2,1,0:T(8,128)(2,1)} custom-call(s32[1]{0:T(128)} %bitcast.1.me_ref, bf16[8,144,128]{2,1,0:T(8,128)(2,1)S(1)} %all-to-all-done.in_ref.near_ref), custom_call_target="tpu_custom_call" | custom-call | bytes 524288 | tf_op jit(solution)/shard_map/segment/pallas_call | solution.py:328
  15.7 17.4 %all-to-all-start.1 = ((bf16[8,80,128]{2,1,0:T(8,128)(2,1)}), bf16[8,80,128]{2,1,0:T(8,128)(2,1)S(1)}, u32[]{:S(2)}, u32[]{:S(2)}) async-start(bf16[8,80,128]{2,1,0:T(8,128)(2,1)} %segment.1), calls=%async_computation.1 | async-start | bytes 327680 | tf_op jit(solution)/shard_map/all_to_all | solution.py:369
  33.1 0.0 copy-start
  33.1 2.6 %block.1 = (f32[264,512]{1,0:T(8,128)S(1)}, f32[264,128]{1,0:T(8,128)S(1)}, bf16[256,512]{1,0:T(8,128)(2,1)S(1)}) custom-call(f32[8,128]{1,0:T(8,128)} %rate_in.3, bf16[128,512]{1,0:T(8,128)(2,1)} %x_in.3, bf16[128,512]{1,0:T(8,128)(2,1)} %g_in.3, bf16[128,128]{1,0:T(8,128)(2,1)} %b_in.5, bf16[128,128]{1,0:T(8,128)(2,1)} %c_in.5), custom_call_target="tpu_custom_call" | custom-call | flops 1073741824 | bytes 4194304 | tf_op jit(solution)/shard_map/block/pallas_call | solution.py:328
  35.7 2.0 %all-to-all-done.1.far_ref = bf16[8,80,128]{2,1,0:T(8,128)(2,1)S(1)} async-done(((bf16[8,80,128]{2,1,0:T(8,128)(2,1)}), bf16[8,80,128]{2,1,0:T(8,128)(2,1)S(1)}, u32[]{:S(2)}, u32[]{:S(2)}) %all-to-all-start.1) | async-done | bytes 163872 | tf_op jit(solution)/shard_map/all_to_all | solution.py:369
  37.7 1.0 %entering.1 = bf16[8,128,128]{2,1,0:T(8,128)(2,1)} custom-call(s32[1]{0:T(128)} %bitcast.1.me_ref, bf16[8,80,128]{2,1,0:T(8,128)(2,1)S(1)} %all-to-all-done.1.far_ref, bf16[8,144,128]{2,1,0:T(8,128)(2,1)S(1)} %all-to-all-done.in_ref.near_ref), custom_call_target="tpu_custom_call" | custom-call | bytes 524288 | tf_op jit(solution)/shard_map/entering/pallas_call | solution.py:328
  38.7 7.5 %all-to-all-start.2 = ((bf16[8,128,128]{2,1,0:T(8,128)(2,1)}), bf16[8,128,128]{2,1,0:T(8,128)(2,1)S(1)}, u32[]{:S(2)}, u32[]{:S(2)}) async-start(bf16[8,128,128]{2,1,0:T(8,128)(2,1)} %entering.1), calls=%async_computation.2 | async-start | bytes 524288 | tf_op jit(solution)/shard_map/all_to_all | solution.py:393
  46.2 2.8 %all-to-all-done.2.state_ref = bf16[8,128,128]{2,1,0:T(8,128)(2,1)S(1)} async-done(((bf16[8,128,128]{2,1,0:T(8,128)(2,1)}), bf16[8,128,128]{2,1,0:T(8,128)(2,1)S(1)}, u32[]{:S(2)}, u32[]{:S(2)}) %all-to-all-start.2) | async-done | bytes 262176 | tf_op jit(solution)/shard_map/all_to_all | solution.py:393
  49.0 0.0 copy-done
  49.0 2.6 %carried.1 = (bf16[128,512]{1,0:T(8,128)(2,1)}, f32[8,128]{1,0:T(8,128)}, bf16[128,128]{1,0:T(8,128)(2,1)}, bf16[128,128]{1,0:T(8,128)(2,1)}, bf16[64,4096]{1,0:...) custom-call(s32[1]{0:T(128)} %bitcast.core_ref, bf16[8,128,128]{2,1,0:T(8,128)(2,1)S(1)} %all-to-all-done.2.state_ref, ...), custom_call_target="tpu_custom_call" | custom-call | flops 536870912 | bytes 4194304 | tf_op jit(solution)/shard_map/carried/pallas_call | solution.py:328
  51.6 5.4 %collective-permute-start = (bf16[64,4096]{1,0:T(8,128)(2,1)S(1)}, bf16[64,4096]{1,0:T(8,128)(2,1)S(1)}, u32[]{:S(2)}, u32[]{:S(2)}) collective-permute-start(bf16[64,4096]{1,0:T(8,128)(2,1)S(1)} %get-tuple-element.30), channel_id=1, source_target_pairs={{0,1},{1,0},{2,3},{3,2},{4,5},{5,4},{6,7},{7,6},{8,9},{9,8},{10,11... | collective-permute-start | bytes 1572872 | tf_op jit(solution)/shard_map/ppermute | solution.py:416
  57.1 1.5 %collective-permute-done = bf16[64,4096]{1,0:T(8,128)(2,1)S(1)} collective-permute-done((bf16[64,4096]{1,0:T(8,128)(2,1)S(1)}, bf16[64,4096]{1,0:T(8,128)(2,1)S(1)}, u32[]{:S(2)}, u32[]{:S(2)}) %collective-permute-start) | collective-permute-done | bytes 524320 | tf_op jit(solution)/shard_map/ppermute | solution.py:416
  58.6 0.1 add_convert_fusion
  58.7 11.6 %all_to_all.20 = bf16[4,16,4096]{2,1,0:T(8,128)(2,1)S(1)} all-to-all(bf16[4,16,4096]{2,1,0:T(8,128)(2,1)S(1)} %bitcast.5), channel_id=1, replica_groups={{4,6,0,2},{5,7,1,3},{12,14,8,10},{13,15,9,11},{20,22,16,18},{21,23,17,1..., dimensions={0} | all-to-all | bytes 1048576 | tf_op jit(solution)/shard_map/all_to_all | solution.py:419
  70.3 0.7 %reduce_sum.12 = bf16[16,4096]{1,0:T(8,128)(2,1)} reduce(bf16[4,16,4096]{2,1,0:T(8,128)(2,1)S(1)} %all_to_all.20, bf16[]{:T(256)} %constant.12.clone.1), dimensions={0}, to_apply=%region_0.0 | reduce | flops 196608 | bytes 655362 | tf_op jit(solution)/shard_map/reduce_sum | solution.py:420
Async XLA Ops:
  3.0 11.8 %all-to-all-start = ((bf16[8,144,128]{2,1,0:T(8,128)(2,1)}), bf16[8,144,128]{2,1,0:T(8,128)(2,1)S(1)}, u32[]{:S(2)}, u32[]{:S(2)}) async-start(bf16[8,144,128]{2,1,0:T(8,128)(2,1)} %states.1), calls=%async_computation | async-start | bytes 589824 | tf_op jit(solution)/shard_map/all_to_all | solution.py:360
  15.7 22.0 %all-to-all-start.1 = ((bf16[8,80,128]{2,1,0:T(8,128)(2,1)}), bf16[8,80,128]{2,1,0:T(8,128)(2,1)S(1)}, u32[]{:S(2)}, u32[]{:S(2)}) async-start(bf16[8,80,128]{2,1,0:T(8,128)(2,1)} %segment.1), calls=%async_computation.1 | async-start | bytes 327680 | tf_op jit(solution)/shard_map/all_to_all | solution.py:369
  33.1 16.0 %copy-start = (bf16[2,128,4096]{2,1,0:T(8,128)(2,1)S(1)}, bf16[2,128,4096]{2,1,0:T(8,128)(2,1)}, u32[]{:S(2)}) copy-start(bf16[2,128,4096]{2,1,0:T(8,128)(2,1)} %param.11) | copy-start | bytes 6291460
  38.7 10.4 %all-to-all-start.2 = ((bf16[8,128,128]{2,1,0:T(8,128)(2,1)}), bf16[8,128,128]{2,1,0:T(8,128)(2,1)S(1)}, u32[]{:S(2)}, u32[]{:S(2)}) async-start(bf16[8,128,128]{2,1,0:T(8,128)(2,1)} %entering.1), calls=%async_computation.2 | async-start | bytes 524288 | tf_op jit(solution)/shard_map/all_to_all | solution.py:393
  51.6 6.9 %collective-permute-start = (bf16[64,4096]{1,0:T(8,128)(2,1)S(1)}, bf16[64,4096]{1,0:T(8,128)(2,1)S(1)}, u32[]{:S(2)}, u32[]{:S(2)}) collective-permute-start(bf16[64,4096]{1,0:T(8,128)(2,1)S(1)} %get-tuple-element.30), channel_id=1, source_target_pairs={{0,1},{1,0},{2,3},{3,2},{4,5},{5,4},{6,7},{7,6},{8,9},{9,8},{10,11... | collective-permute-start | bytes 1572872 | tf_op jit(solution)/shard_map/ppermute | solution.py:416

commit v4 on v3

--- a/solution.py
+++ b/solution.py
@@ -22,14 +22,13 @@
 STATE = GROUPS * ROWS
 NEAR = 2 * STATE + 16
 FAR = STATE + 16
-NEAR_ORDER = [4, 5, 6, 7, 0, 1, 2, 3]
+NEAR_ORDER = [7, 0, 1, 2, 3, 4, 5, 6]
 FAR_ORDER = [4, 5, 6, 7, 0, 1, 2, 3]
 BACK_ORDER = [6, 7, 0, 1, 2, 3, 4, 5]
 X_ORDER = [2, 3, 0, 1]
 NEAR_ORDER_OF = [NEAR_ORDER.index(k) for k in range(LO)]
 VMEM = pl.BlockSpec(memory_space=pltpu.VMEM)
 HBM = pl.BlockSpec(memory_space=pltpu.HBM)
-SMEM = pl.BlockSpec(memory_space=pltpu.SMEM)
 
 
 def iota(shape, axis):
@@ -139,8 +138,8 @@
     ]
 
 
-def segment_kernel(me_ref, in_ref, out_ref):
-    me = me_ref[0]
+def segment_kernel(in_ref, out_ref):
+    me = lax.axis_index("hi")
     rows, wide = totals_of(in_ref, 2 * STATE)
     decay = chunk_decays(wide)
     state = jnp.zeros((STATE, LANES), F32)
@@ -160,8 +159,8 @@
         out_ref[k, STATE:FAR, :] = total
 
 
-def entering_kernel(me_ref, far_ref, near_ref, out_ref):
-    me = me_ref[0]
+def entering_kernel(far_ref, near_ref, out_ref):
+    me = lax.axis_index("hi")
     far = chunk_decays(totals_of(far_ref, STATE)[1])
     near = chunk_decays(totals_of(near_ref, 2 * STATE)[1])
     state = jnp.zeros((STATE, LANES), F32)
@@ -193,6 +192,7 @@
     wide_ref,
     narrow_ref,
     scaled_ref,
+    maps_ref,
     rate_ref,
     x_ref,
     g_ref,
@@ -215,6 +215,8 @@
     scaled_ref[0:length, :] = (x_ref[...].astype(F32) * tail).astype(BF16)
     scaled_ref[length : 2 * length, :] = (g_ref[...].astype(F32) * jnp.exp(wide)).astype(BF16)
     b, c = b_ref[...], c_ref[...]
+    maps_ref[0:length, :] = b
+    maps_ref[length : 2 * length, :] = c
     scores = matmul_nt(b, c)
     source, target = iota((length, length), 0), iota((length, length), 1)
     lower = source <= target
@@ -248,66 +250,29 @@
     narrow_ref[length : 2 * length, :] = matmul(jnp.transpose(grad_scores).astype(BF16), b)
 
 
-def carried_kernel(
-    core_ref,
-    state_ref,
-    wide_ref,
-    narrow_ref,
-    scaled_ref,
-    w_ref,
-    b_in,
-    c_in,
-    out_x_ref,
-    out_d_ref,
-    out_b_ref,
-    out_c_ref,
-    keep_ref,
-    send_ref,
-    b_ref,
-    c_ref,
-    sems,
-):
-    copies = start_copies((b_in, c_in), (b_ref, c_ref), sems)
-    length = b_ref.shape[0]
+def whole_state(ref, row):
+    parts = []
+    for k in range(GROUPS):
+        at = slice(row + k * ROWS, row + (k + 1) * ROWS)
+        chunks = [ref[BACK_ORDER.index(block), at, :] for block in range(LO)]
+        parts.append(jnp.concatenate(chunks, axis=0))
+    return jnp.concatenate(parts, axis=1)
+
+
+def tokens_kernel(state_ref, narrow_ref, scaled_ref, w_ref, both_ref, keep_ref, send_ref):
+    length = scaled_ref.shape[0] // 2
     first, second = slice(0, length), slice(length, 2 * length)
-    heads = slice(2 * length, 2 * length + HEADS)
-
-    def whole_state(row):
-        parts = []
-        for k in range(GROUPS):
-            at = slice(row + k * ROWS, row + (k + 1) * ROWS)
-            chunks = [state_ref[BACK_ORDER.index(block), at, :] for block in range(LO)]
-            parts.append(jnp.concatenate(chunks, axis=0))
-        return jnp.concatenate(parts, axis=1)
-
-    state, grad = whole_state(0), whole_state(STATE)
-    sx, sg = scaled_ref[first, :], scaled_ref[second, :]
-    grad_c = (matmul_nt(sg, state) + narrow_ref[second, :]).astype(BF16)
-    grad_b = (matmul_nt(sx, grad) + narrow_ref[first, :]).astype(BF16)
-    out_b_ref[...] = grad_b
-    out_c_ref[...] = grad_c
-    copies[0].wait()
-    copies[1].wait()
-    from_state = matmul(c_ref[...], state)
-    state_back = matmul(b_ref[...], grad)
-    out_x_ref[...] = (wide_ref[first, :] + wide_ref[second, :] * state_back).astype(BF16)
-    pick = (iota((HEADS, WIDE), 0) == iota((HEADS, WIDE), 1) >> 6).astype(F32)
-    through_head = matmul_nt(pick, sg.astype(F32) * from_state, HIGHEST)
-    through_tail = matmul_nt(pick, sx.astype(F32) * state_back, HIGHEST)
-    whole = jnp.sum(grad.astype(F32) * state.astype(F32), axis=0, keepdims=True) * wide_ref[heads, :]
-    whole = jnp.sum(pick * whole, axis=1, keepdims=True)
-    one, two = iota((length, length), 0), iota((length, length), 1)
-    out_d_ref[...] = (
-        narrow_ref[heads, :]
-        + matmul(through_head, (one >= two).astype(F32), HIGHEST)
-        + matmul(through_tail, (one < two).astype(F32), HIGHEST)
-        + whole
-    )
+    grad_c = matmul_nt(scaled_ref[second, :], whole_state(state_ref, 0))
+    grad_b = matmul_nt(scaled_ref[first, :], whole_state(state_ref, STATE))
+    grad_c = (grad_c + narrow_ref[second, :]).astype(BF16)
+    grad_b = (grad_b + narrow_ref[first, :]).astype(BF16)
+    both_ref[first, :] = grad_b
+    both_ref[second, :] = grad_c
     both = jnp.concatenate([grad_b, grad_c], axis=1)
-    sixteen = length // 8
-    even = jnp.concatenate([both[2 * k * sixteen : (2 * k + 1) * sixteen] for k in X_ORDER], axis=0)
-    odd = jnp.concatenate([both[(2 * k + 1) * sixteen : (2 * k + 2) * sixteen] for k in X_ORDER], axis=0)
-    here = core_ref[0] == 0
+    rows = length // 8
+    even = jnp.concatenate([both[2 * k * rows : (2 * k + 1) * rows] for k in X_ORDER], axis=0)
+    odd = jnp.concatenate([both[(2 * k + 1) * rows : (2 * k + 2) * rows] for k in X_ORDER], axis=0)
+    here = lax.axis_index("core") == 0
     keep = jnp.where(here, even, odd)
     send = jnp.where(here, odd, even)
     both = jnp.concatenate([keep, send], axis=0)
@@ -318,6 +283,49 @@
         part = matmul(both, w_ref[:, at]).astype(BF16)
         keep_ref[:, at] = part[:half]
         send_ref[:, at] = part[half:]
+
+
+def sum_heads(pick, values):
+    pick = pick.astype(BF16)
+    high = values.astype(BF16)
+    low = (values - high.astype(F32)).astype(BF16)
+    return matmul_nt(pick, high) + matmul_nt(pick, low)
+
+
+def carried_kernel(
+    state_ref,
+    wide_ref,
+    narrow_ref,
+    scaled_ref,
+    both_ref,
+    maps_ref,
+    out_x_ref,
+    out_d_ref,
+    out_b_ref,
+    out_c_ref,
+):
+    length = out_b_ref.shape[0]
+    first, second = slice(0, length), slice(length, 2 * length)
+    heads = slice(2 * length, 2 * length + HEADS)
+    out_b_ref[...] = both_ref[first, :]
+    out_c_ref[...] = both_ref[second, :]
+    state, grad = whole_state(state_ref, 0), whole_state(state_ref, STATE)
+    sx, sg = scaled_ref[first, :], scaled_ref[second, :]
+    pick = (iota((HEADS, WIDE), 0) == iota((HEADS, WIDE), 1) >> 6).astype(F32)
+    whole = jnp.sum(grad.astype(F32) * state.astype(F32), axis=0, keepdims=True) * wide_ref[heads, :]
+    whole = jnp.sum(pick * whole, axis=1, keepdims=True)
+    from_state = matmul(maps_ref[second, :], state)
+    state_back = matmul(maps_ref[first, :], grad)
+    out_x_ref[...] = (wide_ref[first, :] + wide_ref[second, :] * state_back).astype(BF16)
+    through_head = sum_heads(pick, sg.astype(F32) * from_state)
+    through_tail = sum_heads(pick, sx.astype(F32) * state_back)
+    one, two = iota((length, length), 0), iota((length, length), 1)
+    out_d_ref[...] = (
+        narrow_ref[heads, :]
+        + matmul(through_head, (one >= two).astype(F32), HIGHEST)
+        + matmul(through_tail, (one < two).astype(F32), HIGHEST)
+        + whole
+    )
 
 
 def struct(shape, dtype):
@@ -340,8 +348,6 @@
 def local(inputs, log_decay, b_proj, c_proj, grad_out, w_bc):
     length = inputs.shape[0]
     width = w_bc.shape[2]
-    hi = lax.axis_index("hi").astype(jnp.int32).reshape(1)
-    core = lax.axis_index("core").astype(jnp.int32).reshape(1)
     block = [
         pltpu.with_memory_space_constraint(part, pltpu.HBM)
         for part in (log_decay, inputs, grad_out, b_proj, c_proj)
@@ -361,9 +367,8 @@
     far = call(
         segment_kernel,
         struct((HI, FAR, LANES), BF16),
-        (hi, near),
+        (near,),
         "segment",
-        specs=[SMEM, VMEM],
         moved=2**19,
     )
     far = lax.all_to_all(far, "hi", 0, 0, axis_index_groups=[FAR_ORDER])
@@ -373,6 +378,7 @@
             struct((2 * length + HEADS, WIDE), F32),
             struct((2 * length + HEADS, N), F32),
             struct((2 * length, WIDE), BF16),
+            struct((2 * length, N), BF16),
         ),
         block,
         "block",
@@ -385,35 +391,40 @@
     states = call(
         entering_kernel,
         struct((LO, 2 * STATE, LANES), BF16),
-        (hi, far, near),
+        (far, near),
         "entering",
-        specs=[SMEM, VMEM, VMEM],
         moved=2**19,
     )
     states = lax.all_to_all(states, "lo", 0, 0, axis_index_groups=[BACK_ORDER])
-    operands = (core, states) + tuple(inside) + (w_bc.reshape(2 * N, width), block[3], block[4])
-    grad_inputs, grad_decay, grad_b, grad_c, keep, send = call(
+    wide, narrow, scaled, maps = inside
+    both, keep, send = call(
+        tokens_kernel,
+        (
+            struct((2 * length, N), BF16),
+            struct((length // 2, width), BF16),
+            struct((length // 2, width), BF16),
+        ),
+        (states, narrow, scaled, w_bc.reshape(2 * N, width)),
+        "tokens",
+        flops=2**29,
+        moved=4 * 2**20,
+    )
+    grad_inputs, grad_decay, grad_b, grad_c = call(
         carried_kernel,
         (
             struct((length, WIDE), BF16),
             struct((HEADS, length), F32),
             struct((length, N), BF16),
             struct((length, N), BF16),
-            struct((length // 2, width), BF16),
-            struct((length // 2, width), BF16),
         ),
-        operands,
+        (states, wide, narrow, scaled, both, maps),
         "carried",
-        specs=[SMEM] + [VMEM] * (len(operands) - 3) + [HBM] * 2,
-        scratch=(
-            pltpu.VMEM(b_proj.shape, BF16),
-            pltpu.VMEM(c_proj.shape, BF16),
-            pltpu.SemaphoreType.DMA((2,)),
-        ),
-        flops=2**29,
-        moved=4 * 2**20,
+        flops=2**28,
+        moved=2 * 2**20,
     )
     other = lax.ppermute(send, "core", [(0, 1), (1, 0)])
+    rest = (grad_inputs, grad_decay, grad_b, grad_c)
+    other, (grad_inputs, grad_decay, grad_b, grad_c) = lax.optimization_barrier((other, rest))
     pair = (keep.astype(F32) + other.astype(F32)).astype(BF16)
     blocks = pair.reshape(4, length // 8, width)
     blocks = lax.all_to_all(blocks, "x", 0, 0, axis_index_groups=[X_ORDER])

time: 71.6 us -> 67.4 us (0.941)
  blocking collectives: 11.6 us -> 34.7 us
  starting transfers between devices: 37 us -> 21.3 us
  waiting for transfers between devices: 11.5 us -> 1.45 us
  Pallas kernels: 9.45 us -> 7.31 us
    all_to_all x0 -> x2, blocking collectives: none -> 23.1 us  [the longest x1 11.9 us: local(): states = lax.all_to_all(states, 'lo', 0, 0, axis_index_groups=[BACK_ORDER])]
    all_to_all x2 -> x0, starting transfers between devices: 14.2 us -> none  [the longest x1 7.51 us: local(): states = lax.all_to_all(states, 'lo', 0, 0, axis_index_groups=[BACK_ORDER])]
    all_to_all x2 -> x0, waiting for transfers between devices: 7.98 us -> none  [the longest x1 5.13 us: local(): near = lax.all_to_all(near, 'lo', 0, 0, axis_index_groups=[NEAR_ORDER])]
    pallas_call x5 -> x6, Pallas kernels: 9.45 us -> 7.31 us  [call(): pl.pallas_call(kernel, out_shape=out, in_specs=specs or [VMEM] * len(oper...]
    ppermute x1, starting transfers between devices: 5.43 us -> 4.08 us  [local(): other = lax.ppermute(send, 'core', [(0, 1), (1, 0)])]
    ppermute x1, waiting for transfers between devices: 1.51 us -> 0.26 us  [local(): other = lax.ppermute(send, 'core', [(0, 1), (1, 0)])]
    all_to_all x1, waiting for transfers between devices: 2 us -> 1.19 us  [local(): far = lax.all_to_all(far, 'hi', 0, 0, axis_index_groups=[FAR_ORDER])]
  transfers between devices with their start and end apart: 4 -> 2, of which waited for: 4 -> 2; matrix products, arithmetic and copies ran while one was open for 0% -> 0% of each run, Pallas kernels for 4% -> 6%
where the time goes in v4:
time: 67.4 us; the launch traced here: 67 us
  blocking collectives  34.7 us (51%)
  starting transfers between devices  21.3 us (32%)
  Pallas kernels  7.31 us (11%)
  waiting for transfers between devices  1.45 us (2%)
  other arithmetic  0.87 us (1%)
  between operations  0.69 us (1%)
    all_to_all x1, starting transfers between devices, local(): far = lax.all_to_all(far, 'hi', 0, 0, axis_index_groups=[FAR_ORDER])  17.2 us
    all_to_all x1, blocking collectives, local(): states = lax.all_to_all(states, 'lo', 0, 0, axis_index_groups=[BACK_ORDER])  11.9 us
    all_to_all x1, blocking collectives, local(): blocks = lax.all_to_all(blocks, 'x', 0, 0, axis_index_groups=[X_ORDER])  11.6 us
    all_to_all x1, blocking collectives, local(): near = lax.all_to_all(near, 'lo', 0, 0, axis_index_groups=[NEAR_ORDER])  11.1 us
    pallas_call x6, Pallas kernels, call(): pl.pallas_call(kernel, out_shape=out, in_specs=specs or [VMEM] * len(oper...  7.31 us
    ppermute x1, starting transfers between devices, local(): other = lax.ppermute(send, 'core', [(0, 1), (1, 0)])  4.08 us
  transfers between devices with their start and end apart: 2, of which 2 were waited for; matrix products, arithmetic and copies ran while one was open for 0% of the time, Pallas kernels for 6%

profile of v4, /device:TPU:1, one launch (start us, length us, event | category | flops | bytes accessed | tf_op | source)
XLA Modules:
  0.0 67.0 jit_solution(11138212505969724389)
XLA Ops:
  0.6 1.7 %states.1 = bf16[8,144,128]{2,1,0:T(8,128)(2,1)S(1)} custom-call(f32[8,128]{1,0:T(8,128)} %rate_in.3, bf16[128,512]{1,0:T(8,128)(2,1)} %x_in.3, bf16[128,512]{1,0:T(8,128)(2,1)} %g_in.3, bf16[128,128]{1,0:T(8,128)(2,1)} %b_in.3, bf16[128,128]{1,0:T(8,128)(2,1)} %c_in.3), custom_call_target="tpu_custom_call" | custom-call | flops 33554432 | bytes 1048576 | tf_op jit(solution)/shard_map/states/pallas_call | solution.py:336
  2.3 11.1 %all_to_all.20.in_ref.near_ref = bf16[8,144,128]{2,1,0:T(8,128)(2,1)S(1)} all-to-all(bf16[8,144,128]{2,1,0:T(8,128)(2,1)S(1)} %states.1), channel_id=1, replica_groups={{56,0,8,16,24,32,40,48},{57,1,9,17,25,33,41,49},{58,2,10,18,26,34,42,50..., dimensions={0} | all-to-all | bytes 589824 | tf_op jit(solution)/shard_map/all_to_all | solution.py:366
  13.5 0.9 %segment.1 = bf16[8,80,128]{2,1,0:T(8,128)(2,1)} custom-call(bf16[8,144,128]{2,1,0:T(8,128)(2,1)S(1)} %all_to_all.20.in_ref.near_ref), custom_call_target="tpu_custom_call" | custom-call | bytes 524288 | tf_op jit(solution)/shard_map/segment/pallas_call | solution.py:336
  14.4 17.2 %all-to-all-start.1 = ((bf16[8,80,128]{2,1,0:T(8,128)(2,1)}), bf16[8,80,128]{2,1,0:T(8,128)(2,1)S(1)}, u32[]{:S(2)}, u32[]{:S(2)}) async-start(bf16[8,80,128]{2,1,0:T(8,128)(2,1)} %segment.1), calls=%async_computation.1 | async-start | bytes 327680 | tf_op jit(solution)/shard_map/all_to_all | solution.py:374
  31.6 0.0 copy-start
  31.6 2.6 %block.1 = (f32[264,512]{1,0:T(8,128)S(1)}, f32[264,128]{1,0:T(8,128)S(1)}, bf16[256,512]{1,0:T(8,128)(2,1)S(1)}, bf16[256,128]{1,0:T(8,128)(2,1)S(1)}) custom-call(f32[8,128]{1,0:T(8,128)} %rate_in.3, bf16[128,512]{1,0:T(8,128)(2,1)} %x_in.3, bf16[128,512]{1,0:T(8,128)(2,1)} %g_in.3, bf16[128,128]{1,0:T(8,128)(2,1)} %b_in.3, bf16[128,128]{1,0:T(8,128)(2,1)} %c_in.3), custom_call_target="tpu_custom_call" | custom-call | flops 1073741824 | bytes 4194304 | tf_op jit(solution)/shard_map/block/pallas_call | solution.py:336
  34.2 0.0 copy-start.1
  34.2 0.6 copy-done.1
  34.9 1.2 %all-to-all-done.1.far_ref = bf16[8,80,128]{2,1,0:T(8,128)(2,1)S(1)} async-done(((bf16[8,80,128]{2,1,0:T(8,128)(2,1)}), bf16[8,80,128]{2,1,0:T(8,128)(2,1)S(1)}, u32[]{:S(2)}, u32[]{:S(2)}) %all-to-all-start.1) | async-done | bytes 163872 | tf_op jit(solution)/shard_map/all_to_all | solution.py:374
  36.0 0.0 copy-start.2
  36.0 0.3 entering.1
  36.3 11.9 %all_to_all.21.state_ref = bf16[8,128,128]{2,1,0:T(8,128)(2,1)S(1)} all-to-all(bf16[8,128,128]{2,1,0:T(8,128)(2,1)S(1)} %entering.1), channel_id=1, replica_groups={{48,56,0,8,16,24,32,40},{49,57,1,9,17,25,33,41},{50,58,2,10,18,26,34,42..., dimensions={0} | all-to-all | bytes 524288 | tf_op jit(solution)/shard_map/all_to_all | solution.py:398
  48.2 0.0 copy-done
  48.2 0.6 tokens.1
  48.9 4.1 %collective-permute-start = (bf16[64,4096]{1,0:T(8,128)(2,1)S(1)}, bf16[64,4096]{1,0:T(8,128)(2,1)S(1)}, u32[]{:S(2)}, u32[]{:S(2)}) collective-permute-start(bf16[64,4096]{1,0:T(8,128)(2,1)S(1)} %get-tuple-element.33), channel_id=1, source_target_pairs={{0,1},{1,0},{2,3},{3,2},{4,5},{5,4},{6,7},{7,6},{8,9},{9,8},{10,11... | collective-permute-start | bytes 1572872 | tf_op jit(solution)/shard_map/ppermute | solution.py:425
  53.0 0.0 copy-done.2
  53.0 1.2 %carried.1 = (bf16[128,512]{1,0:T(8,128)(2,1)}, f32[8,128]{1,0:T(8,128)}, bf16[128,128]{1,0:T(8,128)(2,1)}, bf16[128,128]{1,0:T(8,128)(2,1)}) custom-call(bf16[8,128,128]{2,1,0:T(8,128)(2,1)S(1)} %all_to_all.21.state_ref, f32[264,512]{1,0:T(8,128)S(1)} %get-tuple-element.34.wide_ref, f32[264,128]{1,0:T(8,128)S(1)} %get-tuple-element.31.narrow_ref, ...), custom_call_target="tpu_custom_call" | custom-call | flops 268435456 | bytes 2097152 | tf_op jit(solution)/shard_map/carried/pallas_call | solution.py:336
  54.2 0.3 collective-permute-done
  54.5 0.1 add_convert_fusion
  54.6 11.6 %all_to_all.22 = bf16[4,16,4096]{2,1,0:T(8,128)(2,1)S(1)} all-to-all(bf16[4,16,4096]{2,1,0:T(8,128)(2,1)S(1)} %bitcast.3), channel_id=1, replica_groups={{4,6,0,2},{5,7,1,3},{12,14,8,10},{13,15,9,11},{20,22,16,18},{21,23,17,1..., dimensions={0} | all-to-all | bytes 1048576 | tf_op jit(solution)/shard_map/all_to_all | solution.py:430
  66.2 0.7 %reduce_sum.12 = bf16[16,4096]{1,0:T(8,128)(2,1)} reduce(bf16[4,16,4096]{2,1,0:T(8,128)(2,1)S(1)} %all_to_all.22, bf16[]{:T(256)} %constant.2.clone.1), dimensions={0}, to_apply=%region_0.0 | reduce | flops 196608 | bytes 655362 | tf_op jit(solution)/shard_map/reduce_sum | solution.py:431
Async XLA Ops:
  14.4 21.7 %all-to-all-start.1 = ((bf16[8,80,128]{2,1,0:T(8,128)(2,1)}), bf16[8,80,128]{2,1,0:T(8,128)(2,1)S(1)}, u32[]{:S(2)}, u32[]{:S(2)}) async-start(bf16[8,80,128]{2,1,0:T(8,128)(2,1)} %segment.1), calls=%async_computation.1 | async-start | bytes 327680 | tf_op jit(solution)/shard_map/all_to_all | solution.py:374
  31.6 16.6 %copy-start = (bf16[2,128,4096]{2,1,0:T(8,128)(2,1)S(1)}, bf16[2,128,4096]{2,1,0:T(8,128)(2,1)}, u32[]{:S(2)}) copy-start(bf16[2,128,4096]{2,1,0:T(8,128)(2,1)} %param.11) | copy-start | bytes 6291460
  34.2 0.6 copy-start.1
  36.0 16.9 %copy-start.2 = (bf16[256,128]{1,0:T(8,128)(2,1)S(1)}, bf16[256,128]{1,0:T(8,128)(2,1)}, u32[]{:S(2)}) copy-start(bf16[256,128]{1,0:T(8,128)(2,1)} %copy-done.1) | copy-start | bytes 196612
  48.9 5.6 %collective-permute-start = (bf16[64,4096]{1,0:T(8,128)(2,1)S(1)}, bf16[64,4096]{1,0:T(8,128)(2,1)S(1)}, u32[]{:S(2)}, u32[]{:S(2)}) collective-permute-start(bf16[64,4096]{1,0:T(8,128)(2,1)S(1)} %get-tuple-element.33), channel_id=1, source_target_pairs={{0,1},{1,0},{2,3},{3,2},{4,5},{5,4},{6,7},{7,6},{8,9},{9,8},{10,11... | collective-permute-start | bytes 1572872 | tf_op jit(solution)/shard_map/ppermute | solution.py:425

commit v5 on v4

--- a/solution.py
+++ b/solution.py
@@ -51,16 +51,26 @@
     return lax.dot_general(a, b, (((0,), (0,)), ((), ())), preferred_element_type=F32)
 
 
+def three_parts(values):
+    first = values.astype(BF16).astype(F32)
+    rest = values - first
+    second = rest.astype(BF16).astype(F32)
+    return jnp.concatenate([first, second, rest - second], axis=0).astype(BF16)
+
+
 def cumulative(rate):
     length = rate.shape[1]
-    upper = (iota((length, length), 0) <= iota((length, length), 1)).astype(F32)
-    rows = matmul(rate, upper, HIGHEST)
-    return rows, jnp.transpose(rows)
-
-
-def widen(columns):
-    pick = (iota((HEADS, WIDE), 0) == iota((HEADS, WIDE), 1) >> 6).astype(F32)
-    return matmul(columns, pick, HIGHEST)
+    upper = (iota((length, length), 0) <= iota((length, length), 1)).astype(BF16)
+    rows = matmul(three_parts(rate), upper)
+    rows = rows[0:HEADS] + rows[HEADS : 2 * HEADS] + rows[2 * HEADS : 3 * HEADS]
+    return rows, three_parts(rows)
+
+
+def widen(parts):
+    part, column = iota((3 * HEADS, WIDE + LANES), 0), iota((3 * HEADS, WIDE + LANES), 1)
+    of_head = jnp.logical_and((part & 7) == (column >> 6), column < WIDE)
+    pick = jnp.logical_or(of_head, column - WIDE == part)
+    return matmul_tn(parts, pick.astype(BF16))
 
 
 def split_three(row):
@@ -94,13 +104,13 @@
         (rate_in, x_in, g_in, b_in, c_in), (rate_ref, x_ref, g_ref, b_ref, c_ref), sems
     )
     copies[0].wait()
-    _, columns = cumulative(rate_ref[...])
-    wide = widen(columns)
+    _, parts = cumulative(rate_ref[...])
+    wide = widen(parts)
     length = wide.shape[0]
-    last = wide[length - 1 : length]
-    repeat = ((iota((HEADS, LANES), 1) & 7) == iota((HEADS, LANES), 0)).astype(F32)
-    total = matmul(columns[length - 1 : length], repeat, HIGHEST)
-    total = jnp.broadcast_to(split_three(total), (NEAR - 2 * STATE, LANES))
+    last = wide[length - 1 : length, 0:WIDE]
+    total = wide[length - 1 : length, WIDE : WIDE + LANES].astype(BF16)
+    total = jnp.broadcast_to(total, (NEAR - 2 * STATE, LANES))
+    wide = wide[:, 0:WIDE]
     tail = jnp.exp(last - wide)
     head = jnp.exp(wide)
     for copy in copies[1:]:
@@ -205,9 +215,10 @@
     )
     for copy in copies:
         copy.wait()
-    rows, columns = cumulative(rate_ref[...])
+    rows, parts = cumulative(rate_ref[...])
+    columns = jnp.transpose(rows)
     length = columns.shape[0]
-    wide = widen(columns)
+    wide = widen(parts)[:, 0:WIDE]
     last = wide[length - 1 : length]
     tail = jnp.exp(last - wide)
     wide_ref[length : 2 * length, :] = tail

time: 67.4 us -> 67.1 us (level)
  Pallas kernels: 7.31 us -> 6.55 us
    pallas_call x6, Pallas kernels: 7.31 us -> 6.55 us  [call(): pl.pallas_call(kernel, out_shape=out, in_specs=specs or [VMEM] * len(oper...]
  transfers between devices with their start and end apart: 2 -> 2, of which waited for: 2 -> 2; matrix products, arithmetic and copies ran while one was open for 0% -> 0% of each run, Pallas kernels for 6% -> 5%
where the time goes in v5:
time: 67.1 us; the launch traced here: 66.7 us
  blocking collectives  34.7 us (52%)
  starting transfers between devices  21.3 us (32%)
  Pallas kernels  6.55 us (10%)
  waiting for transfers between devices  1.92 us (3%)
  other arithmetic  0.87 us (1%)
  between operations  0.69 us (1%)
    all_to_all x1, starting transfers between devices, local(): far = lax.all_to_all(far, 'hi', 0, 0, axis_index_groups=[FAR_ORDER])  17.3 us
    all_to_all x1, blocking collectives, local(): states = lax.all_to_all(states, 'lo', 0, 0, axis_index_groups=[BACK_ORDER])  11.9 us
    all_to_all x1, blocking collectives, local(): blocks = lax.all_to_all(blocks, 'x', 0, 0, axis_index_groups=[X_ORDER])  11.6 us
    all_to_all x1, blocking collectives, local(): near = lax.all_to_all(near, 'lo', 0, 0, axis_index_groups=[NEAR_ORDER])  11.1 us
    pallas_call x6, Pallas kernels, call(): pl.pallas_call(kernel, out_shape=out, in_specs=specs or [VMEM] * len(oper...  6.55 us
    ppermute x1, starting transfers between devices, local(): other = lax.ppermute(send, 'core', [(0, 1), (1, 0)])  4.08 us
    all_to_all x1, waiting for transfers between devices, local(): far = lax.all_to_all(far, 'hi', 0, 0, axis_index_groups=[FAR_ORDER])  1.66 us
  transfers between devices with their start and end apart: 2, of which 2 were waited for; matrix products, arithmetic and copies ran while one was open for 0% of the time, Pallas kernels for 5%

profile of v5, /device:TPU:1, one launch (start us, length us, event | category | flops | bytes accessed | tf_op | source)
XLA Modules:
  0.0 66.7 jit_solution(9299386153452787548)
XLA Ops:
  0.6 1.4 %states.1 = bf16[8,144,128]{2,1,0:T(8,128)(2,1)S(1)} custom-call(f32[8,128]{1,0:T(8,128)} %rate_in.3, bf16[128,512]{1,0:T(8,128)(2,1)} %x_in.3, bf16[128,512]{1,0:T(8,128)(2,1)} %g_in.3, bf16[128,128]{1,0:T(8,128)(2,1)} %b_in.3, bf16[128,128]{1,0:T(8,128)(2,1)} %c_in.3), custom_call_target="tpu_custom_call" | custom-call | flops 33554432 | bytes 1048576 | tf_op jit(solution)/shard_map/states/pallas_call | solution.py:347
  2.0 11.1 %all_to_all.20.in_ref.near_ref = bf16[8,144,128]{2,1,0:T(8,128)(2,1)S(1)} all-to-all(bf16[8,144,128]{2,1,0:T(8,128)(2,1)S(1)} %states.1), channel_id=1, replica_groups={{56,0,8,16,24,32,40,48},{57,1,9,17,25,33,41,49},{58,2,10,18,26,34,42,50..., dimensions={0} | all-to-all | bytes 589824 | tf_op jit(solution)/shard_map/all_to_all | solution.py:377
  13.2 0.9 %segment.1 = bf16[8,80,128]{2,1,0:T(8,128)(2,1)} custom-call(bf16[8,144,128]{2,1,0:T(8,128)(2,1)S(1)} %all_to_all.20.in_ref.near_ref), custom_call_target="tpu_custom_call" | custom-call | bytes 524288 | tf_op jit(solution)/shard_map/segment/pallas_call | solution.py:347
  14.0 17.3 %all-to-all-start.1 = ((bf16[8,80,128]{2,1,0:T(8,128)(2,1)}), bf16[8,80,128]{2,1,0:T(8,128)(2,1)S(1)}, u32[]{:S(2)}, u32[]{:S(2)}) async-start(bf16[8,80,128]{2,1,0:T(8,128)(2,1)} %segment.1), calls=%async_computation.1 | async-start | bytes 327680 | tf_op jit(solution)/shard_map/all_to_all | solution.py:385
  31.3 0.0 copy-start
  31.3 2.1 %block.1 = (f32[264,512]{1,0:T(8,128)S(1)}, f32[264,128]{1,0:T(8,128)S(1)}, bf16[256,512]{1,0:T(8,128)(2,1)S(1)}, bf16[256,128]{1,0:T(8,128)(2,1)S(1)}) custom-call(f32[8,128]{1,0:T(8,128)} %rate_in.3, bf16[128,512]{1,0:T(8,128)(2,1)} %x_in.3, bf16[128,512]{1,0:T(8,128)(2,1)} %g_in.3, bf16[128,128]{1,0:T(8,128)(2,1)} %b_in.3, bf16[128,128]{1,0:T(8,128)(2,1)} %c_in.3), custom_call_target="tpu_custom_call" | custom-call | flops 1073741824 | bytes 4194304 | tf_op jit(solution)/shard_map/block/pallas_call | solution.py:347
  33.5 0.0 copy-start.1
  33.5 0.6 copy-done.1
  34.1 1.7 %all-to-all-done.1.far_ref = bf16[8,80,128]{2,1,0:T(8,128)(2,1)S(1)} async-done(((bf16[8,80,128]{2,1,0:T(8,128)(2,1)}), bf16[8,80,128]{2,1,0:T(8,128)(2,1)S(1)}, u32[]{:S(2)}, u32[]{:S(2)}) %all-to-all-start.1) | async-done | bytes 163872 | tf_op jit(solution)/shard_map/all_to_all | solution.py:385
  35.7 0.0 copy-start.2
  35.7 0.3 entering.1
  36.0 11.9 %all_to_all.21.state_ref = bf16[8,128,128]{2,1,0:T(8,128)(2,1)S(1)} all-to-all(bf16[8,128,128]{2,1,0:T(8,128)(2,1)S(1)} %entering.1), channel_id=1, replica_groups={{48,56,0,8,16,24,32,40},{49,57,1,9,17,25,33,41},{50,58,2,10,18,26,34,42..., dimensions={0} | all-to-all | bytes 524288 | tf_op jit(solution)/shard_map/all_to_all | solution.py:409
  48.0 0.0 copy-done
  48.0 0.6 tokens.1
  48.6 4.1 %collective-permute-start = (bf16[64,4096]{1,0:T(8,128)(2,1)S(1)}, bf16[64,4096]{1,0:T(8,128)(2,1)S(1)}, u32[]{:S(2)}, u32[]{:S(2)}) collective-permute-start(bf16[64,4096]{1,0:T(8,128)(2,1)S(1)} %get-tuple-element.33), channel_id=1, source_target_pairs={{0,1},{1,0},{2,3},{3,2},{4,5},{5,4},{6,7},{7,6},{8,9},{9,8},{10,11... | collective-permute-start | bytes 1572872 | tf_op jit(solution)/shard_map/ppermute | solution.py:436
  52.7 0.0 copy-done.2
  52.7 1.2 %carried.1 = (bf16[128,512]{1,0:T(8,128)(2,1)}, f32[8,128]{1,0:T(8,128)}, bf16[128,128]{1,0:T(8,128)(2,1)}, bf16[128,128]{1,0:T(8,128)(2,1)}) custom-call(bf16[8,128,128]{2,1,0:T(8,128)(2,1)S(1)} %all_to_all.21.state_ref, f32[264,512]{1,0:T(8,128)S(1)} %get-tuple-element.34.wide_ref, f32[264,128]{1,0:T(8,128)S(1)} %get-tuple-element.31.narrow_ref, ...), custom_call_target="tpu_custom_call" | custom-call | flops 268435456 | bytes 2097152 | tf_op jit(solution)/shard_map/carried/pallas_call | solution.py:347
  53.9 0.3 collective-permute-done
  54.2 0.1 add_convert_fusion
  54.3 11.6 %all_to_all.22 = bf16[4,16,4096]{2,1,0:T(8,128)(2,1)S(1)} all-to-all(bf16[4,16,4096]{2,1,0:T(8,128)(2,1)S(1)} %bitcast.3), channel_id=1, replica_groups={{4,6,0,2},{5,7,1,3},{12,14,8,10},{13,15,9,11},{20,22,16,18},{21,23,17,1..., dimensions={0} | all-to-all | bytes 1048576 | tf_op jit(solution)/shard_map/all_to_all | solution.py:441
  65.9 0.7 %reduce_sum.12 = bf16[16,4096]{1,0:T(8,128)(2,1)} reduce(bf16[4,16,4096]{2,1,0:T(8,128)(2,1)S(1)} %all_to_all.22, bf16[]{:T(256)} %constant.2.clone.1), dimensions={0}, to_apply=%region_0.0 | reduce | flops 196608 | bytes 655362 | tf_op jit(solution)/shard_map/reduce_sum | solution.py:442
Async XLA Ops:
  14.0 21.7 %all-to-all-start.1 = ((bf16[8,80,128]{2,1,0:T(8,128)(2,1)}), bf16[8,80,128]{2,1,0:T(8,128)(2,1)S(1)}, u32[]{:S(2)}, u32[]{:S(2)}) async-start(bf16[8,80,128]{2,1,0:T(8,128)(2,1)} %segment.1), calls=%async_computation.1 | async-start | bytes 327680 | tf_op jit(solution)/shard_map/all_to_all | solution.py:385
  31.3 16.6 %copy-start = (bf16[2,128,4096]{2,1,0:T(8,128)(2,1)S(1)}, bf16[2,128,4096]{2,1,0:T(8,128)(2,1)}, u32[]{:S(2)}) copy-start(bf16[2,128,4096]{2,1,0:T(8,128)(2,1)} %param.11) | copy-start | bytes 6291460
  33.5 0.6 copy-start.1
  35.7 16.9 %copy-start.2 = (bf16[256,128]{1,0:T(8,128)(2,1)S(1)}, bf16[256,128]{1,0:T(8,128)(2,1)}, u32[]{:S(2)}) copy-start(bf16[256,128]{1,0:T(8,128)(2,1)} %copy-done.1) | copy-start | bytes 196612
  48.6 5.6 %collective-permute-start = (bf16[64,4096]{1,0:T(8,128)(2,1)S(1)}, bf16[64,4096]{1,0:T(8,128)(2,1)S(1)}, u32[]{:S(2)}, u32[]{:S(2)}) collective-permute-start(bf16[64,4096]{1,0:T(8,128)(2,1)S(1)} %get-tuple-element.33), channel_id=1, source_target_pairs={{0,1},{1,0},{2,3},{3,2},{4,5},{5,4},{6,7},{7,6},{8,9},{9,8},{10,11... | collective-permute-start | bytes 1572872 | tf_op jit(solution)/shard_map/ppermute | solution.py:436

commit v6 on v5

--- a/solution.py
+++ b/solution.py
@@ -22,7 +22,8 @@
 STATE = GROUPS * ROWS
 NEAR = 2 * STATE + 16
 FAR = STATE + 16
-NEAR_ORDER = [7, 0, 1, 2, 3, 4, 5, 6]
+EARLY = 3
+NEAR_ORDER = [7, 6, 5, 4, 3, 2, 1, 0]
 FAR_ORDER = [4, 5, 6, 7, 0, 1, 2, 3]
 BACK_ORDER = [6, 7, 0, 1, 2, 3, 4, 5]
 X_ORDER = [2, 3, 0, 1]
@@ -148,52 +149,7 @@
     ]
 
 
-def segment_kernel(in_ref, out_ref):
-    me = lax.axis_index("hi")
-    rows, wide = totals_of(in_ref, 2 * STATE)
-    decay = chunk_decays(wide)
-    state = jnp.zeros((STATE, LANES), F32)
-    grad = jnp.zeros((STATE, LANES), F32)
-    for k in NEAR_ORDER_OF:
-        state = decay[k] * state + in_ref[k, 0:STATE, :].astype(F32)
-    for j in reversed(NEAR_ORDER_OF):
-        grad = decay[j] * grad + in_ref[j, STATE : 2 * STATE, :].astype(F32)
-    lane, other = iota((LANES, LANES), 0), iota((LANES, LANES), 1)
-    fold = jnp.logical_and((lane & 7) == (other & 7), lane < 3 * HEADS).astype(F32)
-    total = jnp.sum(matmul(rows, fold, HIGHEST), axis=0, keepdims=True)
-    total = jnp.broadcast_to(split_three(total), (FAR - STATE, LANES))
-    state = state.astype(BF16)
-    grad = grad.astype(BF16)
-    for k, segment in enumerate(FAR_ORDER):
-        out_ref[k, 0:STATE, :] = jnp.where(segment > me, state, grad)
-        out_ref[k, STATE:FAR, :] = total
-
-
-def entering_kernel(far_ref, near_ref, out_ref):
-    me = lax.axis_index("hi")
-    far = chunk_decays(totals_of(far_ref, STATE)[1])
-    near = chunk_decays(totals_of(near_ref, 2 * STATE)[1])
-    state = jnp.zeros((STATE, LANES), F32)
-    grad = jnp.zeros((STATE, LANES), F32)
-    for k in range(HI):
-        at = FAR_ORDER.index(k)
-        new = far[at] * state + far_ref[at, 0:STATE, :].astype(F32)
-        state = jnp.where(k < me, new, state)
-        j = HI - 1 - k
-        at = FAR_ORDER.index(j)
-        new = far[at] * grad + far_ref[at, 0:STATE, :].astype(F32)
-        grad = jnp.where(j > me, new, grad)
-    for k in range(LO):
-        at = NEAR_ORDER.index(k)
-        out_ref[BACK_ORDER.index(k), 0:STATE, :] = state.astype(BF16)
-        state = near[at] * state + near_ref[at, 0:STATE, :].astype(F32)
-        k = LO - 1 - k
-        j = NEAR_ORDER.index(k)
-        out_ref[BACK_ORDER.index(k), STATE : 2 * STATE, :] = grad.astype(BF16)
-        grad = near[j] * grad + near_ref[j, STATE : 2 * STATE, :].astype(F32)
-
-
-def block_kernel(
+def block_body(
     rate_in,
     x_in,
     g_in,
@@ -261,6 +217,59 @@
     narrow_ref[length : 2 * length, :] = matmul(jnp.transpose(grad_scores).astype(BF16), b)
 
 
+def segment_kernel(in_ref, rate_in, x_in, g_in, b_in, c_in, out_ref, *rest):
+    me = lax.axis_index("hi")
+    rows, wide = totals_of(in_ref, 2 * STATE)
+    decay = chunk_decays(wide)
+    state = jnp.zeros((STATE, LANES), F32)
+    grad = jnp.zeros((STATE, LANES), F32)
+    for k in NEAR_ORDER_OF:
+        state = decay[k] * state + in_ref[k, 0:STATE, :].astype(F32)
+    for j in reversed(NEAR_ORDER_OF):
+        grad = decay[j] * grad + in_ref[j, STATE : 2 * STATE, :].astype(F32)
+    lane, other = iota((LANES, LANES), 0), iota((LANES, LANES), 1)
+    fold = jnp.logical_and((lane & 7) == (other & 7), lane < 3 * HEADS).astype(F32)
+    total = jnp.sum(matmul(rows, fold, HIGHEST), axis=0, keepdims=True)
+    total = jnp.broadcast_to(split_three(total), (FAR - STATE, LANES))
+    state = state.astype(BF16)
+    grad = grad.astype(BF16)
+    for k, segment in enumerate(FAR_ORDER):
+        out_ref[k, 0:STATE, :] = jnp.where(segment > me, state, grad)
+        out_ref[k, STATE:FAR, :] = total
+
+    @pl.when(me < EARLY)
+    def _():
+        block_body(rate_in, x_in, g_in, b_in, c_in, *rest)
+
+
+def entering_kernel(far_ref, near_ref, rate_in, x_in, g_in, b_in, c_in, out_ref, *rest):
+    me = lax.axis_index("hi")
+    far = chunk_decays(totals_of(far_ref, STATE)[1])
+    near = chunk_decays(totals_of(near_ref, 2 * STATE)[1])
+    state = jnp.zeros((STATE, LANES), F32)
+    grad = jnp.zeros((STATE, LANES), F32)
+    for k in range(HI):
+        at = FAR_ORDER.index(k)
+        new = far[at] * state + far_ref[at, 0:STATE, :].astype(F32)
+        state = jnp.where(k < me, new, state)
+        j = HI - 1 - k
+        at = FAR_ORDER.index(j)
+        new = far[at] * grad + far_ref[at, 0:STATE, :].astype(F32)
+        grad = jnp.where(j > me, new, grad)
+    for k in range(LO):
+        at = NEAR_ORDER.index(k)
+        out_ref[BACK_ORDER.index(k), 0:STATE, :] = state.astype(BF16)
+        state = near[at] * state + near_ref[at, 0:STATE, :].astype(F32)
+        k = LO - 1 - k
+        j = NEAR_ORDER.index(k)
+        out_ref[BACK_ORDER.index(k), STATE : 2 * STATE, :] = grad.astype(BF16)
+        grad = near[j] * grad + near_ref[j, STATE : 2 * STATE, :].astype(F32)
+
+    @pl.when(me >= EARLY)
+    def _():
+        block_body(rate_in, x_in, g_in, b_in, c_in, *rest)
+
+
 def whole_state(ref, row):
     parts = []
     for k in range(GROUPS):
@@ -270,13 +279,18 @@
     return jnp.concatenate(parts, axis=1)
 
 
-def tokens_kernel(state_ref, narrow_ref, scaled_ref, w_ref, both_ref, keep_ref, send_ref):
-    length = scaled_ref.shape[0] // 2
+def either(pair, at):
+    return jnp.where(lax.axis_index("hi") < EARLY, pair[0][at, :], pair[1][at, :])
+
+
+def tokens_kernel(state_ref, narrow_a, scaled_a, narrow_b, scaled_b, w_ref, both_ref, keep_ref, send_ref):
+    narrow, scaled = (narrow_a, narrow_b), (scaled_a, scaled_b)
+    length = scaled_a.shape[0] // 2
     first, second = slice(0, length), slice(length, 2 * length)
-    grad_c = matmul_nt(scaled_ref[second, :], whole_state(state_ref, 0))
-    grad_b = matmul_nt(scaled_ref[first, :], whole_state(state_ref, STATE))
-    grad_c = (grad_c + narrow_ref[second, :]).astype(BF16)
-    grad_b = (grad_b + narrow_ref[first, :]).astype(BF16)
+    grad_c = matmul_nt(either(scaled, second), whole_state(state_ref, 0))
+    grad_b = matmul_nt(either(scaled, first), whole_state(state_ref, STATE))
+    grad_c = (grad_c + either(narrow, second)).astype(BF16)
+    grad_b = (grad_b + either(narrow, first)).astype(BF16)
     both_ref[first, :] = grad_b
     both_ref[second, :] = grad_c
     both = jnp.concatenate([grad_b, grad_c], axis=1)
@@ -305,34 +319,40 @@
 
 def carried_kernel(
     state_ref,
-    wide_ref,
-    narrow_ref,
-    scaled_ref,
     both_ref,
-    maps_ref,
+    wide_a,
+    narrow_a,
+    scaled_a,
+    maps_a,
+    wide_b,
+    narrow_b,
+    scaled_b,
+    maps_b,
     out_x_ref,
     out_d_ref,
     out_b_ref,
     out_c_ref,
 ):
+    wide, narrow = (wide_a, wide_b), (narrow_a, narrow_b)
+    scaled, maps = (scaled_a, scaled_b), (maps_a, maps_b)
     length = out_b_ref.shape[0]
     first, second = slice(0, length), slice(length, 2 * length)
     heads = slice(2 * length, 2 * length + HEADS)
     out_b_ref[...] = both_ref[first, :]
     out_c_ref[...] = both_ref[second, :]
     state, grad = whole_state(state_ref, 0), whole_state(state_ref, STATE)
-    sx, sg = scaled_ref[first, :], scaled_ref[second, :]
+    sx, sg = either(scaled, first), either(scaled, second)
     pick = (iota((HEADS, WIDE), 0) == iota((HEADS, WIDE), 1) >> 6).astype(F32)
-    whole = jnp.sum(grad.astype(F32) * state.astype(F32), axis=0, keepdims=True) * wide_ref[heads, :]
+    whole = jnp.sum(grad.astype(F32) * state.astype(F32), axis=0, keepdims=True) * either(wide, heads)
     whole = jnp.sum(pick * whole, axis=1, keepdims=True)
-    from_state = matmul(maps_ref[second, :], state)
-    state_back = matmul(maps_ref[first, :], grad)
-    out_x_ref[...] = (wide_ref[first, :] + wide_ref[second, :] * state_back).astype(BF16)
+    from_state = matmul(either(maps, second), state)
+    state_back = matmul(either(maps, first), grad)
+    out_x_ref[...] = (either(wide, first) + either(wide, second) * state_back).astype(BF16)
     through_head = sum_heads(pick, sg.astype(F32) * from_state)
     through_tail = sum_heads(pick, sx.astype(F32) * state_back)
     one, two = iota((length, length), 0), iota((length, length), 1)
     out_d_ref[...] = (
-        narrow_ref[heads, :]
+        either(narrow, heads)
         + matmul(through_head, (one >= two).astype(F32), HIGHEST)
         + matmul(through_tail, (one < two).astype(F32), HIGHEST)
         + whole
@@ -375,39 +395,33 @@
         moved=2**20,
     )
     near = lax.all_to_all(near, "lo", 0, 0, axis_index_groups=[NEAR_ORDER])
-    far = call(
+    inside = (
+        struct((2 * length + HEADS, WIDE), F32),
+        struct((2 * length + HEADS, N), F32),
+        struct((2 * length, WIDE), BF16),
+        struct((2 * length, N), BF16),
+    )
+    scratch = held + [pltpu.SemaphoreType.DMA((5,))]
+    far, *before = call(
         segment_kernel,
-        struct((HI, FAR, LANES), BF16),
-        (near,),
+        (struct((HI, FAR, LANES), BF16),) + inside,
+        [near] + block,
         "segment",
+        specs=[VMEM] + [HBM] * 5,
+        scratch=scratch,
         moved=2**19,
     )
     far = lax.all_to_all(far, "hi", 0, 0, axis_index_groups=[FAR_ORDER])
-    inside = call(
-        block_kernel,
-        (
-            struct((2 * length + HEADS, WIDE), F32),
-            struct((2 * length + HEADS, N), F32),
-            struct((2 * length, WIDE), BF16),
-            struct((2 * length, N), BF16),
-        ),
-        block,
-        "block",
-        specs=[HBM] * 5,
-        scratch=held + [pltpu.SemaphoreType.DMA((5,))],
-        flops=2**30,
-        moved=4 * 2**20,
-    )
-    far, inside = lax.optimization_barrier((far, inside))
-    states = call(
+    states, *after = call(
         entering_kernel,
-        struct((LO, 2 * STATE, LANES), BF16),
-        (far, near),
+        (struct((LO, 2 * STATE, LANES), BF16),) + inside,
+        [far, near] + block,
         "entering",
+        specs=[VMEM] * 2 + [HBM] * 5,
+        scratch=scratch,
         moved=2**19,
     )
     states = lax.all_to_all(states, "lo", 0, 0, axis_index_groups=[BACK_ORDER])
-    wide, narrow, scaled, maps = inside
     both, keep, send = call(
         tokens_kernel,
         (
@@ -415,7 +429,7 @@
             struct((length // 2, width), BF16),
             struct((length // 2, width), BF16),
         ),
-        (states, narrow, scaled, w_bc.reshape(2 * N, width)),
+        (states, before[1], before[2], after[1], after[2], w_bc.reshape(2 * N, width)),
         "tokens",
         flops=2**29,
         moved=4 * 2**20,
@@ -428,7 +442,7 @@
             struct((length, N), BF16),
             struct((length, N), BF16),
         ),
-        (states, wide, narrow, scaled, both, maps),
+        (states, both, *before, *after),
         "carried",
         flops=2**28,
         moved=2 * 2**20,

time: 67.1 us -> 66.3 us (0.988)
  blocking collectives: 34.7 us -> 53.3 us
  starting transfers between devices: 21.3 us -> 4.84 us
  waiting for transfers between devices: 1.92 us -> 0.25 us
    all_to_all x0 -> x1, blocking collectives: none -> 21.7 us  [local(): far = lax.all_to_all(far, 'hi', 0, 0, axis_index_groups=[FAR_ORDER])]
    all_to_all x1 -> x0, starting transfers between devices: 17.3 us -> none  [local(): far = lax.all_to_all(far, 'hi', 0, 0, axis_index_groups=[FAR_ORDER])]
    all_to_all x1, blocking collectives: 11.9 us -> 8.88 us  [local(): states = lax.all_to_all(states, 'lo', 0, 0, axis_index_groups=[BACK_ORDER])]
    all_to_all x1 -> x0, waiting for transfers between devices: 1.66 us -> none  [local(): far = lax.all_to_all(far, 'hi', 0, 0, axis_index_groups=[FAR_ORDER])]
    ppermute x1, starting transfers between devices: 4.08 us -> 4.84 us  [local(): other = lax.ppermute(send, 'core', [(0, 1), (1, 0)])]
    pallas_call x6 -> x5, Pallas kernels: 6.55 us -> 5.95 us  [call(): pl.pallas_call(kernel, out_shape=out, in_specs=specs or [VMEM] * len(oper...]
  transfers between devices with their start and end apart: 2 -> 1, of which waited for: 2 -> 1; matrix products, arithmetic and copies ran while one was open for 0% -> 0% of each run, Pallas kernels for 5% -> 2%
where the time goes in v6:
time: 66.3 us; the launch traced here: 65.9 us
  blocking collectives  53.3 us (80%)
  Pallas kernels  5.95 us (9%)
  starting transfers between devices  4.84 us (7%)
  other arithmetic  0.86 us (1%)
  between operations  0.69 us (1%)
    all_to_all x1, blocking collectives, local(): far = lax.all_to_all(far, 'hi', 0, 0, axis_index_groups=[FAR_ORDER])  21.7 us
    all_to_all x1, blocking collectives, local(): blocks = lax.all_to_all(blocks, 'x', 0, 0, axis_index_groups=[X_ORDER])  11.6 us
    all_to_all x1, blocking collectives, local(): near = lax.all_to_all(near, 'lo', 0, 0, axis_index_groups=[NEAR_ORDER])  11.2 us
    all_to_all x1, blocking collectives, local(): states = lax.all_to_all(states, 'lo', 0, 0, axis_index_groups=[BACK_ORDER])  8.88 us
    pallas_call x5, Pallas kernels, call(): pl.pallas_call(kernel, out_shape=out, in_specs=specs or [VMEM] * len(oper...  5.95 us
    ppermute x1, starting transfers between devices, local(): other = lax.ppermute(send, 'core', [(0, 1), (1, 0)])  4.84 us
  transfers between devices with their start and end apart: 1, of which 1 were waited for; matrix products, arithmetic and copies ran while one was open for 0% of the time, Pallas kernels for 2%

profile of v6, /device:TPU:1, one launch (start us, length us, event | category | flops | bytes accessed | tf_op | source)
XLA Modules:
  0.0 65.9 jit_solution(10374570935787725315)
XLA Ops:
  0.6 0.0 copy-start
  0.6 1.5 %states.1 = bf16[8,144,128]{2,1,0:T(8,128)(2,1)S(1)} custom-call(f32[8,128]{1,0:T(8,128)} %rate_in.5, bf16[128,512]{1,0:T(8,128)(2,1)} %x_in.5, bf16[128,512]{1,0:T(8,128)(2,1)} %g_in.5, bf16[128,128]{1,0:T(8,128)(2,1)} %b_in.5, bf16[128,128]{1,0:T(8,128)(2,1)} %c_in.5), custom_call_target="tpu_custom_call" | custom-call | flops 33554432 | bytes 1048576 | tf_op jit(solution)/shard_map/states/pallas_call | solution.py:367
  2.2 11.2 %all_to_all.20.in_ref.near_ref = bf16[8,144,128]{2,1,0:T(8,128)(2,1)S(1)} all-to-all(bf16[8,144,128]{2,1,0:T(8,128)(2,1)S(1)} %states.1), channel_id=1, replica_groups={{56,48,40,32,24,16,8,0},{57,49,41,33,25,17,9,1},{58,50,42,34,26,18,10,2..., dimensions={0} | all-to-all | bytes 589824 | tf_op jit(solution)/shard_map/all_to_all | solution.py:397
  13.4 2.2 %segment.1 = (bf16[8,80,128]{2,1,0:T(8,128)(2,1)S(1)}, f32[264,512]{1,0:T(8,128)S(1)}, f32[264,128]{1,0:T(8,128)S(1)}, bf16[256,512]{1,0:T(8,128)(2,1)S(1)}, bf16[256,128]{1,0:T(8,128)(2,1)S(1)}) custom-call(bf16[8,144,128]{2,1,0:T(8,128)(2,1)S(1)} %all_to_all.20.in_ref.near_ref, f32[8,128]{1,0:T(8,128)} %rate_in.5, bf16[128,512]{1,0:T(8,128)(2,1)} %x_in.5, ...), custom_call_target="tpu_custom_call" | custom-call | bytes 524288 | tf_op jit(solution)/shard_map/segment/pallas_call | solution.py:367
  15.6 21.7 %all_to_all.21.far_ref = bf16[8,80,128]{2,1,0:T(8,128)(2,1)S(1)} all-to-all(bf16[8,80,128]{2,1,0:T(8,128)(2,1)S(1)} %get-tuple-element.27), channel_id=1, replica_groups={{256,320,384,448,0,64,128,192},{257,321,385,449,1,65,129,193},{258,322,..., dimensions={0} | all-to-all | bytes 327680 | tf_op jit(solution)/shard_map/all_to_all | solution.py:414
  37.3 0.3 entering.1
  37.6 8.9 %all_to_all.22.state_ref = bf16[8,128,128]{2,1,0:T(8,128)(2,1)S(1)} all-to-all(bf16[8,128,128]{2,1,0:T(8,128)(2,1)S(1)} %get-tuple-element.28), channel_id=1, replica_groups={{48,56,0,8,16,24,32,40},{49,57,1,9,17,25,33,41},{50,58,2,10,18,26,34,42..., dimensions={0} | all-to-all | bytes 524288 | tf_op jit(solution)/shard_map/all_to_all | solution.py:424
  46.4 0.0 copy-done
  46.5 0.6 tokens.1
  47.1 4.8 %collective-permute-start = (bf16[64,4096]{1,0:T(8,128)(2,1)S(1)}, bf16[64,4096]{1,0:T(8,128)(2,1)S(1)}, u32[]{:S(2)}, u32[]{:S(2)}) collective-permute-start(bf16[64,4096]{1,0:T(8,128)(2,1)S(1)} %get-tuple-element.33), channel_id=1, source_target_pairs={{0,1},{1,0},{2,3},{3,2},{4,5},{5,4},{6,7},{7,6},{8,9},{9,8},{10,11... | collective-permute-start | bytes 1572872 | tf_op jit(solution)/shard_map/ppermute | solution.py:450
  51.9 1.3 %carried.1 = (bf16[128,512]{1,0:T(8,128)(2,1)}, f32[8,128]{1,0:T(8,128)}, bf16[128,128]{1,0:T(8,128)(2,1)}, bf16[128,128]{1,0:T(8,128)(2,1)}) custom-call(bf16[8,128,128]{2,1,0:T(8,128)(2,1)S(1)} %all_to_all.22.state_ref, bf16[256,128]{1,0:T(8,128)(2,1)S(1)} %get-tuple-element.34.both_ref, f32[264,512]{1,0:T(8,128)S(1)} %get-tuple-element.35.wide_a, ...), custom_call_target="tpu_custom_call" | custom-call | flops 268435456 | bytes 2097152 | tf_op jit(solution)/shard_map/carried/pallas_call | solution.py:367
  53.2 0.3 collective-permute-done
  53.5 0.1 add_convert_fusion
  53.6 11.6 %all_to_all.23 = bf16[4,16,4096]{2,1,0:T(8,128)(2,1)S(1)} all-to-all(bf16[4,16,4096]{2,1,0:T(8,128)(2,1)S(1)} %bitcast.3), channel_id=1, replica_groups={{4,6,0,2},{5,7,1,3},{12,14,8,10},{13,15,9,11},{20,22,16,18},{21,23,17,1..., dimensions={0} | all-to-all | bytes 1048576 | tf_op jit(solution)/shard_map/all_to_all | solution.py:455
  65.2 0.7 %reduce_sum.12 = bf16[16,4096]{1,0:T(8,128)(2,1)} reduce(bf16[4,16,4096]{2,1,0:T(8,128)(2,1)S(1)} %all_to_all.23, bf16[]{:T(256)} %constant.2.clone.1), dimensions={0}, to_apply=%region_0.0 | reduce | flops 196608 | bytes 655362 | tf_op jit(solution)/shard_map/reduce_sum | solution.py:456
Async XLA Ops:
  0.6 45.8 %copy-start = (bf16[2,128,4096]{2,1,0:T(8,128)(2,1)S(1)}, bf16[2,128,4096]{2,1,0:T(8,128)(2,1)}, u32[]{:S(2)}) copy-start(bf16[2,128,4096]{2,1,0:T(8,128)(2,1)} %param.11) | copy-start | bytes 6291460
  47.1 6.4 %collective-permute-start = (bf16[64,4096]{1,0:T(8,128)(2,1)S(1)}, bf16[64,4096]{1,0:T(8,128)(2,1)S(1)}, u32[]{:S(2)}, u32[]{:S(2)}) collective-permute-start(bf16[64,4096]{1,0:T(8,128)(2,1)S(1)} %get-tuple-element.33), channel_id=1, source_target_pairs={{0,1},{1,0},{2,3},{3,2},{4,5},{5,4},{6,7},{7,6},{8,9},{9,8},{10,11... | collective-permute-start | bytes 1572872 | tf_op jit(solution)/shard_map/ppermute | solution.py:450

commit v7 on v6

--- a/solution.py
+++ b/solution.py
@@ -21,7 +21,7 @@
 GROUPS = WIDE // LANES
 STATE = GROUPS * ROWS
 NEAR = 2 * STATE + 16
-FAR = STATE + 16
+FAR = STATE + 8
 EARLY = 3
 NEAR_ORDER = [7, 6, 5, 4, 3, 2, 1, 0]
 FAR_ORDER = [4, 5, 6, 7, 0, 1, 2, 3]
@@ -130,7 +130,7 @@
 
 
 def totals_of(ref, row):
-    rows = [ref[k, row : row + 16, :].astype(F32)[0:1] for k in range(ref.shape[0])]
+    rows = [ref[k, row : ref.shape[1], :].astype(F32)[0:1] for k in range(ref.shape[0])]
     rows = jnp.concatenate(rows, axis=0)
     return rows, join_three(rows.astype(BF16))
 

time: 66.3 us -> 65.4 us (0.986)
  blocking collectives: 53.3 us -> 52.6 us
    all_to_all x1, blocking collectives: 8.88 us -> 8.15 us  [local(): states = lax.all_to_all(states, 'lo', 0, 0, axis_index_groups=[BACK_ORDER])]
where the time goes in v7:
time: 65.4 us; the launch traced here: 65.1 us
  blocking collectives  52.6 us (80%)
  Pallas kernels  5.95 us (9%)
  starting transfers between devices  4.79 us (7%)
  other arithmetic  0.86 us (1%)
  between operations  0.69 us (1%)
    all_to_all x1, blocking collectives, local(): far = lax.all_to_all(far, 'hi', 0, 0, axis_index_groups=[FAR_ORDER])  21.6 us
    all_to_all x1, blocking collectives, local(): blocks = lax.all_to_all(blocks, 'x', 0, 0, axis_index_groups=[X_ORDER])  11.6 us
    all_to_all x1, blocking collectives, local(): near = lax.all_to_all(near, 'lo', 0, 0, axis_index_groups=[NEAR_ORDER])  11.2 us
    all_to_all x1, blocking collectives, local(): states = lax.all_to_all(states, 'lo', 0, 0, axis_index_groups=[BACK_ORDER])  8.15 us
    pallas_call x5, Pallas kernels, call(): pl.pallas_call(kernel, out_shape=out, in_specs=specs or [VMEM] * len(oper...  5.95 us
    ppermute x1, starting transfers between devices, local(): other = lax.ppermute(send, 'core', [(0, 1), (1, 0)])  4.79 us
  transfers between devices with their start and end apart: 1, of which 1 were waited for; matrix products, arithmetic and copies ran while one was open for 0% of the time, Pallas kernels for 2%

profile of v7, /device:TPU:1, one launch (start us, length us, event | category | flops | bytes accessed | tf_op | source)
XLA Modules:
  0.0 65.1 jit_solution(15594057217431093821)
XLA Ops:
  0.6 0.0 copy-start
  0.6 1.5 %states.1 = bf16[8,144,128]{2,1,0:T(8,128)(2,1)S(1)} custom-call(f32[8,128]{1,0:T(8,128)} %rate_in.5, bf16[128,512]{1,0:T(8,128)(2,1)} %x_in.5, bf16[128,512]{1,0:T(8,128)(2,1)} %g_in.5, bf16[128,128]{1,0:T(8,128)(2,1)} %b_in.5, bf16[128,128]{1,0:T(8,128)(2,1)} %c_in.5), custom_call_target="tpu_custom_call" | custom-call | flops 33554432 | bytes 1048576 | tf_op jit(solution)/shard_map/states/pallas_call | solution.py:367
  2.2 11.2 %all_to_all.20.in_ref.near_ref = bf16[8,144,128]{2,1,0:T(8,128)(2,1)S(1)} all-to-all(bf16[8,144,128]{2,1,0:T(8,128)(2,1)S(1)} %states.1), channel_id=1, replica_groups={{56,48,40,32,24,16,8,0},{57,49,41,33,25,17,9,1},{58,50,42,34,26,18,10,2..., dimensions={0} | all-to-all | bytes 589824 | tf_op jit(solution)/shard_map/all_to_all | solution.py:397
  13.4 2.2 %segment.1 = (bf16[8,72,128]{2,1,0:T(8,128)(2,1)S(1)}, f32[264,512]{1,0:T(8,128)S(1)}, f32[264,128]{1,0:T(8,128)S(1)}, bf16[256,512]{1,0:T(8,128)(2,1)S(1)}, bf16[256,128]{1,0:T(8,128)(2,1)S(1)}) custom-call(bf16[8,144,128]{2,1,0:T(8,128)(2,1)S(1)} %all_to_all.20.in_ref.near_ref, f32[8,128]{1,0:T(8,128)} %rate_in.5, bf16[128,512]{1,0:T(8,128)(2,1)} %x_in.5, ...), custom_call_target="tpu_custom_call" | custom-call | bytes 524288 | tf_op jit(solution)/shard_map/segment/pallas_call | solution.py:367
  15.6 21.6 %all_to_all.21.far_ref = bf16[8,72,128]{2,1,0:T(8,128)(2,1)S(1)} all-to-all(bf16[8,72,128]{2,1,0:T(8,128)(2,1)S(1)} %get-tuple-element.27), channel_id=1, replica_groups={{256,320,384,448,0,64,128,192},{257,321,385,449,1,65,129,193},{258,322,..., dimensions={0} | all-to-all | bytes 294912 | tf_op jit(solution)/shard_map/all_to_all | solution.py:414
  37.2 0.3 entering.1
  37.5 8.2 %all_to_all.22.state_ref = bf16[8,128,128]{2,1,0:T(8,128)(2,1)S(1)} all-to-all(bf16[8,128,128]{2,1,0:T(8,128)(2,1)S(1)} %get-tuple-element.28), channel_id=1, replica_groups={{48,56,0,8,16,24,32,40},{49,57,1,9,17,25,33,41},{50,58,2,10,18,26,34,42..., dimensions={0} | all-to-all | bytes 524288 | tf_op jit(solution)/shard_map/all_to_all | solution.py:424
  45.7 0.0 copy-done
  45.7 0.6 tokens.1
  46.3 4.8 %collective-permute-start = (bf16[64,4096]{1,0:T(8,128)(2,1)S(1)}, bf16[64,4096]{1,0:T(8,128)(2,1)S(1)}, u32[]{:S(2)}, u32[]{:S(2)}) collective-permute-start(bf16[64,4096]{1,0:T(8,128)(2,1)S(1)} %get-tuple-element.33), channel_id=1, source_target_pairs={{0,1},{1,0},{2,3},{3,2},{4,5},{5,4},{6,7},{7,6},{8,9},{9,8},{10,11... | collective-permute-start | bytes 1572872 | tf_op jit(solution)/shard_map/ppermute | solution.py:450
  51.1 1.3 %carried.1 = (bf16[128,512]{1,0:T(8,128)(2,1)}, f32[8,128]{1,0:T(8,128)}, bf16[128,128]{1,0:T(8,128)(2,1)}, bf16[128,128]{1,0:T(8,128)(2,1)}) custom-call(bf16[8,128,128]{2,1,0:T(8,128)(2,1)S(1)} %all_to_all.22.state_ref, bf16[256,128]{1,0:T(8,128)(2,1)S(1)} %get-tuple-element.34.both_ref, f32[264,512]{1,0:T(8,128)S(1)} %get-tuple-element.35.wide_a, ...), custom_call_target="tpu_custom_call" | custom-call | flops 268435456 | bytes 2097152 | tf_op jit(solution)/shard_map/carried/pallas_call | solution.py:367
  52.4 0.2 collective-permute-done
  52.6 0.1 add_convert_fusion
  52.7 11.6 %all_to_all.23 = bf16[4,16,4096]{2,1,0:T(8,128)(2,1)S(1)} all-to-all(bf16[4,16,4096]{2,1,0:T(8,128)(2,1)S(1)} %bitcast.3), channel_id=1, replica_groups={{4,6,0,2},{5,7,1,3},{12,14,8,10},{13,15,9,11},{20,22,16,18},{21,23,17,1..., dimensions={0} | all-to-all | bytes 1048576 | tf_op jit(solution)/shard_map/all_to_all | solution.py:455
  64.4 0.7 %reduce_sum.12 = bf16[16,4096]{1,0:T(8,128)(2,1)} reduce(bf16[4,16,4096]{2,1,0:T(8,128)(2,1)S(1)} %all_to_all.23, bf16[]{:T(256)} %constant.2.clone.1), dimensions={0}, to_apply=%region_0.0 | reduce | flops 196608 | bytes 655362 | tf_op jit(solution)/shard_map/reduce_sum | solution.py:456
Async XLA Ops:
  0.6 45.0 %copy-start = (bf16[2,128,4096]{2,1,0:T(8,128)(2,1)S(1)}, bf16[2,128,4096]{2,1,0:T(8,128)(2,1)}, u32[]{:S(2)}) copy-start(bf16[2,128,4096]{2,1,0:T(8,128)(2,1)} %param.11) | copy-start | bytes 6291460
  46.3 6.3 %collective-permute-start = (bf16[64,4096]{1,0:T(8,128)(2,1)S(1)}, bf16[64,4096]{1,0:T(8,128)(2,1)S(1)}, u32[]{:S(2)}, u32[]{:S(2)}) collective-permute-start(bf16[64,4096]{1,0:T(8,128)(2,1)S(1)} %get-tuple-element.33), channel_id=1, source_target_pairs={{0,1},{1,0},{2,3},{3,2},{4,5},{5,4},{6,7},{7,6},{8,9},{9,8},{10,11... | collective-permute-start | bytes 1572872 | tf_op jit(solution)/shard_map/ppermute | solution.py:450

commit v8 on v7

--- a/solution.py
+++ b/solution.py
@@ -20,7 +20,7 @@
 HIGHEST = lax.Precision.HIGHEST
 GROUPS = WIDE // LANES
 STATE = GROUPS * ROWS
-NEAR = 2 * STATE + 16
+NEAR = 2 * STATE + 8
 FAR = STATE + 8
 EARLY = 3
 NEAR_ORDER = [7, 6, 5, 4, 3, 2, 1, 0]
@@ -155,10 +155,12 @@
     g_in,
     b_in,
     c_in,
+    w_in,
     wide_ref,
     narrow_ref,
     scaled_ref,
     maps_ref,
+    w_ref,
     rate_ref,
     x_ref,
     g_ref,
@@ -169,6 +171,8 @@
     copies = start_copies(
         (rate_in, x_in, g_in, b_in, c_in), (rate_ref, x_ref, g_ref, b_ref, c_ref), sems
     )
+    fetch = pltpu.make_async_copy(w_in, w_ref, sems.at[len(copies)])
+    fetch.start()
     for copy in copies:
         copy.wait()
     rows, parts = cumulative(rate_ref[...])
@@ -215,9 +219,10 @@
     narrow_ref[2 * length : 2 * length + HEADS, :] = jnp.concatenate(decay_rows, axis=0)
     narrow_ref[0:length, :] = matmul(grad_scores.astype(BF16), c)
     narrow_ref[length : 2 * length, :] = matmul(jnp.transpose(grad_scores).astype(BF16), b)
-
-
-def segment_kernel(in_ref, rate_in, x_in, g_in, b_in, c_in, out_ref, *rest):
+    fetch.wait()
+
+
+def segment_kernel(in_ref, rate_in, x_in, g_in, b_in, c_in, w_in, out_ref, *rest):
     me = lax.axis_index("hi")
     rows, wide = totals_of(in_ref, 2 * STATE)
     decay = chunk_decays(wide)
@@ -228,8 +233,8 @@
     for j in reversed(NEAR_ORDER_OF):
         grad = decay[j] * grad + in_ref[j, STATE : 2 * STATE, :].astype(F32)
     lane, other = iota((LANES, LANES), 0), iota((LANES, LANES), 1)
-    fold = jnp.logical_and((lane & 7) == (other & 7), lane < 3 * HEADS).astype(F32)
-    total = jnp.sum(matmul(rows, fold, HIGHEST), axis=0, keepdims=True)
+    fold = jnp.logical_and((lane & 7) == (other & 7), lane < 3 * HEADS).astype(BF16)
+    total = jnp.sum(matmul(rows.astype(BF16), fold), axis=0, keepdims=True)
     total = jnp.broadcast_to(split_three(total), (FAR - STATE, LANES))
     state = state.astype(BF16)
     grad = grad.astype(BF16)
@@ -239,10 +244,10 @@
 
     @pl.when(me < EARLY)
     def _():
-        block_body(rate_in, x_in, g_in, b_in, c_in, *rest)
-
-
-def entering_kernel(far_ref, near_ref, rate_in, x_in, g_in, b_in, c_in, out_ref, *rest):
+        block_body(rate_in, x_in, g_in, b_in, c_in, w_in, *rest)
+
+
+def entering_kernel(far_ref, near_ref, rate_in, x_in, g_in, b_in, c_in, w_in, out_ref, *rest):
     me = lax.axis_index("hi")
     far = chunk_decays(totals_of(far_ref, STATE)[1])
     near = chunk_decays(totals_of(near_ref, 2 * STATE)[1])
@@ -267,7 +272,7 @@
 
     @pl.when(me >= EARLY)
     def _():
-        block_body(rate_in, x_in, g_in, b_in, c_in, *rest)
+        block_body(rate_in, x_in, g_in, b_in, c_in, w_in, *rest)
 
 
 def whole_state(ref, row):
@@ -283,7 +288,9 @@
     return jnp.where(lax.axis_index("hi") < EARLY, pair[0][at, :], pair[1][at, :])
 
 
-def tokens_kernel(state_ref, narrow_a, scaled_a, narrow_b, scaled_b, w_ref, both_ref, keep_ref, send_ref):
+def tokens_kernel(
+    state_ref, narrow_a, scaled_a, w_a, narrow_b, scaled_b, w_b, both_ref, keep_ref, send_ref
+):
     narrow, scaled = (narrow_a, narrow_b), (scaled_a, scaled_b)
     length = scaled_a.shape[0] // 2
     first, second = slice(0, length), slice(length, 2 * length)
@@ -303,11 +310,17 @@
     both = jnp.concatenate([keep, send], axis=0)
     half = length // 2
     step = 512
-    for k in range(w_ref.shape[1] // step):
-        at = slice(k * step, (k + 1) * step)
-        part = matmul(both, w_ref[:, at]).astype(BF16)
-        keep_ref[:, at] = part[:half]
-        send_ref[:, at] = part[half:]
+
+    def times(w_ref):
+        for k in range(w_ref.shape[1] // step):
+            at = slice(k * step, (k + 1) * step)
+            part = matmul(both, w_ref[:, at]).astype(BF16)
+            keep_ref[:, at] = part[:half]
+            send_ref[:, at] = part[half:]
+
+    early = lax.axis_index("hi") < EARLY
+    pl.when(early)(lambda: times(w_a))
+    pl.when(jnp.logical_not(early))(lambda: times(w_b))
 
 
 def sum_heads(pick, values):
@@ -400,14 +413,16 @@
         struct((2 * length + HEADS, N), F32),
         struct((2 * length, WIDE), BF16),
         struct((2 * length, N), BF16),
-    )
-    scratch = held + [pltpu.SemaphoreType.DMA((5,))]
+        struct((2 * N, width), BF16),
+    )
+    scratch = held + [pltpu.SemaphoreType.DMA((6,))]
+    block.append(pltpu.with_memory_space_constraint(w_bc.reshape(2 * N, width), pltpu.HBM))
     far, *before = call(
         segment_kernel,
         (struct((HI, FAR, LANES), BF16),) + inside,
         [near] + block,
         "segment",
-        specs=[VMEM] + [HBM] * 5,
+        specs=[VMEM] + [HBM] * 6,
         scratch=scratch,
         moved=2**19,
     )
@@ -417,7 +432,7 @@
         (struct((LO, 2 * STATE, LANES), BF16),) + inside,
         [far, near] + block,
         "entering",
-        specs=[VMEM] * 2 + [HBM] * 5,
+        specs=[VMEM] * 2 + [HBM] * 6,
         scratch=scratch,
         moved=2**19,
     )
@@ -429,7 +444,7 @@
             struct((length // 2, width), BF16),
             struct((length // 2, width), BF16),
         ),
-        (states, before[1], before[2], after[1], after[2], w_bc.reshape(2 * N, width)),
+        (states, before[1], before[2], before[4], after[1], after[2], after[4]),
         "tokens",
         flops=2**29,
         moved=4 * 2**20,
@@ -442,7 +457,7 @@
             struct((length, N), BF16),
             struct((length, N), BF16),
         ),
-        (states, both, *before, *after),
+        (states, both, *before[:4], *after[:4]),
         "carried",
         flops=2**28,
         moved=2 * 2**20,

time: 65.4 us -> 65.2 us (level)
  blocking collectives: 52.6 us -> 51.7 us
  starting transfers between devices: 4.79 us -> 5.5 us
    all_to_all x1, blocking collectives: 21.6 us -> 19.3 us  [local(): far = lax.all_to_all(far, 'hi', 0, 0, axis_index_groups=[FAR_ORDER])]
    all_to_all x1, blocking collectives: 8.15 us -> 9.67 us  [local(): states = lax.all_to_all(states, 'lo', 0, 0, axis_index_groups=[BACK_ORDER])]
    ppermute x1, starting transfers between devices: 4.79 us -> 5.5 us  [local(): other = lax.ppermute(send, 'core', [(0, 1), (1, 0)])]
where the time goes in v8:
time: 65.2 us; the launch traced here: 64.9 us
  blocking collectives  51.7 us (79%)
  Pallas kernels  5.88 us (9%)
  starting transfers between devices  5.5 us (8%)
  other arithmetic  0.87 us (1%)
  between operations  0.68 us (1%)
    all_to_all x1, blocking collectives, local(): far = lax.all_to_all(far, 'hi', 0, 0, axis_index_groups=[FAR_ORDER])  19.3 us
    all_to_all x1, blocking collectives, local(): blocks = lax.all_to_all(blocks, 'x', 0, 0, axis_index_groups=[X_ORDER])  11.6 us
    all_to_all x1, blocking collectives, local(): near = lax.all_to_all(near, 'lo', 0, 0, axis_index_groups=[NEAR_ORDER])  11.1 us
    all_to_all x1, blocking collectives, local(): states = lax.all_to_all(states, 'lo', 0, 0, axis_index_groups=[BACK_ORDER])  9.67 us
    pallas_call x5, Pallas kernels, call(): pl.pallas_call(kernel, out_shape=out, in_specs=specs or [VMEM] * len(oper...  5.88 us
    ppermute x1, starting transfers between devices, local(): other = lax.ppermute(send, 'core', [(0, 1), (1, 0)])  5.5 us
  transfers between devices with their start and end apart: 1, of which 1 were waited for; matrix products, arithmetic and copies ran while one was open for 0% of the time, Pallas kernels for 2%

profile of v8, /device:TPU:1, one launch (start us, length us, event | category | flops | bytes accessed | tf_op | source)
XLA Modules:
  0.0 64.9 jit_solution(16732281819615813165)
XLA Ops:
  0.6 1.4 %states.1 = bf16[8,136,128]{2,1,0:T(8,128)(2,1)S(1)} custom-call(f32[8,128]{1,0:T(8,128)} %rate_in.5, bf16[128,512]{1,0:T(8,128)(2,1)} %x_in.5, bf16[128,512]{1,0:T(8,128)(2,1)} %g_in.5, bf16[128,128]{1,0:T(8,128)(2,1)} %b_in.5, bf16[128,128]{1,0:T(8,128)(2,1)} %c_in.5), custom_call_target="tpu_custom_call" | custom-call | flops 33554432 | bytes 1048576 | tf_op jit(solution)/shard_map/states/pallas_call | solution.py:380
  2.0 11.1 %all_to_all.20.in_ref.near_ref = bf16[8,136,128]{2,1,0:T(8,128)(2,1)S(1)} all-to-all(bf16[8,136,128]{2,1,0:T(8,128)(2,1)S(1)} %states.1), channel_id=1, replica_groups={{56,48,40,32,24,16,8,0},{57,49,41,33,25,17,9,1},{58,50,42,34,26,18,10,2..., dimensions={0} | all-to-all | bytes 557056 | tf_op jit(solution)/shard_map/all_to_all | solution.py:410
  13.2 2.2 %segment.1 = (bf16[8,72,128]{2,1,0:T(8,128)(2,1)S(1)}, f32[264,512]{1,0:T(8,128)S(1)}, f32[264,128]{1,0:T(8,128)S(1)}, bf16[256,512]{1,0:T(8,128)(2,1)S(1)}, bf1...) custom-call(bf16[8,136,128]{2,1,0:T(8,128)(2,1)S(1)} %all_to_all.20.in_ref.near_ref, f32[8,128]{1,0:T(8,128)} %rate_in.5, ...), custom_call_target="tpu_custom_call" | custom-call | bytes 524288 | tf_op jit(solution)/shard_map/segment/pallas_call | solution.py:380
  15.4 19.3 %all_to_all.21.far_ref = bf16[8,72,128]{2,1,0:T(8,128)(2,1)S(1)} all-to-all(bf16[8,72,128]{2,1,0:T(8,128)(2,1)S(1)} %get-tuple-element.29), channel_id=1, replica_groups={{256,320,384,448,0,64,128,192},{257,321,385,449,1,65,129,193},{258,322,..., dimensions={0} | all-to-all | bytes 294912 | tf_op jit(solution)/shard_map/all_to_all | solution.py:429
  34.7 0.3 entering.1
  35.0 9.7 %all_to_all.22.state_ref = bf16[8,128,128]{2,1,0:T(8,128)(2,1)S(1)} all-to-all(bf16[8,128,128]{2,1,0:T(8,128)(2,1)S(1)} %get-tuple-element.30), channel_id=1, replica_groups={{48,56,0,8,16,24,32,40},{49,57,1,9,17,25,33,41},{50,58,2,10,18,26,34,42..., dimensions={0} | all-to-all | bytes 524288 | tf_op jit(solution)/shard_map/all_to_all | solution.py:439
  44.7 0.7 %tokens.1 = (bf16[256,128]{1,0:T(8,128)(2,1)S(1)}, bf16[64,4096]{1,0:T(8,128)(2,1)S(1)}, bf16[64,4096]{1,0:T(8,128)(2,1)S(1)}) custom-call(bf16[8,128,128]{2,1,0:T(8,128)(2,1)S(1)} %all_to_all.22.state_ref, f32[264,128]{1,0:T(8,128)S(1)} %get-tuple-element.31.narrow_a, bf16[256,512]{1,0:T(8,128)(2,1)S(1)} %get-tuple-element.32.scaled_a, ...), custom_call_target="tpu_custom_call" | custom-call | flops 536870912 | bytes 4194304 | tf_op jit(solution)/shard_map/tokens/pallas_call | solution.py:380
  45.3 5.5 %collective-permute-start = (bf16[64,4096]{1,0:T(8,128)(2,1)S(1)}, bf16[64,4096]{1,0:T(8,128)(2,1)S(1)}, u32[]{:S(2)}, u32[]{:S(2)}) collective-permute-start(bf16[64,4096]{1,0:T(8,128)(2,1)S(1)} %get-tuple-element.37), channel_id=1, source_target_pairs={{0,1},{1,0},{2,3},{3,2},{4,5},{5,4},{6,7},{7,6},{8,9},{9,8},{10,11... | collective-permute-start | bytes 1572872 | tf_op jit(solution)/shard_map/ppermute | solution.py:465
  50.8 1.3 %carried.1 = (bf16[128,512]{1,0:T(8,128)(2,1)}, f32[8,128]{1,0:T(8,128)}, bf16[128,128]{1,0:T(8,128)(2,1)}, bf16[128,128]{1,0:T(8,128)(2,1)}) custom-call(bf16[8,128,128]{2,1,0:T(8,128)(2,1)S(1)} %all_to_all.22.state_ref, bf16[256,128]{1,0:T(8,128)(2,1)S(1)} %get-tuple-element.38.both_ref, f32[264,512]{1,0:T(8,128)S(1)} %get-tuple-element.39.wide_a, ...), custom_call_target="tpu_custom_call" | custom-call | flops 268435456 | bytes 2097152 | tf_op jit(solution)/shard_map/carried/pallas_call | solution.py:380
  52.1 0.2 collective-permute-done
  52.4 0.1 add_convert_fusion
  52.5 11.6 %all_to_all.23 = bf16[4,16,4096]{2,1,0:T(8,128)(2,1)S(1)} all-to-all(bf16[4,16,4096]{2,1,0:T(8,128)(2,1)S(1)} %bitcast.4), channel_id=1, replica_groups={{4,6,0,2},{5,7,1,3},{12,14,8,10},{13,15,9,11},{20,22,16,18},{21,23,17,1..., dimensions={0} | all-to-all | bytes 1048576 | tf_op jit(solution)/shard_map/all_to_all | solution.py:470
  64.1 0.7 %reduce_sum.12 = bf16[16,4096]{1,0:T(8,128)(2,1)} reduce(bf16[4,16,4096]{2,1,0:T(8,128)(2,1)S(1)} %all_to_all.23, bf16[]{:T(256)} %constant.2.clone.1), dimensions={0}, to_apply=%region_0.0 | reduce | flops 196608 | bytes 655362 | tf_op jit(solution)/shard_map/reduce_sum | solution.py:471
Async XLA Ops:
  45.3 7.0 %collective-permute-start = (bf16[64,4096]{1,0:T(8,128)(2,1)S(1)}, bf16[64,4096]{1,0:T(8,128)(2,1)S(1)}, u32[]{:S(2)}, u32[]{:S(2)}) collective-permute-start(bf16[64,4096]{1,0:T(8,128)(2,1)S(1)} %get-tuple-element.37), channel_id=1, source_target_pairs={{0,1},{1,0},{2,3},{3,2},{4,5},{5,4},{6,7},{7,6},{8,9},{9,8},{10,11... | collective-permute-start | bytes 1572872 | tf_op jit(solution)/shard_map/ppermute | solution.py:465

commit v9 on v8

--- a/solution.py
+++ b/solution.py
@@ -372,6 +372,22 @@
     )
 
 
+def sum_kernel(in_ref, out_ref, sum_ref, sems):
+    step = in_ref.shape[2] // 4
+    copies = []
+    for k in range(4):
+        at = slice(k * step, (k + 1) * step)
+        total = in_ref[0, :, at].astype(F32)
+        for block in range(1, in_ref.shape[0]):
+            total = total + in_ref[block, :, at].astype(F32)
+        sum_ref[:, at] = total.astype(BF16)
+        copy = pltpu.make_async_copy(sum_ref.at[:, at], out_ref.at[:, at], sems.at[k])
+        copy.start()
+        copies.append(copy)
+    for copy in copies:
+        copy.wait()
+
+
 def struct(shape, dtype):
     return jax.ShapeDtypeStruct(shape, dtype)
 
@@ -468,7 +484,17 @@
     pair = (keep.astype(F32) + other.astype(F32)).astype(BF16)
     blocks = pair.reshape(4, length // 8, width)
     blocks = lax.all_to_all(blocks, "x", 0, 0, axis_index_groups=[X_ORDER])
-    grad_tokens = jnp.sum(blocks.astype(F32), axis=0).astype(BF16)
+    rows = length // 8
+    grad_tokens = pl.pallas_call(
+        sum_kernel,
+        out_shape=pltpu.HBM((rows, width), BF16),
+        in_specs=[VMEM],
+        out_specs=HBM,
+        scratch_shapes=[pltpu.VMEM((rows, width), BF16), pltpu.SemaphoreType.DMA((4,))],
+        cost_estimate=pl.CostEstimate(flops=2**18, bytes_accessed=2**20, transcendentals=0),
+        compiler_params=pltpu.CompilerParams(vmem_limit_bytes=8 * 2**20),
+        name="sum",
+    )(blocks)
     return grad_inputs, grad_decay, grad_b, grad_c, grad_tokens
 
 

time: 65.2 us -> 65.2 us (level)
  other arithmetic: 0.87 us -> 0.13 us
  Pallas kernels: 5.88 us -> 6.59 us
    reduce_sum x1 -> x0, other arithmetic: 0.74 us -> none  [local(): grad_tokens = jnp.sum(blocks.astype(F32), axis=0).astype(BF16)]
    pallas_call x0 -> x1, Pallas kernels: none -> 0.72 us  [local(): pl.pallas_call(sum_kernel, out_shape=pltpu.HBM((rows, width), BF16), in_s...]
where the time goes in v9:
time: 65.2 us; the launch traced here: 64.8 us
  blocking collectives  51.7 us (79%)
  Pallas kernels  6.59 us (10%)
  starting transfers between devices  5.5 us (8%)
  between operations  0.68 us (1%)
    all_to_all x1, blocking collectives, local(): far = lax.all_to_all(far, 'hi', 0, 0, axis_index_groups=[FAR_ORDER])  19.3 us
    all_to_all x1, blocking collectives, local(): blocks = lax.all_to_all(blocks, 'x', 0, 0, axis_index_groups=[X_ORDER])  11.6 us
    all_to_all x1, blocking collectives, local(): near = lax.all_to_all(near, 'lo', 0, 0, axis_index_groups=[NEAR_ORDER])  11.1 us
    all_to_all x1, blocking collectives, local(): states = lax.all_to_all(states, 'lo', 0, 0, axis_index_groups=[BACK_ORDER])  9.67 us
    pallas_call x5, Pallas kernels, call(): pl.pallas_call(kernel, out_shape=out, in_specs=specs or [VMEM] * len(oper...  5.88 us
    ppermute x1, starting transfers between devices, local(): other = lax.ppermute(send, 'core', [(0, 1), (1, 0)])  5.5 us
  transfers between devices with their start and end apart: 1, of which 1 were waited for; matrix products, arithmetic and copies ran while one was open for 0% of the time, Pallas kernels for 2%

profile of v9, /device:TPU:1, one launch (start us, length us, event | category | flops | bytes accessed | tf_op | source)
XLA Modules:
  0.0 64.8 jit_solution(2984640601214972131)
XLA Ops:
  0.6 1.4 %states.1 = bf16[8,136,128]{2,1,0:T(8,128)(2,1)S(1)} custom-call(f32[8,128]{1,0:T(8,128)} %rate_in.5, bf16[128,512]{1,0:T(8,128)(2,1)} %x_in.5, bf16[128,512]{1,0:T(8,128)(2,1)} %g_in.5, bf16[128,128]{1,0:T(8,128)(2,1)} %b_in.5, bf16[128,128]{1,0:T(8,128)(2,1)} %c_in.5), custom_call_target="tpu_custom_call" | custom-call | flops 33554432 | bytes 1048576 | tf_op jit(solution)/shard_map/states/pallas_call | solution.py:396
  2.0 11.1 %all_to_all.20.in_ref.near_ref = bf16[8,136,128]{2,1,0:T(8,128)(2,1)S(1)} all-to-all(bf16[8,136,128]{2,1,0:T(8,128)(2,1)S(1)} %states.1), channel_id=1, replica_groups={{56,48,40,32,24,16,8,0},{57,49,41,33,25,17,9,1},{58,50,42,34,26,18,10,2..., dimensions={0} | all-to-all | bytes 557056 | tf_op jit(solution)/shard_map/all_to_all | solution.py:426
  13.2 2.2 %segment.1 = (bf16[8,72,128]{2,1,0:T(8,128)(2,1)S(1)}, f32[264,512]{1,0:T(8,128)S(1)}, f32[264,128]{1,0:T(8,128)S(1)}, bf16[256,512]{1,0:T(8,128)(2,1)S(1)}, bf1...) custom-call(bf16[8,136,128]{2,1,0:T(8,128)(2,1)S(1)} %all_to_all.20.in_ref.near_ref, f32[8,128]{1,0:T(8,128)} %rate_in.5, ...), custom_call_target="tpu_custom_call" | custom-call | bytes 524288 | tf_op jit(solution)/shard_map/segment/pallas_call | solution.py:396
  15.4 19.3 %all_to_all.21.far_ref = bf16[8,72,128]{2,1,0:T(8,128)(2,1)S(1)} all-to-all(bf16[8,72,128]{2,1,0:T(8,128)(2,1)S(1)} %get-tuple-element.29), channel_id=1, replica_groups={{256,320,384,448,0,64,128,192},{257,321,385,449,1,65,129,193},{258,322,..., dimensions={0} | all-to-all | bytes 294912 | tf_op jit(solution)/shard_map/all_to_all | solution.py:445
  34.7 0.3 entering.1
  35.0 9.7 %all_to_all.22.state_ref = bf16[8,128,128]{2,1,0:T(8,128)(2,1)S(1)} all-to-all(bf16[8,128,128]{2,1,0:T(8,128)(2,1)S(1)} %get-tuple-element.30), channel_id=1, replica_groups={{48,56,0,8,16,24,32,40},{49,57,1,9,17,25,33,41},{50,58,2,10,18,26,34,42..., dimensions={0} | all-to-all | bytes 524288 | tf_op jit(solution)/shard_map/all_to_all | solution.py:455
  44.7 0.7 %tokens.1 = (bf16[256,128]{1,0:T(8,128)(2,1)S(1)}, bf16[64,4096]{1,0:T(8,128)(2,1)S(1)}, bf16[64,4096]{1,0:T(8,128)(2,1)S(1)}) custom-call(bf16[8,128,128]{2,1,0:T(8,128)(2,1)S(1)} %all_to_all.22.state_ref, f32[264,128]{1,0:T(8,128)S(1)} %get-tuple-element.31.narrow_a, bf16[256,512]{1,0:T(8,128)(2,1)S(1)} %get-tuple-element.32.scaled_a, ...), custom_call_target="tpu_custom_call" | custom-call | flops 536870912 | bytes 4194304 | tf_op jit(solution)/shard_map/tokens/pallas_call | solution.py:396
  45.3 5.5 %collective-permute-start = (bf16[64,4096]{1,0:T(8,128)(2,1)S(1)}, bf16[64,4096]{1,0:T(8,128)(2,1)S(1)}, u32[]{:S(2)}, u32[]{:S(2)}) collective-permute-start(bf16[64,4096]{1,0:T(8,128)(2,1)S(1)} %get-tuple-element.37), channel_id=1, source_target_pairs={{0,1},{1,0},{2,3},{3,2},{4,5},{5,4},{6,7},{7,6},{8,9},{9,8},{10,11... | collective-permute-start | bytes 1572872 | tf_op jit(solution)/shard_map/ppermute | solution.py:481
  50.8 1.3 %carried.1 = (bf16[128,512]{1,0:T(8,128)(2,1)}, f32[8,128]{1,0:T(8,128)}, bf16[128,128]{1,0:T(8,128)(2,1)}, bf16[128,128]{1,0:T(8,128)(2,1)}) custom-call(bf16[8,128,128]{2,1,0:T(8,128)(2,1)S(1)} %all_to_all.22.state_ref, bf16[256,128]{1,0:T(8,128)(2,1)S(1)} %get-tuple-element.38.both_ref, f32[264,512]{1,0:T(8,128)S(1)} %get-tuple-element.39.wide_a, ...), custom_call_target="tpu_custom_call" | custom-call | flops 268435456 | bytes 2097152 | tf_op jit(solution)/shard_map/carried/pallas_call | solution.py:396
  52.1 0.2 collective-permute-done
  52.4 0.1 add_convert_fusion
  52.5 11.6 %all_to_all.23.in_ref = bf16[4,16,4096]{2,1,0:T(8,128)(2,1)S(1)} all-to-all(bf16[4,16,4096]{2,1,0:T(8,128)(2,1)S(1)} %bitcast.4), channel_id=1, replica_groups={{4,6,0,2},{5,7,1,3},{12,14,8,10},{13,15,9,11},{20,22,16,18},{21,23,17,1..., dimensions={0} | all-to-all | bytes 1048576 | tf_op jit(solution)/shard_map/all_to_all | solution.py:486
  64.1 0.7 %sum.1 = bf16[16,4096]{1,0:T(8,128)(2,1)} custom-call(bf16[4,16,4096]{2,1,0:T(8,128)(2,1)S(1)} %all_to_all.23.in_ref), custom_call_target="tpu_custom_call" | custom-call | flops 262144 | bytes 1048576 | tf_op jit(solution)/shard_map/sum/pallas_call | solution.py:488
Async XLA Ops:
  45.3 7.0 %collective-permute-start = (bf16[64,4096]{1,0:T(8,128)(2,1)S(1)}, bf16[64,4096]{1,0:T(8,128)(2,1)S(1)}, u32[]{:S(2)}, u32[]{:S(2)}) collective-permute-start(bf16[64,4096]{1,0:T(8,128)(2,1)S(1)} %get-tuple-element.37), channel_id=1, source_target_pairs={{0,1},{1,0},{2,3},{3,2},{4,5},{5,4},{6,7},{7,6},{8,9},{9,8},{10,11... | collective-permute-start | bytes 1572872 | tf_op jit(solution)/shard_map/ppermute | solution.py:481
